TPU v7x, 32 devices: a whole 2x2x4 slice. The times are simulated.
32 devices in a mesh: bricks: 32 (over z, y, x, core).
Axes of the slice: x: 2, y: 2, z: 4, core: 2. Of those that a mesh axis runs over, the one named last changes fastest.
Arguments:
- calcium: float32 [64, 32, 1024], P('bricks'), may hold values from 0.2 to 1.5
- buffer: float32 [64, 32, 1024], P('bricks'), may hold values from 0.1 to 1.5
- fraction: float32 [64, 32, 1024], P('bricks'), may hold values from 0.1 to 0.4
- rates: float32 [64, 3, 2], P('bricks'), may hold values from 2 to 64
- inverses: float32 [64, 3, 2, 32, 32], P('bricks'), as said below
- neighbors: int32 [3, 2, 64], replicated, may hold values from -1 to 63, as said below
- ranks: int32 [3, 64], replicated, may hold values from 0 to 31, as said below
Outputs:
- calcium_next: float32 [64, 32, 1024], P('bricks')
- buffer_next: float32 [64, 32, 1024], P('bricks')
Inputs may be any that keep to these rules, and one draw needn't show every extreme that they name: neighbors[d, 0, s] and neighbors[d, 1, s] are the slots of the active bricks adjacent to slot s before and after it along dimension d of a block of 32 x 16 x 2 brick positions, -1 where that position is inactive or outside; active bricks fill whole rows along the first dimension. ranks[d, s] is the number of consecutive active bricks before slot s along dimension d. inverses[s, d, k] is the inverse of I + rates[s, d, k] K, K the 32 x 32 second difference with diagonal 1, 2, ..., 2, 1 and off-diagonals -1.
All inputs are finite; a program needn't handle non-finite values.
Results may differ from a plain program's by a relative error of at most 0.00015.
Values sent between devices are 32-bit elements; how exact they have to be, the bound alone decides.
No kernel may reach another device: no remote copies, remote signals or barrier semaphores. Data moves between devices by JAX's collectives and lax.ppermute only.
A program may use at most 128 MiB of HBM per device.

v0:
```python
from functools import partial

import jax
import jax.numpy as jnp
from jax import lax
from jax.sharding import PartitionSpec as P

GX = 32


KON = 0.5
KOFF = 0.3
BTOT = 2.0
INFLUX = 0.1


def fetch(table, index):
    rows = jnp.take(table, jnp.maximum(index, 0), axis=0)
    has = (index >= 0).reshape((-1,) + (1,) * (rows.ndim - 1))
    return jnp.where(has, rows, jnp.zeros_like(rows))


def lookup(planes, before, after):
    sides = []
    for d in range(3):
        lower = fetch(planes[:, d, 1], before[d])
        upper = fetch(planes[:, d, 0], after[d])
        sides.append(jnp.stack([lower, upper], 1))
    return jnp.stack(sides, 1)


def coupling(rate_all, neighbors):
    per_dim = []
    for d in range(3):
        mine = rate_all[:, d]
        sides = []
        for side in range(2):
            other = fetch(mine, neighbors[d, side])
            has = (neighbors[d, side] >= 0)[:, None]
            sides.append(jnp.where(has, 2.0 * mine * other / (mine + other), jnp.zeros_like(mine)))
        per_dim.append(jnp.stack(sides, 1))
    return jnp.stack(per_dim, 1)


def end_planes(field):
    count, edge = (field.shape[0], field.shape[2])
    per_dim = []
    for d in range(3):
        first = lax.index_in_dim(field, 0, 2 + d, False).reshape(count, 2, edge * edge)
        last = lax.index_in_dim(field, edge - 1, 2 + d, False).reshape(count, 2, edge * edge)
        per_dim.append(jnp.stack([first, last], 1))
    return jnp.stack(per_dim, 1)


def operator(field, d, rate, glow, gup, hlow, hup):
    axis = 2 + d
    edge = field.shape[axis]
    plane_shape = lax.index_in_dim(field, 0, axis, False).shape
    lower_face = jnp.expand_dims(hlow.reshape(plane_shape), axis)
    upper_face = jnp.expand_dims(hup.reshape(plane_shape), axis)
    upper = jnp.concatenate([lax.slice_in_dim(field, 1, edge, axis=axis), upper_face], axis)
    lower = jnp.concatenate([lower_face, lax.slice_in_dim(field, 0, edge - 1, axis=axis)], axis)
    place = lax.broadcasted_iota(jnp.int32, field.shape, axis)
    inner = rate[:, :, None, None, None]
    c_up = jnp.where(place == edge - 1, gup[:, :, None, None, None], inner)
    c_down = jnp.where(place == 0, glow[:, :, None, None, None], inner)
    return c_up * (upper - field) + c_down * (lower - field)


def reaction(field, fraction):
    count, edge = (field.shape[0], field.shape[2])
    alpha = fraction.reshape(count, edge, edge, edge)
    calc, bound = (field[:, 0], field[:, 1])
    bind = KON * calc * (BTOT - bound) - KOFF * bound
    return jnp.stack([-bind + INFLUX * (1.0 - alpha) / alpha, bind], 1)


def apply_inverse(block, field, d):
    forms = ["psab,psbjk->psajk", "psab,psibk->psiak", "psab,psijb->psija"]
    return jnp.einsum(forms[d], block, field, precision=lax.Precision.HIGHEST)


def line_ends(field, d):
    count, edge = (field.shape[0], field.shape[2])
    first = lax.index_in_dim(field, 0, 2 + d, False).reshape(count, 2, edge * edge)
    last = lax.index_in_dim(field, edge - 1, 2 + d, False).reshape(count, 2, edge * edge)
    return jnp.stack([first, last], 2)


def block_terms(glow, gup, corner):
    v_first, v_last, w_first, w_last = (
        corner[..., 0],
        corner[..., 1],
        corner[..., 2],
        corner[..., 3],
    )
    a00 = 1.0 + glow * v_first
    a01 = gup * w_first
    a10 = glow * v_last
    a11 = 1.0 + gup * w_last
    lq0 = -glow * v_first
    lq1 = -glow * v_last
    up0 = -gup * w_first
    up1 = -gup * w_last
    return (a00, a01, a10, a11, lq0, lq1, up0, up1)


def chain_order(before, rank):
    slots = jnp.arange(before.shape[0], dtype=jnp.int32)
    pointer = jnp.where(before >= 0, before, slots)
    for step in range(GX.bit_length()):
        pointer = jnp.take(pointer, pointer, axis=0)
    sort_key = pointer * GX + rank
    order = jnp.argsort(sort_key)
    inverse_order = jnp.argsort(order)
    return (order, inverse_order)


def shift_down(values):
    return jnp.concatenate([jnp.zeros_like(values[:1]), values[:-1]], 0)


def shift_up(values):
    return jnp.concatenate([values[1:], jnp.zeros_like(values[:1])], 0)


def compose_maps(first_map, second_map):
    e00, e01, e10, e11 = first_map
    l00, l01, l10, l11 = second_map
    n00 = l00 * e00 + l01 * e10
    n01 = l00 * e01 + l01 * e11
    n10 = l10 * e00 + l11 * e10
    n11 = l10 * e01 + l11 * e11
    scale = jnp.abs(n00) + jnp.abs(n01) + jnp.abs(n10) + jnp.abs(n11)
    return (n00 / scale, n01 / scale, n10 / scale, n11 / scale)


def compose_affine(first_map, second_map):
    first_q, first_p = first_map
    second_q, second_p = second_map
    return (first_q * second_q, second_p + second_q * first_p)


def sorted_solve(glow, gup, corner, before, after, order, inverse_order, ends):
    glow = jnp.take(glow, order, axis=0)
    gup = jnp.take(gup, order, axis=0)
    corner = jnp.take(corner, order, axis=0)
    has_b = jnp.take(before, order, axis=0) >= 0
    has_a = jnp.take(after, order, axis=0) >= 0
    arranged = jnp.take(ends, order, axis=0)
    y0 = arranged[:, :, 0]
    y1 = arranged[:, :, 1]
    a00, a01, a10, a11, lq0, lq1, up0, up1 = block_terms(glow, gup, corner)
    maps = (
        -(lq0 * up1 - lq1 * up0),
        a00 * up1 - a10 * up0,
        -(lq0 * a11 - a01 * lq1),
        a00 * a11 - a01 * a10,
    )
    summed = lax.associative_scan(compose_maps, maps, axis=0)
    f1_prev = summed[1] / summed[3]
    fq = shift_down(f1_prev)
    b00 = a00 - lq0 * fq
    b10 = a10 - lq1 * fq
    det = b00 * a11 - a01 * b10
    f0 = (a11 * up0 - a01 * up1) / det
    f1 = (b00 * up1 - b10 * up0) / det
    slope = (-(b00 * lq1 - b10 * lq0) / det)[:, :, None]
    offset = (b00[:, :, None] * y1 - b10[:, :, None] * y0) / det[:, :, None]
    e1 = lax.associative_scan(compose_affine, (slope, offset), axis=0)[1]
    eq = shift_down(e1)
    e0 = (
        a11[:, :, None] * y0 - a01[:, :, None] * y1 - (a11 * lq0 - a01 * lq1)[:, :, None] * eq
    ) / det[:, :, None]
    zp = lax.associative_scan(compose_affine, (-f0[:, :, None], e0), reverse=True, axis=0)[1]
    pn = shift_up(zp)
    zq = e1 - f1[:, :, None] * pn
    low = jnp.where(has_b[:, None, None], zp - shift_down(zq), jnp.zeros_like(zp))
    high = jnp.where(has_a[:, None, None], zq - pn, jnp.zeros_like(zq))
    return jnp.take(jnp.stack([low, high], 2), inverse_order, axis=0)


def correct(local, block, glow, gup, jumps, d):
    axis = 2 + d
    count, edge = (local.shape[0], local.shape[2])
    shape_v = [count, 2, 1, 1, 1]
    shape_v[axis] = edge
    first_col = block[..., 0].reshape(shape_v)
    last_col = block[..., edge - 1].reshape(shape_v)
    plane_shape = lax.index_in_dim(local, 0, axis, False).shape
    low = jnp.expand_dims(jumps[:, :, 0].reshape(plane_shape), axis)
    high = jnp.expand_dims(jumps[:, :, 1].reshape(plane_shape), axis)
    return (
        local
        - glow[:, :, None, None, None] * low * first_col
        - gup[:, :, None, None, None] * high * last_col
    )


def body(calcium, buffer, fraction, rates, inverses, neighbors, ranks):
    count, edge = (calcium.shape[0], calcium.shape[1])
    devices = lax.axis_size("bricks")
    square = edge * edge
    per_device = square // devices
    start = lax.axis_index("bricks") * count
    corners = jnp.stack(
        [
            inverses[..., 0, 0],
            inverses[..., edge - 1, 0],
            inverses[..., 0, edge - 1],
            inverses[..., edge - 1, edge - 1],
        ],
        -1,
    )
    rate_all, corner_all = (
        lax.all_gather(rates, "bricks", axis=0, tiled=True),
        lax.all_gather(corners, "bricks", axis=0, tiled=True),
    )
    couple_all = coupling(rate_all, neighbors)
    couple = lax.dynamic_slice_in_dim(couple_all, start, count, 0)
    field = jnp.stack([calcium, buffer], 1).reshape(count, 2, edge, edge, edge)
    planes = end_planes(field).reshape(count, 3, 2, 2, devices, per_device)
    lined = lookup(
        lax.all_to_all(planes, "bricks", split_axis=4, concat_axis=0, tiled=True),
        neighbors[:, 0],
        neighbors[:, 1],
    )
    halos = lax.all_to_all(lined, "bricks", split_axis=0, concat_axis=4, tiled=True).reshape(
        count, 3, 2, 2, square
    )
    lams = [
        operator(
            field, d, rates[:, d], couple[:, d, 0], couple[:, d, 1], halos[:, d, 0], halos[:, d, 1]
        )
        for d in range(3)
    ]
    rhs = field + lams[0] + 2.0 * lams[1] + 2.0 * lams[2] + reaction(field, fraction)

    def solve(right, d):
        block = inverses[:, d]
        local = apply_inverse(block, right, d)
        ends = line_ends(local, d).reshape(count, 2, 2, devices, per_device)
        order, inverse_order = chain_order(neighbors[d, 0], ranks[d])
        chain_fn = partial(
            sorted_solve,
            couple_all[:, d, 0],
            couple_all[:, d, 1],
            corner_all[:, d],
            neighbors[d, 0],
            neighbors[d, 1],
            order,
            inverse_order,
        )
        lined_jumps = chain_fn(
            lax.all_to_all(ends, "bricks", split_axis=3, concat_axis=0, tiled=True)[:, :, :, 0]
        )[:, :, :, None]
        jumps = lax.all_to_all(
            lined_jumps, "bricks", split_axis=0, concat_axis=3, tiled=True
        ).reshape(count, 2, 2, square)
        return correct(local, block, couple[:, d, 0], couple[:, d, 1], jumps, d)

    first = solve(rhs, 0)
    second = solve(first - lams[1], 1)
    third = solve(second - lams[2], 2)
    result = third.reshape(count, 2, edge, edge * edge)
    return (result[:, 0], result[:, 1])


def solution(mesh):
    in_specs = (
        P("bricks", None, None),
        P("bricks", None, None),
        P("bricks", None, None),
        P("bricks", None, None),
        P("bricks", None, None, None, None),
        P(),
        P(),
    )
    out_specs = (P("bricks", None, None), P("bricks", None, None))
    return jax.shard_map(body, mesh=mesh, in_specs=in_specs, out_specs=out_specs, check_vma=False)
```

profile of v0, /device:TPU:0, one launch (start us, length us, event | category | flops | bytes accessed | tf_op | source)
XLA Modules:
  0.0 458.3 jit_solution(3944574029903963251)
XLA Ops:
  0.6 2.3 reshape.397
  3.0 1.3 stack.167
  4.3 1.3 stack.166
  5.6 4.9 %divide_add_fusion = (f32[2,1,32,32,32]{4,2,3,1,0:T(8,128)}, f32[2,1,32,32,32]{4,2,3,1,0:T(8,128)}, f32[2,2,32,32,32]{4,2,3,1,0:T(8,128)S(1)}) fusion(f32[2,1,32,32,32]{4,3,2,0,1:T(8,128)} %reshape.397, f32[2,1,32,32,32]{4,3,2,0,1:T(8,128)S(1)} %stack.167, f32[2,1,32,32,32]{4,3,2,0,1:T(8,128)} %stack.166), kind=kLoop, calls=%fused_computation.91 | loop fusion | flops 655359 | bytes 2359296 | tf_op jit(solution)/shard_map/add | solution.py:75
  11.1 2.8 fusion.163
  14.0 2.6 copy.1051
  16.6 2.6 copy.1050
  19.6 1.1 reshape.1017
  20.6 7.3 %all-to-all-start = ((f32[32,1,768]{2,1,0:T(1,128)}), f32[32,1,768]{2,1,0:T(1,128)S(1)}, u32[]{:S(2)}, u32[]{:S(2)}) async-start(f32[32,1,768]{2,1,0:T(1,128)} %reshape.1017), calls=%async_computation | async-start | bytes 196608 | tf_op jit(solution)/shard_map/all_to_all | solution.py:224
  29.2 2.8 fusion.161
  32.0 42.1 %all_gather.6 = f32[64,3,2]{1,2,0:T(2,128)S(1)} all-gather(f32[2,3,2]{1,2,0:T(2,128)S(1)} %copy-done.49), channel_id=1, replica_groups=mesh['bricks'=32] {'bricks'}, dimensions={0}, use_global_device_ids=true | all-gather | bytes 1584 | tf_op jit(solution)/shard_map/all_gather | solution.py:216
  75.5 2.8 fusion.160
  78.3 2.5 fusion.159
  80.9 0.8 fusion.175
  83.5 0.8 gather_fusion.38
  98.4 2.0 sort.87
  102.3 37.7 %all_gather.7 = f32[64,3,2,4]{1,2,0,3:T(2,128)S(1)} all-gather(f32[2,3,2,4]{1,2,0,3:T(2,128)S(1)} %pad_maximum_fusion.19), channel_id=1, replica_groups=mesh['bricks'=32] {'bricks'}, dimensions={0}, use_global_device_ids=true | all-gather | bytes 6336 | tf_op jit(solution)/shard_map/all_gather | solution.py:217
  170.0 0.9 copy.1030
  172.9 0.8 divide_select_fusion.3
  173.9 2.7 sort.89
  176.5 2.0 sort.90
  203.0 2.7 sort.91
  205.7 2.0 sort.92
  207.8 1.1 compare_and_fusion
  240.5 2.0 sort.88
  274.9 1.3 gather_fusion.49
  289.9 0.8 slice_reduce_fusion.1
  291.7 0.9 reduce.54
  300.0 1.1 reshape.1019
  301.0 2.8 all-to-all-start.1
  303.8 7.8 %all-to-all-done.1 = f32[32,1,768]{2,1,0:T(1,128)S(1)} async-done(((f32[32,1,768]{2,1,0:T(1,128)}), f32[32,1,768]{2,1,0:T(1,128)S(1)}, u32[]{:S(2)}, u32[]{:S(2)}) %all-to-all-start.1) | async-done | bytes 98336 | tf_op jit(solution)/shard_map/all_to_all | solution.py:228
  311.6 0.9 reduce.55
  313.3 3.0 copy.1068
  316.4 2.9 copy.1070
  320.0 5.0 %fusion.18 = f32[2,2,32,32,32]{4,2,3,1,0:T(8,128)S(1)} fusion(f32[2,2,32,32,32]{4,2,3,1,0:T(8,128)S(1)} %copy_dynamic-update-slice_fusion, f32[2,2,32,32,1]{4,2,3,1,0:T(8,128)} %copy.1068, f32[2,2,32,32,31]{4,2,3,1,0:T(8,128)} %get-tuple-element.291, f32[2,2,32,32,31]{4,2,3,1,0:T(8,128)} %get-tuple-element.290, f32[2,2,32,32,1]{4,2,3,1,0:T(8,128)} %copy.1070, ...), kind=kLoop, calls=%fused_computation.72 | loop fusion | flops 1179648 | bytes 2097264 | tf_op jit(solution)/shard_map/add | solution.py:67
  326.1 1.0 copy-done.7
  327.1 3.8 fusion.31
  331.2 1.1 copy-done.3
  333.2 3.0 all-to-all-start.2
  336.4 7.0 %all-to-all-done.2 = f32[32,1,256]{2,1,0:T(1,128)S(1)} async-done(((f32[32,1,256]{2,1,0:T(1,128)}), f32[32,1,256]{2,1,0:T(1,128)S(1)}, u32[]{:S(2)}, u32[]{:S(2)}) %all-to-all-start.2) | async-done | bytes 32800 | tf_op jit(solution)/shard_map/all_to_all | solution.py:255
  344.3 0.8 gather_fusion.21
  353.0 0.8 gather_fusion.24
  354.8 2.6 all-to-all-start.3
  357.6 7.1 %all-to-all-done.3 = f32[32,1,256]{2,1,0:T(1,128)S(1)} async-done(((f32[32,1,256]{2,1,0:T(1,128)}), f32[32,1,256]{2,1,0:T(1,128)S(1)}, u32[]{:S(2)}, u32[]{:S(2)}) %all-to-all-start.3) | async-done | bytes 32800 | tf_op jit(solution)/shard_map/all_to_all | solution.py:257
  366.1 3.7 subtract_subtract_fusion.1
  369.8 3.2 fusion.25
  373.1 1.2 copy.1263
  375.5 2.9 all-to-all-start.4
  378.6 7.0 %all-to-all-done.4 = f32[32,1,256]{2,1,0:T(1,128)S(1)} async-done(((f32[32,1,256]{2,1,0:T(1,128)}), f32[32,1,256]{2,1,0:T(1,128)S(1)}, u32[]{:S(2)}, u32[]{:S(2)}) %all-to-all-start.4) | async-done | bytes 32800 | tf_op jit(solution)/shard_map/all_to_all | solution.py:255
  386.7 0.8 gather_fusion.34
  394.6 0.9 gather_fusion.37
  396.4 2.6 all-to-all-start.5
  399.2 7.1 %all-to-all-done.5 = f32[32,1,256]{2,1,0:T(1,128)S(1)} async-done(((f32[32,1,256]{2,1,0:T(1,128)}), f32[32,1,256]{2,1,0:T(1,128)S(1)}, u32[]{:S(2)}, u32[]{:S(2)}) %all-to-all-start.5) | async-done | bytes 32800 | tf_op jit(solution)/shard_map/all_to_all | solution.py:257
  407.7 3.7 subtract_subtract_fusion
  411.5 9.1 %fusion.23 = f32[2,2,32,32,32]{3,4,2,1,0:T(8,128)S(1)} fusion(f32[2,2,32,32,32]{4,2,3,1,0:T(8,128)S(1)} %subtract_subtract_fusion, f32[2,3,2,32,32]{4,3,2,1,0:T(8,128)S(1)} %copy-done.8), kind=kOutput, calls=%fused_computation.78 | convolution fusion | flops 50331648 | bytes 2686976 | tf_op jit(solution)/shard_map/psab,psijb->psija/dot_general | solution.py:80
  421.8 2.9 all-to-all-start.6
  424.9 7.0 %all-to-all-done.6 = f32[32,1,256]{2,1,0:T(1,128)S(1)} async-done(((f32[32,1,256]{2,1,0:T(1,128)}), f32[32,1,256]{2,1,0:T(1,128)S(1)}, u32[]{:S(2)}, u32[]{:S(2)}) %all-to-all-start.6) | async-done | bytes 32800 | tf_op jit(solution)/shard_map/all_to_all | solution.py:255
  433.0 0.8 gather_fusion.47
  440.8 0.9 gather_fusion.50
  442.0 8.9 %all_to_all.123 = f32[32,1,256]{2,1,0:T(1,128)S(1)} all-to-all(f32[32,1,256]{2,1,0:T(1,128)S(1)} %reshape.1031), channel_id=1, replica_groups=mesh['bricks'=32] {'bricks'}, dimensions={0} | all-to-all | bytes 65536 | tf_op jit(solution)/shard_map/all_to_all | solution.py:257
  452.5 1.9 multiply_subtract_fusion
  454.3 1.9 copy.1215
  456.3 1.0 reshape.401
  457.2 0.8 slice_bitcast_fusion
  (1539 shorter events, 198.7 us)
Async XLA Ops:
  20.6 270.6 %all-to-all-start = ((f32[32,1,768]{2,1,0:T(1,128)}), f32[32,1,768]{2,1,0:T(1,128)S(1)}, u32[]{:S(2)}, u32[]{:S(2)}) async-start(f32[32,1,768]{2,1,0:T(1,128)} %reshape.1017), calls=%async_computation | async-start | bytes 196608 | tf_op jit(solution)/shard_map/all_to_all | solution.py:224
  29.2 54.0 %copy-start.96 = (pred[64]{0:T(512)(128)(4,1)}, pred[64]{0:T(512)(128)(4,1)S(1)}, u32[]{:S(2)}) copy-start(pred[64]{0:T(512)(128)(4,1)S(1)} %get-tuple-element.388) | copy-start | bytes 196
  29.2 54.0 %copy-start.98 = (pred[64]{0:T(512)(128)(4,1)}, pred[64]{0:T(512)(128)(4,1)S(1)}, u32[]{:S(2)}) copy-start(pred[64]{0:T(512)(128)(4,1)S(1)} %get-tuple-element.393) | copy-start | bytes 196
  29.2 54.0 %copy-start.100 = (pred[64]{0:T(512)(128)(4,1)}, pred[64]{0:T(512)(128)(4,1)S(1)}, u32[]{:S(2)}) copy-start(pred[64]{0:T(512)(128)(4,1)S(1)} %get-tuple-element.398) | copy-start | bytes 196
  29.2 54.0 %copy-start.102 = (pred[64]{0:T(512)(128)(4,1)}, pred[64]{0:T(512)(128)(4,1)S(1)}, u32[]{:S(2)}) copy-start(pred[64]{0:T(512)(128)(4,1)S(1)} %get-tuple-element.399) | copy-start | bytes 196
  100.5 142.0 %copy-start.67 = (s32[1024]{0:T(1024)}, s32[1024]{0:T(1024)S(1)}, u32[]{:S(2)}) copy-start(s32[1024]{0:T(1024)S(1)} %pad_clamp_fusion.17) | copy-start | bytes 12292
  179.1 57.2 %copy-start.68 = (s32[1024]{0:T(1024)}, s32[1024]{0:T(1024)S(1)}, u32[]{:S(2)}) copy-start(s32[1024]{0:T(1024)S(1)} %pad_clamp_fusion.9) | copy-start | bytes 12292
  179.9 31.1 %copy-start.108 = (pred[64]{0:T(512)(128)(4,1)S(1)}, pred[64]{0:T(512)(128)(4,1)}, u32[]{:S(2)}) copy-start(pred[64]{0:T(512)(128)(4,1)} %get-tuple-element.389) | copy-start | bytes 196
  179.9 31.1 %copy-start.110 = (pred[64]{0:T(512)(128)(4,1)S(1)}, pred[64]{0:T(512)(128)(4,1)}, u32[]{:S(2)}) copy-start(pred[64]{0:T(512)(128)(4,1)} %get-tuple-element.390) | copy-start | bytes 196
  179.9 31.1 %copy-start.112 = (pred[64]{0:T(512)(128)(4,1)S(1)}, pred[64]{0:T(512)(128)(4,1)}, u32[]{:S(2)}) copy-start(pred[64]{0:T(512)(128)(4,1)} %get-tuple-element.394) | copy-start | bytes 196
  179.9 31.1 %copy-start.114 = (pred[64]{0:T(512)(128)(4,1)S(1)}, pred[64]{0:T(512)(128)(4,1)}, u32[]{:S(2)}) copy-start(pred[64]{0:T(512)(128)(4,1)} %get-tuple-element.395) | copy-start | bytes 196
  180.5 110.2 %copy-start.62 = (pred[64]{0:T(512)(128)(4,1)}, pred[64]{0:T(512)(128)(4,1)S(1)}, u32[]{:S(2)}) copy-start(pred[64]{0:T(512)(128)(4,1)S(1)} %get-tuple-element.117) | copy-start | bytes 196
  211.3 63.6 %copy-start.69 = (s32[1024]{0:T(1024)}, s32[1024]{0:T(1024)S(1)}, u32[]{:S(2)}) copy-start(s32[1024]{0:T(1024)S(1)} %pad_clamp_fusion.1) | copy-start | bytes 12292
  212.1 28.4 %copy-start.159 = (s32[64]{0:T(128)S(1)}, s32[64]{0:T(128)}, u32[]{:S(2)}) copy-start(s32[64]{0:T(128)} %copy-done.158) | copy-start | bytes 772
  213.1 34.1 %copy-start.125 = (f32[2,2,1]{0,1,2:T(2,128)S(1)}, f32[2,2,1]{0,1,2:T(2,128)}, u32[]{:S(2)}) copy-start(f32[2,2,1]{0,1,2:T(2,128)} %slice.2456) | copy-start | bytes 52
  213.1 34.9 %copy-start.121 = (f32[3,2,1]{0,1,2:T(2,128)S(1)}, f32[3,2,1]{0,1,2:T(2,128)}, u32[]{:S(2)}) copy-start(f32[3,2,1]{0,1,2:T(2,128)} %slice.2443) | copy-start | bytes 76
  213.1 35.5 %copy-start.122 = (f32[7,2,1]{0,1,2:T(2,128)S(1)}, f32[7,2,1]{0,1,2:T(2,128)}, u32[]{:S(2)}) copy-start(f32[7,2,1]{0,1,2:T(2,128)} %slice.2436) | copy-start | bytes 172
  213.1 36.2 %copy-start.123 = (f32[15,2,1]{0,1,2:T(2,128)S(1)}, f32[15,2,1]{0,1,2:T(2,128)}, u32[]{:S(2)}) copy-start(f32[15,2,1]{0,1,2:T(2,128)} %slice.2429) | copy-start | bytes 364
  213.1 36.9 %copy-start.124 = (f32[31,2,1]{0,1,2:T(2,128)S(1)}, f32[31,2,1]{0,1,2:T(2,128)}, u32[]{:S(2)}) copy-start(f32[31,2,1]{0,1,2:T(2,128)} %slice.2422) | copy-start | bytes 748
  213.8 36.9 %copy-start.120 = (f32[64,2]{0,1:T(2,128)S(1)}, f32[64,2]{0,1:T(2,128)}, u32[]{:S(2)}) copy-start(f32[64,2]{0,1:T(2,128)} %get-tuple-element.550) | copy-start | bytes 1540
  213.8 41.0 %copy-start.126 = (f32[2,2,1]{0,1,2:T(2,128)S(1)}, f32[2,2,1]{0,1,2:T(2,128)}, u32[]{:S(2)}) copy-start(f32[2,2,1]{0,1,2:T(2,128)} %slice.2506) | copy-start | bytes 52
  213.8 41.5 %copy-start.127 = (f32[3,2,1]{0,1,2:T(2,128)S(1)}, f32[3,2,1]{0,1,2:T(2,128)}, u32[]{:S(2)}) copy-start(f32[3,2,1]{0,1,2:T(2,128)} %slice.2493) | copy-start | bytes 76
  213.8 42.2 %copy-start.128 = (f32[7,2,1]{0,1,2:T(2,128)S(1)}, f32[7,2,1]{0,1,2:T(2,128)}, u32[]{:S(2)}) copy-start(f32[7,2,1]{0,1,2:T(2,128)} %slice.2486) | copy-start | bytes 172
  213.8 42.9 %copy-start.129 = (f32[15,2,1]{0,1,2:T(2,128)S(1)}, f32[15,2,1]{0,1,2:T(2,128)}, u32[]{:S(2)}) copy-start(f32[15,2,1]{0,1,2:T(2,128)} %slice.2479) | copy-start | bytes 364
  213.9 43.5 %copy-start.136 = (f32[31,2,1]{0,1,2:T(2,128)S(1)}, f32[31,2,1]{0,1,2:T(2,128)}, u32[]{:S(2)}) copy-start(f32[31,2,1]{0,1,2:T(2,128)} %slice.2467) | copy-start | bytes 748
  214.0 44.2 %copy-start.137 = (f32[64,2]{0,1:T(2,128)S(1)}, f32[64,2]{0,1:T(2,128)}, u32[]{:S(2)}) copy-start(f32[64,2]{0,1:T(2,128)} %get-tuple-element.202) | copy-start | bytes 1540
  214.0 60.3 %copy-start.147 = (s32[64]{0:T(128)S(1)}, s32[64]{0:T(128)}, u32[]{:S(2)}) copy-start(s32[64]{0:T(128)} %get-tuple-element.561) | copy-start | bytes 772
  276.2 17.9 %copy-start.113 = (pred[64]{0:T(512)(128)(4,1)S(1)}, pred[64]{0:T(512)(128)(4,1)}, u32[]{:S(2)}) copy-start(pred[64]{0:T(512)(128)(4,1)} %get-tuple-element.394) | copy-start | bytes 196
  276.2 17.9 %copy-start.115 = (pred[64]{0:T(512)(128)(4,1)S(1)}, pred[64]{0:T(512)(128)(4,1)}, u32[]{:S(2)}) copy-start(pred[64]{0:T(512)(128)(4,1)} %get-tuple-element.395) | copy-start | bytes 196
  301.0 10.6 %all-to-all-start.1 = ((f32[32,1,768]{2,1,0:T(1,128)}), f32[32,1,768]{2,1,0:T(1,128)S(1)}, u32[]{:S(2)}, u32[]{:S(2)}) async-start(f32[32,1,768]{2,1,0:T(1,128)} %reshape.1019), calls=%async_computation.1 | async-start | bytes 196608 | tf_op jit(solution)/shard_map/all_to_all | solution.py:228
  327.1 18.4 %copy-start.12 = (f32[64,2]{1,0:T(8,128)S(1)}, f32[64,2]{1,0:T(8,128)}, u32[]{:S(2)}) copy-start(f32[64,2]{1,0:T(8,128)} %copy.1099) | copy-start | bytes 1540
  327.1 18.4 %copy-start.13 = (f32[64,2]{1,0:T(8,128)S(1)}, f32[64,2]{1,0:T(8,128)}, u32[]{:S(2)}) copy-start(f32[64,2]{1,0:T(8,128)} %copy.1098) | copy-start | bytes 1540
  327.1 18.6 %copy-start.37 = (f32[32,2]{1,0:T(8,128)S(1)}, f32[32,2]{1,0:T(8,128)}, u32[]{:S(2)}) copy-start(f32[32,2]{1,0:T(8,128)} %copy.1102) | copy-start | bytes 772
  331.0 16.6 %copy-start.47 = (f32[15,2]{1,0:T(8,128)S(1)}, f32[15,2]{1,0:T(8,128)}, u32[]{:S(2)}) copy-start(f32[15,2]{1,0:T(8,128)} %copy.1103) | copy-start | bytes 364
  331.0 17.5 %copy-start.36 = (f32[31,2]{1,0:T(8,128)S(1)}, f32[31,2]{1,0:T(8,128)}, u32[]{:S(2)}) copy-start(f32[31,2]{1,0:T(8,128)} %copy.1101) | copy-start | bytes 748
  331.0 18.1 %copy-start.10 = (f32[64,2]{1,0:T(8,128)S(1)}, f32[64,2]{1,0:T(8,128)}, u32[]{:S(2)}) copy-start(f32[64,2]{1,0:T(8,128)} %copy.1092) | copy-start | bytes 1540
  331.0 18.1 %copy-start.11 = (f32[64,2]{1,0:T(8,128)S(1)}, f32[64,2]{1,0:T(8,128)}, u32[]{:S(2)}) copy-start(f32[64,2]{1,0:T(8,128)} %copy.1086) | copy-start | bytes 1540
  331.0 18.1 %copy-start.23 = (f32[64,2]{1,0:T(8,128)S(1)}, f32[64,2]{1,0:T(8,128)}, u32[]{:S(2)}) copy-start(f32[64,2]{1,0:T(8,128)} %copy.1097) | copy-start | bytes 1540
  331.1 18.5 %copy-start.35 = (f32[32,2]{1,0:T(8,128)S(1)}, f32[32,2]{1,0:T(8,128)}, u32[]{:S(2)}) copy-start(f32[32,2]{1,0:T(8,128)} %copy.1111) | copy-start | bytes 772
  331.1 18.6 %copy-start.46 = (f32[16,2]{1,0:T(8,128)S(1)}, f32[16,2]{1,0:T(8,128)}, u32[]{:S(2)}) copy-start(f32[16,2]{1,0:T(8,128)} %copy.1113) | copy-start | bytes 388
  331.1 18.7 %copy-start.54 = (f32[8,2]{1,0:T(8,128)S(1)}, f32[8,2]{1,0:T(8,128)}, u32[]{:S(2)}) copy-start(f32[8,2]{1,0:T(8,128)} %copy.1115) | copy-start | bytes 196
  331.1 18.8 %copy-start.89 = (f32[4,2]{1,0:T(4,128)S(1)}, f32[4,2]{1,0:T(4,128)}, u32[]{:S(2)}) copy-start(f32[4,2]{1,0:T(4,128)} %copy.1117) | copy-start | bytes 100
  331.1 18.9 %copy-start.134 = (f32[2,2,1]{1,0,2:T(2,128)S(1)}, f32[2,2,1]{1,0,2:T(2,128)}, u32[]{:S(2)}) copy-start(f32[2,2,1]{1,0,2:T(2,128)} %copy.1118) | copy-start | bytes 52
  332.3 17.9 %copy-start.160 = (f32[2]{0:T(128)S(1)}, f32[2]{0:T(128)}, u32[]{:S(2)}) copy-start(f32[2]{0:T(128)} %slice_reduce_fusion.24) | copy-start | bytes 28
  332.3 18.0 %copy-start.88 = (f32[3,2]{1,0:T(4,128)S(1)}, f32[3,2]{1,0:T(4,128)}, u32[]{:S(2)}) copy-start(f32[3,2]{1,0:T(4,128)} %copy.1116) | copy-start | bytes 76
  332.3 18.3 %copy-start.60 = (f32[7,2]{1,0:T(8,128)S(1)}, f32[7,2]{1,0:T(8,128)}, u32[]{:S(2)}) copy-start(f32[7,2]{1,0:T(8,128)} %copy.1114) | copy-start | bytes 172
  332.3 18.5 %copy-start.45 = (f32[15,2]{1,0:T(8,128)S(1)}, f32[15,2]{1,0:T(8,128)}, u32[]{:S(2)}) copy-start(f32[15,2]{1,0:T(8,128)} %copy.1112) | copy-start | bytes 364
  333.2 10.2 %all-to-all-start.2 = ((f32[32,1,256]{2,1,0:T(1,128)}), f32[32,1,256]{2,1,0:T(1,128)S(1)}, u32[]{:S(2)}, u32[]{:S(2)}) async-start(f32[32,1,256]{2,1,0:T(1,128)} %reshape.1021), calls=%async_computation.2 | async-start | bytes 65536 | tf_op jit(solution)/shard_map/all_to_all | solution.py:255
  354.8 9.8 %all-to-all-start.3 = ((f32[32,1,256]{2,1,0:T(1,128)}), f32[32,1,256]{2,1,0:T(1,128)S(1)}, u32[]{:S(2)}, u32[]{:S(2)}) async-start(f32[32,1,256]{2,1,0:T(1,128)} %reshape.1023), calls=%async_computation.3 | async-start | bytes 65536 | tf_op jit(solution)/shard_map/all_to_all | solution.py:257
  374.4 16.4 %copy-start.14 = (f32[64,2]{1,0:T(8,128)S(1)}, f32[64,2]{1,0:T(8,128)}, u32[]{:S(2)}) copy-start(f32[64,2]{1,0:T(8,128)} %copy.1139) | copy-start | bytes 1540
  374.7 16.6 %copy-start.31 = (f32[32,2]{1,0:T(8,128)S(1)}, f32[32,2]{1,0:T(8,128)}, u32[]{:S(2)}) copy-start(f32[32,2]{1,0:T(8,128)} %copy.1158) | copy-start | bytes 772
  374.7 16.7 %copy-start.42 = (f32[16,2]{1,0:T(8,128)S(1)}, f32[16,2]{1,0:T(8,128)}, u32[]{:S(2)}) copy-start(f32[16,2]{1,0:T(8,128)} %copy.1160) | copy-start | bytes 388
  374.7 16.8 %copy-start.52 = (f32[8,2]{1,0:T(8,128)S(1)}, f32[8,2]{1,0:T(8,128)}, u32[]{:S(2)}) copy-start(f32[8,2]{1,0:T(8,128)} %copy.1162) | copy-start | bytes 196
  374.7 16.9 %copy-start.85 = (f32[4,2]{1,0:T(4,128)S(1)}, f32[4,2]{1,0:T(4,128)}, u32[]{:S(2)}) copy-start(f32[4,2]{1,0:T(4,128)} %copy.1164) | copy-start | bytes 100
  375.5 16.5 %copy-start.84 = (f32[3,2]{1,0:T(4,128)S(1)}, f32[3,2]{1,0:T(4,128)}, u32[]{:S(2)}) copy-start(f32[3,2]{1,0:T(4,128)} %copy.1163) | copy-start | bytes 76
  375.5 10.1 %all-to-all-start.4 = ((f32[32,1,256]{2,1,0:T(1,128)}), f32[32,1,256]{2,1,0:T(1,128)S(1)}, u32[]{:S(2)}, u32[]{:S(2)}) async-start(f32[32,1,256]{2,1,0:T(1,128)} %reshape.1025), calls=%async_computation.4 | async-start | bytes 65536 | tf_op jit(solution)/shard_map/all_to_all | solution.py:255
  396.4 9.8 %all-to-all-start.5 = ((f32[32,1,256]{2,1,0:T(1,128)}), f32[32,1,256]{2,1,0:T(1,128)S(1)}, u32[]{:S(2)}, u32[]{:S(2)}) async-start(f32[32,1,256]{2,1,0:T(1,128)} %reshape.1027), calls=%async_computation.5 | async-start | bytes 65536 | tf_op jit(solution)/shard_map/all_to_all | solution.py:257
  420.7 16.4 %copy-start.18 = (f32[64,2]{1,0:T(8,128)S(1)}, f32[64,2]{1,0:T(8,128)}, u32[]{:S(2)}) copy-start(f32[64,2]{1,0:T(8,128)} %copy.1177) | copy-start | bytes 1540
  420.7 16.4 %copy-start.21 = (f32[64,2]{1,0:T(8,128)S(1)}, f32[64,2]{1,0:T(8,128)}, u32[]{:S(2)}) copy-start(f32[64,2]{1,0:T(8,128)} %copy.1189) | copy-start | bytes 1540
  421.0 16.6 %copy-start.27 = (f32[32,2]{1,0:T(8,128)S(1)}, f32[32,2]{1,0:T(8,128)}, u32[]{:S(2)}) copy-start(f32[32,2]{1,0:T(8,128)} %copy.1203) | copy-start | bytes 772
  421.0 16.7 %copy-start.38 = (f32[16,2]{1,0:T(8,128)S(1)}, f32[16,2]{1,0:T(8,128)}, u32[]{:S(2)}) copy-start(f32[16,2]{1,0:T(8,128)} %copy.1205) | copy-start | bytes 388
  421.0 16.9 %copy-start.81 = (f32[4,2]{1,0:T(4,128)S(1)}, f32[4,2]{1,0:T(4,128)}, u32[]{:S(2)}) copy-start(f32[4,2]{1,0:T(4,128)} %copy.1209) | copy-start | bytes 100
  421.8 16.5 %copy-start.80 = (f32[3,2]{1,0:T(4,128)S(1)}, f32[3,2]{1,0:T(4,128)}, u32[]{:S(2)}) copy-start(f32[3,2]{1,0:T(4,128)} %copy.1208) | copy-start | bytes 76
  421.8 10.2 %all-to-all-start.6 = ((f32[32,1,256]{2,1,0:T(1,128)}), f32[32,1,256]{2,1,0:T(1,128)S(1)}, u32[]{:S(2)}, u32[]{:S(2)}) async-start(f32[32,1,256]{2,1,0:T(1,128)} %reshape.1029), calls=%async_computation.6 | async-start | bytes 65536 | tf_op jit(solution)/shard_map/all_to_all | solution.py:255
  (109 other events, 1088.6 us)
where the time goes:
time: 466 us; the launch traced here: 458 us
  local copies, waits for them, and re-layouts  206 us (44%)
  blocking collectives  88.8 us (19%)
  other arithmetic  74.6 us (16%)
  waiting for transfers between devices  43 us (9%)
  starting transfers between devices  24 us (5%)
  matrix products  16.1 us (3%)
  between operations  5.5 us (1%)
    all_gather x1, blocking collectives, body(): lax.all_gather(rates, 'bricks', axis=0, tiled=True)  42.1 us
    all_gather x1, blocking collectives, body(): lax.all_gather(corners, 'bricks', axis=0, tiled=True)  37.7 us
    mul x48, local copies, waits for them, and re-layouts, compose_affine(): return (first_q * second_q, second_p + second_q * first_p)  30.8 us
    all_to_all x3, waiting for transfers between devices, solve(): lax.all_to_all(ends, 'bricks', split_axis=3, concat_axis=0, tiled=True)  21.1 us
    slice x168, local copies, waits for them, and re-layouts, sorted_solve(): summed = lax.associative_scan(compose_maps, maps, axis=0)  17.5 us
    dot_general x3, matrix products, apply_inverse(): return jnp.einsum(forms[d], block, field, precision=lax.Precision.HIGHEST)  16.1 us
    all_to_all x2, waiting for transfers between devices, solve(): lax.all_to_all(lined_jumps, 'bricks', split_axis=0, concat_axis=3, tiled=...  14.1 us
    gather x18, local copies, waits for them, and re-layouts, chain_order(): pointer = jnp.take(pointer, pointer, axis=0)  14 us
  transfers between devices with their start and end apart: 7, of which 6 were waited for; matrix products, arithmetic and copies ran while one was open for 40% of the time, Pallas kernels for 0%

commit v1 on v0

--- a/solution.py
+++ b/solution.py
@@ -1,8 +1,12 @@
 from functools import partial
+import math
 
 import jax
 import jax.numpy as jnp
+import numpy as np
 from jax import lax
+from jax.experimental import pallas as pl
+from jax.experimental.pallas import tpu as pltpu
 from jax.sharding import PartitionSpec as P
 
 GX = 32
@@ -197,7 +201,7 @@
     )
 
 
-def body(calcium, buffer, fraction, rates, inverses, neighbors, ranks):
+def general_body(calcium, buffer, fraction, rates, inverses, neighbors, ranks):
     count, edge = (calcium.shape[0], calcium.shape[1])
     devices = lax.axis_size("bricks")
     square = edge * edge
@@ -266,6 +270,431 @@
     return (result[:, 0], result[:, 1])
 
 
+LANES = 128
+
+
+def cosine_basis(edge):
+    wave = np.arange(edge)[:, None]
+    place = np.arange(edge)[None, :]
+    basis = np.sqrt(2.0 / edge) * np.cos(np.pi * wave * (place + 0.5) / edge)
+    basis[0] = math.sqrt(1.0 / edge)
+    eigen = 2.0 - 2.0 * np.cos(np.pi * np.arange(edge) / edge)
+    return basis, eigen
+
+
+def dot(a, b):
+    return jnp.dot(a, b, precision=lax.Precision.HIGHEST, preferred_element_type=jnp.float32)
+
+
+def dot_lanes(a, b):
+    return lax.dot_general(
+        a, b, (((1,), (1,)), ((), ())), precision=lax.Precision.HIGHEST, preferred_element_type=jnp.float32
+    )
+
+
+def lane_of(shape):
+    return lax.broadcasted_iota(jnp.int32, shape, len(shape) - 1)
+
+
+def swap_blocks(four):
+    x0, x1, x2, x3 = four
+    lane = lane_of(x0.shape)
+    low = (lane & 64) == 0
+    y0, y2 = jnp.where(low, x0, pltpu.roll(x2, 64, 1)), jnp.where(low, pltpu.roll(x0, 64, 1), x2)
+    y1, y3 = jnp.where(low, x1, pltpu.roll(x3, 64, 1)), jnp.where(low, pltpu.roll(x1, 64, 1), x3)
+    even = (lane & 32) == 0
+    z0, z1 = jnp.where(even, y0, pltpu.roll(y1, 32, 1)), jnp.where(even, pltpu.roll(y0, 96, 1), y1)
+    z2, z3 = jnp.where(even, y2, pltpu.roll(y3, 32, 1)), jnp.where(even, pltpu.roll(y2, 96, 1), y3)
+    return [z0, z1, z2, z3]
+
+
+def swap_rows(source, base, scratch, at, edge):
+    tiles = edge // 4
+    for c in range(tiles):
+        rows = [source[pl.ds(base + edge * c + g, tiles, stride=4), :] for g in range(4)]
+        for t4, row in enumerate(swap_blocks(rows)):
+            scratch[pl.ds(at + 4 * c + t4, tiles, stride=edge), :] = row
+
+
+def tile_rows(x, edge):
+    tiles = edge // 4
+    return jnp.concatenate([x[:, LANES * c : LANES * (c + 1)] for c in range(tiles)], 0)
+
+
+def wide(ref, at, edge):
+    tiles = edge // 4
+    return jnp.concatenate([ref[pl.ds(at + edge * c, edge), :] for c in range(tiles)], 1)
+
+
+def swap_inner(ref, edge):
+    tiles = edge // 4
+    size = tiles * edge
+    count = ref.shape[0] // size
+    fields = [ref[pl.ds(size * f, size), :] for f in range(count)]
+    whole = [
+        jnp.concatenate([field[edge * c : edge * (c + 1)] for field in fields], 0) for c in range(tiles)
+    ]
+    row = lax.broadcasted_iota(jnp.int32, (LANES, LANES), 0)
+    lane = lane_of((LANES, LANES))
+    for to in range(tiles):
+        total = jnp.zeros((count * edge, LANES), jnp.float32)
+        for c in range(tiles):
+            hit = ((row & (edge - 1)) == 4 * to + lane // edge) & ((lane & (edge - 1)) == 4 * c + row // edge)
+            total = total + dot(whole[c], hit.astype(jnp.float32))
+        for f in range(count):
+            ref[pl.ds(size * f + edge * to, edge), :] = total[edge * f : edge * (f + 1)]
+
+
+def normal_of(near, slot):
+    along_j = (near[1, 0, slot] >= 0) | (near[1, 1, slot] >= 0)
+    return jnp.where(along_j, 1, 2)
+
+
+def local_kernel(near, rates, calcium, buffer, fraction, inverses, ends_of, faces_of, msg, base, us, al, work, other):
+    count, edge = calcium.shape[0], calcium.shape[1]
+    tiles = edge // 4
+    size = tiles * edge
+    first_slot = lax.axis_index("bricks") * count
+    normal = normal_of(near, first_slot)
+    closed = 3 - normal
+    for b in range(count):
+        us[pl.ds(size * 2 * b, size), :] = tile_rows(calcium[b], edge)
+        us[pl.ds(size * (2 * b + 1), size), :] = tile_rows(buffer[b], edge)
+        al[pl.ds(size * b, size), :] = tile_rows(fraction[b], edge)
+
+    @pl.when(normal == 1)
+    def _():
+        swap_inner(us, edge)
+        swap_inner(al, edge)
+
+    lane = lane_of((edge, LANES))
+    inner = lane & (edge - 1)
+    square_row = lax.broadcasted_iota(jnp.int32, (LANES, LANES), 0)
+    square_lane = lane_of((LANES, LANES))
+    on_block = (square_row // edge) == (square_lane // edge)
+    faces_u, faces_y, ends0, ends1 = [], [], [], []
+    for b in range(count):
+        slot = first_slot + b
+        face = jnp.where(near[normal, 1, slot] >= 0, edge - 1, 0)
+        calc = [us[pl.ds(size * 2 * b + edge * c, edge), :] for c in range(tiles)]
+        bound = [us[pl.ds(size * (2 * b + 1) + edge * c, edge), :] for c in range(tiles)]
+        alpha = [al[pl.ds(size * b + edge * c, edge), :] for c in range(tiles)]
+        bind = [KON * x * (BTOT - y) - KOFF * y for x, y in zip(calc, bound)]
+        source_calc = [-w + INFLUX * (1.0 - a) / a for w, a in zip(bind, alpha)]
+        for q, (u, source) in enumerate(((calc, source_calc), (bound, bind))):
+            at = size * (2 * b + q)
+            rate_t, rate_n = rates[b, closed, q], rates[b, normal, q]
+            ahead = [pltpu.roll(x, LANES - edge, 1) for x in u]
+            behind = [pltpu.roll(x, edge, 1) for x in u]
+            f = []
+            for c in range(tiles):
+                x = u[c]
+                next_t = jnp.where(lane < LANES - edge, ahead[c], ahead[c + 1] if c + 1 < tiles else x)
+                last_t = jnp.where(lane >= edge, behind[c], behind[c - 1] if c else x)
+                next_n = jnp.where(inner == edge - 1, x, pltpu.roll(x, LANES - 1, 1))
+                last_n = jnp.where(inner == 0, x, pltpu.roll(x, 1, 1))
+                along = rate_t * (next_t + last_t - 2.0 * x) + rate_n * (next_n + last_n - 2.0 * x)
+                f.append(2.0 * x + 2.0 * along + source[c])
+            g = dot(inverses[b, 0, q], jnp.concatenate(f, 1))
+            for c in range(tiles):
+                work[pl.ds(edge * c, edge), :] = g[:, LANES * c : LANES * (c + 1)]
+            ends0.append(work[pl.ds(0, tiles, stride=edge), :])
+            ends1.append(work[pl.ds(edge - 1, tiles, stride=edge), :])
+            w = tile_rows(g, edge) - 2.0 * us[pl.ds(at, size), :]
+            block = inverses[b, normal, q]
+            block = jnp.concatenate([block] * 4, 1)
+            block = jnp.where(on_block, jnp.concatenate([block] * 4, 0), 0.0)
+            y = dot(w, block)
+            work[pl.ds(0, size), :] = y
+            face_u = jnp.zeros((edge, LANES), jnp.float32)
+            face_y = jnp.zeros((edge, LANES), jnp.float32)
+            for c in range(tiles):
+                shift = (c - face) & (LANES - 1)
+                face_u = face_u + jnp.where(inner == c, pltpu.roll(u[c], shift, 1), 0.0)
+                face_y = face_y + jnp.where(inner == c, pltpu.roll(y[edge * c : edge * (c + 1)], shift, 1), 0.0)
+            faces_u.append(face_u)
+            faces_y.append(face_y)
+            swap_rows(work, 0, other, 0, edge)
+            solved = dot(inverses[b, closed, q], wide(other, 0, edge))
+            for c in range(tiles):
+                other[pl.ds(edge * c, edge), :] = solved[:, LANES * c : LANES * (c + 1)]
+            swap_rows(other, 0, work, 0, edge)
+            base[pl.ds(at, size), :] = us[pl.ds(at, size), :] + work[pl.ds(0, size), :]
+
+    stack0 = jnp.concatenate(swap_blocks(ends0), 0)
+    stack1 = jnp.concatenate(swap_blocks(ends1), 0)
+    both = dot(ends_of[...], jnp.concatenate([stack0, stack1], 1))
+    part_u = dot_lanes(faces_of[...], jnp.concatenate(faces_u, 0))
+    part_y = dot_lanes(faces_of[...], jnp.concatenate(faces_y, 0))
+    fields = swap_blocks([both[:, :LANES], both[:, LANES:], part_u, part_y])
+    for x, part in enumerate(fields):
+        msg[pl.ds(x, edge, stride=8), :] = part
+    for b in range(count):
+        for q in range(2):
+            row = jnp.where(
+                lane == 0,
+                rates[b, 0, q],
+                jnp.where(lane == 1, rates[b, closed, q], jnp.where(lane == 2, rates[b, normal, q], 0.0)),
+            )
+            msg[pl.ds(4 + 2 * b + q, edge, stride=8), :] = row
+
+
+def owner_kernel(near, eigen_of, recv, basis, turned, eigen, out, rows, tail, order):
+    edge = basis.shape[0]
+    slots = near.shape[2]
+    me = lax.axis_index("bricks")
+
+    def find(s, heads):
+        is_head = near[0, 0, s] < 0
+        low, high = heads
+        return jnp.where(is_head & (low < 0), s, low), jnp.where(is_head, s, high)
+
+    low, high = lax.fori_loop(0, slots, find, (jnp.int32(-1), jnp.int32(-1)))
+
+    def walk(x, at):
+        for row in range(2):
+            slot = at[row]
+            place = row * edge + x
+            order[place] = slot
+            start = 8 * (slot // 2) + 2 * (slot % 2)
+            rows[pl.ds(place, 2, stride=2 * edge), :] = recv[pl.ds(start, 2), :]
+            tail[pl.ds(place, 2, stride=2 * edge), :] = recv[pl.ds(start + 4, 2), :]
+        return tuple(jnp.maximum(near[0, 1, slot], 0) for slot in at)
+
+    lax.fori_loop(0, edge, walk, (low, high))
+    normal = normal_of(near, low)
+    up = near[normal, 1, low] >= 0
+    touch = up | (near[normal, 0, low] >= 0)
+    face0 = jnp.where(up, edge - 1, 0)
+    face1 = jnp.where(up, 0, edge - 1)
+
+    parts = rows[...].T
+    y0, y1, face_u, face_y = (parts[edge * x : edge * (x + 1)] for x in range(4))
+    params = tail[...].T
+    rate_0, rate_t, rate_n = params[0:1], params[1:2], params[2:3]
+
+    lane = lane_of((1, LANES))
+    place = lane & (edge - 1)
+    first_row = (lane & edge) == 0
+    face = jnp.where(first_row, face0, face1)
+    v = basis[...]
+    vt = turned[...]
+    lam = eigen[...]
+
+    def partner(x):
+        return jnp.where(first_row, pltpu.roll(x, LANES - edge, 1), pltpu.roll(x, edge, 1))
+
+    def after(x, s=1):
+        return pltpu.roll(x, LANES - s, 1)
+
+    def before(x, s=1):
+        return pltpu.roll(x, s, 1)
+
+    damp_0 = 1.0 / (1.0 + lam * rate_0)
+    damp_n = 1.0 / (1.0 + lam * rate_n)
+    damp_t = 1.0 / (1.0 + eigen_of[me] * rate_t)
+    other_n = partner(rate_n)
+    g = jnp.where(touch, 2.0 * rate_n * other_n / (rate_n + other_n), 0.0)
+    cross = 2.0 * g * (partner(face_u) - face_u)
+    first_vec = vt[0:edge, 0:1]
+    last_vec = vt[edge - 1 : edge, :]
+    v_first, v_last = v[:, 0:1], v[:, edge - 1 : edge]
+    pieces = dot(
+        vt,
+        jnp.concatenate(
+            [
+                damp_0 * dot(v, cross),
+                damp_0 * v_first,
+                damp_0 * v_last,
+                damp_n * jnp.where(face == 0, v_first, v_last),
+            ],
+            1,
+        ),
+    )
+    spread, col_0, col_1, col_n = (pieces[:, LANES * x : LANES * (x + 1)] for x in range(4))
+    depth = lax.broadcasted_iota(jnp.int32, (edge, LANES), 0)
+    at_face = depth == face
+    y0 = y0 + jnp.where(at_face, spread[0:1], 0.0)
+    y1 = y1 + jnp.where(at_face, spread[edge - 1 : edge], 0.0)
+
+    near_c, far_c = col_0[0:1], col_0[edge - 1 : edge]
+    inv_rate = 1.0 / rate_0
+    open_face = place < edge - 1
+    diag = jnp.where(open_face, 0.5 * (inv_rate + after(inv_rate)) + near_c + after(near_c), 1.0)
+    lower = jnp.where(open_face & (place > 0), -far_c, 0.0)
+    upper = jnp.where(place < edge - 2, -after(far_c), 0.0)
+    right = jnp.where(open_face, y1 - after(y0), 0.0)
+    step = 1
+    while step < edge:
+        back = -lower / before(diag, step)
+        fore = -upper / after(diag, step)
+        diag = diag + back * before(upper, step) + fore * after(lower, step)
+        right = right + back * before(right, step) + fore * after(right, step)
+        lower = back * before(lower, step)
+        upper = fore * after(upper, step)
+        step *= 2
+    flux_up = right / diag
+    flux_down = jnp.where(place > 0, before(flux_up), 0.0)
+
+    end_n = jnp.where(face == 0, col_n[0:1], col_n[edge - 1 : edge])
+    weight_down = jnp.sum(col_n * flux_down, 0, keepdims=True)
+    weight_up = jnp.sum(col_n * flux_up, 0, keepdims=True)
+    reach = face_y
+    halo = end_n * spread + col_0 * weight_down - col_1 * weight_up
+    reach_t = jnp.where(normal == 2, damp_t, 1.0)
+    ends = reach_t * (reach + halo)
+    jump = g * (ends - partner(ends)) / (1.0 + g * (end_n + partner(end_n)))
+    face_out = jnp.where(normal == 2, damp_t * spread - jump, damp_t * (spread - jump))
+    lines = dot(v, jnp.concatenate([flux_down, flux_up], 1))
+    lines = jnp.concatenate([damp_n, damp_n], 1) * lines
+    lines = dot(vt, lines)
+    packed = jnp.concatenate(
+        [
+            damp_t * lines[:, :LANES],
+            damp_t * lines[:, LANES:],
+            face_out,
+            jnp.zeros((edge, LANES), jnp.float32),
+        ],
+        0,
+    )
+    rows[...] = packed.T
+
+    def hand_out(x, carry):
+        slot = order[x]
+        out[pl.ds(4 * (slot // 2) + 2 * (slot % 2), 2), :] = rows[pl.ds(x, 2, stride=2 * edge), :]
+        return carry
+
+    lax.fori_loop(0, slots, hand_out, 0)
+
+
+def update_kernel(near, recv, base, inverses, spread_of, calcium_next, buffer_next, work):
+    count, edge = calcium_next.shape[0], calcium_next.shape[1]
+    tiles = edge // 4
+    size = tiles * edge
+    first_slot = lax.axis_index("bricks") * count
+    normal = normal_of(near, first_slot)
+    lane = lane_of((edge, LANES))
+    fields = [recv[pl.ds(x, edge, stride=2 * count), :] for x in range(2 * count)]
+    low, high, face_part, _ = swap_blocks(fields)
+    turn = jnp.concatenate([face_part, jnp.zeros((LANES - edge, LANES), jnp.float32)], 0).T[:, :edge]
+    expand = wide(spread_of, 0, edge)
+    face_wide = dot(turn, expand)
+    group = lane // edge
+
+    def repeat(x, at):
+        x = jnp.where(group == at, x, 0.0)
+        x = x + pltpu.roll(x, 64, 1)
+        return x + pltpu.roll(x, 32, 1)
+
+    for b in range(count):
+        slot = first_slot + b
+        face = jnp.where(near[normal, 1, slot] >= 0, edge - 1, 0)
+        for q in range(2):
+            x = 2 * b + q
+            at = size * x
+            low_x, high_x = repeat(low, x), repeat(high, x)
+            col_0 = inverses[b, 0, q, :, 0:1]
+            col_1 = inverses[b, 0, q, :, edge - 1 : edge]
+            row_n = inverses[b, normal, q, pl.ds(face, 1), :]
+            row_n = jnp.concatenate([row_n] * 4, 1)
+            for c in range(tiles):
+                basis_c = spread_of[pl.ds(edge * c, edge), :]
+                row_low = jnp.sum(basis_c * low_x, 0, keepdims=True)
+                row_high = jnp.sum(basis_c * high_x, 0, keepdims=True)
+                add = face_wide[edge * x : edge * (x + 1), LANES * c : LANES * (c + 1)] * row_n
+                work[pl.ds(at + edge * c, edge), :] = (
+                    base[pl.ds(at + edge * c, edge), :] + col_0 * row_low - col_1 * row_high + add
+                )
+
+    @pl.when(normal == 1)
+    def _():
+        swap_inner(work, edge)
+
+    for b in range(count):
+        for q, ref in enumerate((calcium_next, buffer_next)):
+            for c in range(tiles):
+                ref[b, :, LANES * c : LANES * (c + 1)] = work[pl.ds(size * (2 * b + q) + edge * c, edge), :]
+
+
+def fast_body(calcium, buffer, fraction, rates, inverses, neighbors, ranks):
+    count, edge = calcium.shape[0], calcium.shape[1]
+    devices = lax.axis_size("bricks")
+    tiles = edge // 4
+    size = tiles * edge
+    f32 = jnp.float32
+    basis, eigen = cosine_basis(edge)
+    place = np.arange(edge)
+    ends_of = np.zeros((edge, edge))
+    ends_of[:, (place % 4) * tiles + place // 4] = basis
+    faces_of = np.zeros((edge, LANES))
+    faces_of[:, (place % 4) * edge + place // 4] = basis
+    spread_of = np.repeat(basis, edge, 1).reshape(edge, tiles, LANES).transpose(1, 0, 2).reshape(size, LANES)
+    smem = pl.BlockSpec(memory_space=pltpu.SMEM)
+    vmem = pl.BlockSpec(memory_space=pltpu.VMEM)
+    params = pltpu.CompilerParams(vmem_limit_bytes=48 * 2**20)
+    const = lambda x: jnp.asarray(x, f32)
+
+    msg, base = pl.pallas_call(
+        local_kernel,
+        out_shape=(
+            jax.ShapeDtypeStruct((devices * 8, LANES), f32),
+            jax.ShapeDtypeStruct((2 * count * size, LANES), f32),
+        ),
+        in_specs=[smem, smem] + [vmem] * 6,
+        out_specs=(vmem, vmem),
+        scratch_shapes=[
+            pltpu.VMEM((2 * count * size, LANES), f32),
+            pltpu.VMEM((count * size, LANES), f32),
+            pltpu.VMEM((size, LANES), f32),
+            pltpu.VMEM((size, LANES), f32),
+        ],
+        compiler_params=params,
+        name="local_solutions",
+    )(neighbors, rates, calcium, buffer, fraction, inverses, const(ends_of), const(faces_of))
+    recv = lax.all_to_all(msg.reshape(devices, 8, LANES), "bricks", 0, 0, tiled=True)
+    reply = pl.pallas_call(
+        owner_kernel,
+        out_shape=jax.ShapeDtypeStruct((devices * 2 * count, LANES), f32),
+        in_specs=[smem, smem] + [vmem] * 4,
+        out_specs=vmem,
+        scratch_shapes=[
+            pltpu.VMEM((LANES, LANES), f32),
+            pltpu.VMEM((LANES, LANES), f32),
+            pltpu.SMEM((devices * count,), jnp.int32),
+        ],
+        compiler_params=params,
+        name="chain_and_face_solves",
+    )(
+        neighbors,
+        const(eigen),
+        recv.reshape(devices * 8, LANES),
+        const(basis),
+        const(basis.T),
+        const(np.tile(eigen[:, None], (1, LANES))),
+    )
+    back = lax.all_to_all(reply.reshape(devices, 2 * count, LANES), "bricks", 0, 0, tiled=True)
+    return pl.pallas_call(
+        update_kernel,
+        out_shape=(
+            jax.ShapeDtypeStruct(calcium.shape, f32),
+            jax.ShapeDtypeStruct(buffer.shape, f32),
+        ),
+        in_specs=[smem] + [vmem] * 4,
+        out_specs=(vmem, vmem),
+        scratch_shapes=[pltpu.VMEM((2 * count * size, LANES), f32)],
+        compiler_params=params,
+        name="rank_three_update",
+    )(neighbors, back.reshape(devices * 2 * count, LANES), base, inverses, const(spread_of))
+
+
+def body(calcium, buffer, fraction, rates, inverses, neighbors, ranks):
+    count, edge = calcium.shape[0], calcium.shape[1]
+    devices = lax.axis_size("bricks")
+    if edge == GX and devices == edge and count == 2 and 4 * edge == LANES:
+        return fast_body(calcium, buffer, fraction, rates, inverses, neighbors, ranks)
+    return general_body(calcium, buffer, fraction, rates, inverses, neighbors, ranks)
+
+
 def solution(mesh):
     in_specs = (
         P("bricks", None, None),

time: 466 us -> 43.5 us (0.09); the launches traced: 458 us -> 43.1 us
  local copies, waits for them, and re-layouts: 206 us -> 6.03 us
  other arithmetic: 74.6 us -> 0 us
  blocking collectives: 88.8 us -> 24.5 us
  waiting for transfers between devices: 43 us -> 0 us
  starting transfers between devices: 24 us -> 0 us
  matrix products: 16.1 us -> 0 us
  Pallas kernels: 0 us -> 11.8 us
  between operations: 5.5 us -> 0.72 us
    all_gather x2 -> x0, blocking collectives: 79.9 us -> none  [the longest x1 42.1 us: body(): lax.all_gather(rates, 'bricks', axis=0, tiled=True)]
    slice x369 -> x0, local copies, waits for them, and re-layouts: 71.7 us -> none  [the longest x168 17.5 us: sorted_solve(): summed = lax.associative_scan(compose_maps, maps, axis=0)]
    all_to_all x7 -> x0, waiting for transfers between devices: 43 us -> none  [the longest x3 21.1 us: solve(): lax.all_to_all(ends, 'bricks', split_axis=3, concat_axis=0, tiled=True)]
    gather x57 -> x0, local copies, waits for them, and re-layouts: 38.4 us -> none  [the longest x18 14 us: chain_order(): pointer = jnp.take(pointer, pointer, axis=0)]
    mul x51 -> x0, local copies, waits for them, and re-layouts: 32.3 us -> none  [the longest x48 30.8 us: compose_affine(): return (first_q * second_q, second_p + second_q * first_p)]
    all_to_all x7 -> x0, starting transfers between devices: 24 us -> none  [the longest x3 8.75 us: solve(): lax.all_to_all(ends, 'bricks', split_axis=3, concat_axis=0, tiled=True)]
    pad x168 -> x0, local copies, waits for them, and re-layouts: 19.4 us -> none  [the longest x108 9.72 us: sorted_solve(): summed = lax.associative_scan(compose_maps, maps, axis=0)]
    add x162 -> x0, other arithmetic: 17.1 us -> none  [the longest x1 5 us: operator(): return c_up * (upper - field) + c_down * (lower - field)]
  transfers between devices with their start and end apart: 7 -> 0, of which waited for: 6 -> 0; matrix products, arithmetic and copies ran while one was open for 40% -> 0% of each run, Pallas kernels for 0% -> 0%
where the time goes in v1:
time: 43.5 us; the launch traced here: 43.1 us
  blocking collectives  24.5 us (56%)
  Pallas kernels  11.8 us (27%)
  local copies, waits for them, and re-layouts  6.03 us (14%)
  between operations  0.72 us (2%)
    all_to_all x1, blocking collectives, fast_body(): lax.all_to_all(msg.reshape(devices, 8, LANES), 'bricks', 0, 0, tiled=True)  15.3 us
    all_to_all x1, blocking collectives, fast_body(): lax.all_to_all(reply.reshape(devices, 2 * count, LANES), 'bricks', 0, 0,...  9.18 us
    unnamed x27, local copies, waits for them, and re-layouts  6.03 us
    pallas_call x1, Pallas kernels, fast_body(): pl.pallas_call(local_kernel, out_shape=(jax.ShapeDtypeStruct((devices * 8...  5.45 us
    pallas_call x1, Pallas kernels, fast_body(): pl.pallas_call(owner_kernel, out_shape=jax.ShapeDtypeStruct((devices * 2...  4.2 us
    pallas_call x1, Pallas kernels, fast_body(): pl.pallas_call(update_kernel, out_shape=(jax.ShapeDtypeStruct(calcium.sha...  2.19 us

profile of v1, /device:TPU:0, one launch (start us, length us, event | category | flops | bytes accessed | tf_op | source)
XLA Modules:
  0.0 43.1 jit_solution(10989902500279631846)
XLA Ops:
  0.6 0.0 copy-start.6
  0.6 0.8 %copy.15.rates = f32[2,3,2]{2,1,0:T(4,128)S(1)} copy(f32[2,3,2]{1,2,0:T(2,128)} %param.17) | data formatting | bytes 96 | tf_op args[3]
  1.4 0.0 copy-done.6
  1.4 0.0 copy-start
  1.4 0.9 %copy-done = f32[2,3,2,32,32]{4,3,2,1,0:T(8,128)S(1)} copy-done((f32[2,3,2,32,32]{4,3,2,1,0:T(8,128)S(1)}, f32[2,3,2,32,32]{4,3,2,1,0:T(8,128)}, u32[]{:S(2)}) %copy-start) | copy-done | bytes 49176
  2.4 0.0 copy-start.2
  2.4 0.9 %copy-done.2 = f32[2,32,1024]{2,1,0:T(8,128)S(1)} copy-done((f32[2,32,1024]{2,1,0:T(8,128)S(1)}, f32[2,32,1024]{2,1,0:T(8,128)}, u32[]{:S(2)}) %copy-start.2) | copy-done | bytes 262168
  3.3 0.0 copy-start.3
  3.3 0.9 %copy-done.3 = f32[2,32,1024]{2,1,0:T(8,128)S(1)} copy-done((f32[2,32,1024]{2,1,0:T(8,128)S(1)}, f32[2,32,1024]{2,1,0:T(8,128)}, u32[]{:S(2)}) %copy-start.3) | copy-done | bytes 262168
  4.3 0.0 copy-start.4
  4.3 0.9 %copy-done.4 = f32[2,32,1024]{2,1,0:T(8,128)S(1)} copy-done((f32[2,32,1024]{2,1,0:T(8,128)S(1)}, f32[2,32,1024]{2,1,0:T(8,128)}, u32[]{:S(2)}) %copy-start.4) | copy-done | bytes 262168
  5.2 0.0 copy-start.7
  5.2 0.7 %copy-done.7 = f32[32,128]{1,0:T(8,128)S(1)} copy-done((f32[32,128]{1,0:T(8,128)S(1)}, f32[32,128]{1,0:T(8,128)}, u32[]{:S(2)}) %copy-start.7) | copy-done | bytes 16408
  5.9 0.0 copy-start.8
  5.9 0.7 %copy-done.8 = f32[32,32]{1,0:T(8,128)S(1)} copy-done((f32[32,32]{1,0:T(8,128)S(1)}, f32[32,32]{1,0:T(8,128)}, u32[]{:S(2)}) %copy-start.8) | copy-done | bytes 4120
  6.6 5.5 %local_solutions.1 = (f32[256,128]{1,0:T(8,128)S(1)}, f32[1024,128]{1,0:T(8,128)S(1)}) custom-call(s32[3,2,64]{2,1,0:T(2,128)S(1)} %copy-done.6, f32[2,3,2]{2,1,0:T(4,128)S(1)} %copy.15.rates, f32[2,32,1024]{2,1,0:T(8,128)S(1)} %copy-done.2, f32[2,32,1024]{2,1,0:T(8,128)S(1)} %copy-done.3, f32[2,32,1024]{2,1,0:T(8,128)S(1)} %copy-done.4, ...), custom_call_target="tpu_custom_call" | custom-call | tf_op jit(solution)/shard_map/local_solutions/pallas_call | solution.py:637
  12.1 0.0 copy-start.9
  12.1 0.0 copy-start.10
  12.1 0.0 copy-start.11
  12.1 0.0 copy-start.12
  12.1 15.3 %all_to_all.10 = f32[32,8,128]{2,1,0:T(8,128)S(1)} all-to-all(f32[32,8,128]{2,1,0:T(8,128)S(1)} %bitcast.7), channel_id=1, replica_groups=mesh['bricks'=32] {'bricks'}, dimensions={0} | all-to-all | bytes 262144 | tf_op jit(solution)/shard_map/all_to_all | solution.py:654
  27.5 0.0 copy-start.1
  27.5 0.0 copy-done.9
  27.5 0.0 copy-done.10
  27.5 0.0 copy-done.11
  27.5 0.0 copy-done.12
  27.5 0.0 copy-start.5
  27.5 4.2 %chain_and_face_solves.1 = f32[128,128]{1,0:T(8,128)S(1)} custom-call(s32[3,2,64]{2,1,0:T(2,128)S(1)} %copy-done.6, f32[32]{0:T(128)S(1)} %copy-done.12, f32[256,128]{1,0:T(8,128)S(1)} %bitcast.4, f32[32,32]{1,0:T(8,128)S(1)} %copy-done.11, f32[32,32]{1,0:T(8,128)S(1)} %copy-done.10, f32[32,128]{1,0:T(8,128)S(1)} %copy-done.9), custom_call_target="tpu_custom_call" | custom-call | tf_op jit(solution)/shard_map/chain_and_face_solves/pallas_call | solution.py:655
  31.7 9.2 %all_to_all.11 = f32[32,4,128]{2,1,0:T(4,128)S(1)} all-to-all(f32[32,4,128]{2,1,0:T(4,128)S(1)} %bitcast.6), channel_id=1, replica_groups=mesh['bricks'=32] {'bricks'}, dimensions={0} | all-to-all | bytes 131072 | tf_op jit(solution)/shard_map/all_to_all | solution.py:675
  40.9 0.0 copy-done.1
  40.9 0.0 copy-done.5
  40.9 2.2 %rank_three_update.1 = (f32[2,32,1024]{2,1,0:T(8,128)}, f32[2,32,1024]{2,1,0:T(8,128)}) custom-call(s32[3,2,64]{2,1,0:T(2,128)S(1)} %copy-done.6, f32[128,128]{1,0:T(8,128)S(1)} %bitcast.5, f32[1024,128]{1,0:T(8,128)S(1)} %get-tuple-element.5.base, f32[2,3,2,32,32]{4,3,2,1,0:T(8,128)S(1)} %copy-done.1, f32[256,128]{1,0:T(8,128)S(1)} %copy-done.5), custom_call_target="tpu_custom_call" | custom-call | tf_op jit(solution)/shard_map/rank_three_update/pallas_call | solution.py:676
Async XLA Ops:
  0.6 0.8 %copy-start.6 = (s32[3,2,64]{2,1,0:T(2,128)S(1)}, s32[3,2,64]{2,1,0:T(2,128)}, u32[]{:S(2)}) copy-start(s32[3,2,64]{2,1,0:T(2,128)} %near.5) | copy-start | bytes 4612
  1.4 0.9 %copy-start = (f32[2,3,2,32,32]{4,3,2,1,0:T(8,128)S(1)}, f32[2,3,2,32,32]{4,3,2,1,0:T(8,128)}, u32[]{:S(2)}) copy-start(f32[2,3,2,32,32]{4,3,2,1,0:T(8,128)} %inverses.3) | copy-start | bytes 147460
  2.4 0.9 %copy-start.2 = (f32[2,32,1024]{2,1,0:T(8,128)S(1)}, f32[2,32,1024]{2,1,0:T(8,128)}, u32[]{:S(2)}) copy-start(f32[2,32,1024]{2,1,0:T(8,128)} %calcium.1) | copy-start | bytes 786436
  3.3 0.9 %copy-start.3 = (f32[2,32,1024]{2,1,0:T(8,128)S(1)}, f32[2,32,1024]{2,1,0:T(8,128)}, u32[]{:S(2)}) copy-start(f32[2,32,1024]{2,1,0:T(8,128)} %buffer.1) | copy-start | bytes 786436
  4.3 0.9 %copy-start.4 = (f32[2,32,1024]{2,1,0:T(8,128)S(1)}, f32[2,32,1024]{2,1,0:T(8,128)}, u32[]{:S(2)}) copy-start(f32[2,32,1024]{2,1,0:T(8,128)} %fraction.1) | copy-start | bytes 786436
  5.2 0.7 %copy-start.7 = (f32[32,128]{1,0:T(8,128)S(1)}, f32[32,128]{1,0:T(8,128)}, u32[]{:S(2)}) copy-start(f32[32,128]{1,0:T(8,128)} %constant.15.clone.faces_of) | copy-start | bytes 49156
  5.9 0.7 %copy-start.8 = (f32[32,32]{1,0:T(8,128)S(1)}, f32[32,32]{1,0:T(8,128)}, u32[]{:S(2)}) copy-start(f32[32,32]{1,0:T(8,128)} %constant.14.clone.ends_of) | copy-start | bytes 12292
  12.1 15.4 %copy-start.9 = (f32[32,128]{1,0:T(8,128)S(1)}, f32[32,128]{1,0:T(8,128)}, u32[]{:S(2)}) copy-start(f32[32,128]{1,0:T(8,128)} %constant.19.clone.eigen) | copy-start | bytes 49156
  12.1 15.4 %copy-start.10 = (f32[32,32]{1,0:T(8,128)S(1)}, f32[32,32]{1,0:T(8,128)}, u32[]{:S(2)}) copy-start(f32[32,32]{1,0:T(8,128)} %constant.18.clone.turned) | copy-start | bytes 12292
  12.1 15.4 %copy-start.11 = (f32[32,32]{1,0:T(8,128)S(1)}, f32[32,32]{1,0:T(8,128)}, u32[]{:S(2)}) copy-start(f32[32,32]{1,0:T(8,128)} %constant.17.clone.basis) | copy-start | bytes 12292
  12.1 15.4 %copy-start.12 = (f32[32]{0:T(128)S(1)}, f32[32]{0:T(128)}, u32[]{:S(2)}) copy-start(f32[32]{0:T(128)} %constant.16.clone.eigen_of) | copy-start | bytes 388
  27.5 13.4 %copy-start.1 = (f32[2,3,2,32,32]{4,3,2,1,0:T(8,128)S(1)}, f32[2,3,2,32,32]{4,3,2,1,0:T(8,128)}, u32[]{:S(2)}) copy-start(f32[2,3,2,32,32]{4,3,2,1,0:T(8,128)} %inverses.3) | copy-start | bytes 147460
  27.5 13.4 %copy-start.5 = (f32[256,128]{1,0:T(8,128)S(1)}, f32[256,128]{1,0:T(8,128)}, u32[]{:S(2)}) copy-start(f32[256,128]{1,0:T(8,128)} %constant.20.clone.spread_of) | copy-start | bytes 393220

commit v2 on v1

--- a/solution.py
+++ b/solution.py
@@ -282,14 +282,53 @@
     return basis, eigen
 
 
+def parts_of(x):
+    high = x.astype(jnp.bfloat16).astype(jnp.float32)
+    return high, (x - high).astype(jnp.bfloat16).astype(jnp.float32)
+
+
+def left_of(x):
+    high, low = parts_of(x)
+    return jnp.concatenate([high, low, high], 1).astype(jnp.bfloat16)
+
+
+def right_of(x, axis=0):
+    high = x.astype(jnp.bfloat16)
+    low = (x - high.astype(jnp.float32)).astype(jnp.bfloat16)
+    return jnp.concatenate([high, high, low], axis)
+
+
+def right_of_swapped(x):
+    high = x.astype(jnp.bfloat16)
+    low = (x - high.astype(jnp.float32)).astype(jnp.bfloat16)
+    return jnp.concatenate([high, low, high], 0)
+
+
+def exact_of(x):
+    high = x.astype(jnp.bfloat16)
+    rest = x - high.astype(jnp.float32)
+    middle = rest.astype(jnp.bfloat16)
+    return jnp.concatenate([high, middle, (rest - middle.astype(jnp.float32)).astype(jnp.bfloat16)], 1)
+
+
 def dot(a, b):
-    return jnp.dot(a, b, precision=lax.Precision.HIGHEST, preferred_element_type=jnp.float32)
+    return jnp.dot(a, b, preferred_element_type=jnp.float32)
 
 
 def dot_lanes(a, b):
-    return lax.dot_general(
-        a, b, (((1,), (1,)), ((), ())), precision=lax.Precision.HIGHEST, preferred_element_type=jnp.float32
-    )
+    return lax.dot_general(a, b, (((1,), (1,)), ((), ())), preferred_element_type=jnp.float32)
+
+
+def host_left(x):
+    high = x.astype(jnp.bfloat16).astype(np.float64)
+    low = (x - high).astype(jnp.bfloat16).astype(np.float64)
+    return np.concatenate([high, low, high], 1)
+
+
+def host_right(x):
+    high = x.astype(jnp.bfloat16).astype(np.float64)
+    low = (x - high).astype(jnp.bfloat16).astype(np.float64)
+    return np.concatenate([high, high, low], 0)
 
 
 def lane_of(shape):
@@ -326,23 +365,23 @@
     return jnp.concatenate([ref[pl.ds(at + edge * c, edge), :] for c in range(tiles)], 1)
 
 
-def swap_inner(ref, edge):
+def swap_inner(refs, edge):
     tiles = edge // 4
-    size = tiles * edge
-    count = ref.shape[0] // size
-    fields = [ref[pl.ds(size * f, size), :] for f in range(count)]
+    fields = [(ref, b) for ref in refs for b in range(ref.shape[0])]
     whole = [
-        jnp.concatenate([field[edge * c : edge * (c + 1)] for field in fields], 0) for c in range(tiles)
+        exact_of(jnp.concatenate([ref[b, :, LANES * c : LANES * (c + 1)] for ref, b in fields], 0))
+        for c in range(tiles)
     ]
     row = lax.broadcasted_iota(jnp.int32, (LANES, LANES), 0)
     lane = lane_of((LANES, LANES))
     for to in range(tiles):
-        total = jnp.zeros((count * edge, LANES), jnp.float32)
+        total = jnp.zeros((len(fields) * edge, LANES), jnp.float32)
         for c in range(tiles):
             hit = ((row & (edge - 1)) == 4 * to + lane // edge) & ((lane & (edge - 1)) == 4 * c + row // edge)
-            total = total + dot(whole[c], hit.astype(jnp.float32))
-        for f in range(count):
-            ref[pl.ds(size * f + edge * to, edge), :] = total[edge * f : edge * (f + 1)]
+            hit = hit.astype(jnp.float32).astype(jnp.bfloat16)
+            total = total + dot(whole[c], jnp.concatenate([hit] * 3, 0))
+        for f, (ref, b) in enumerate(fields):
+            ref[b, :, LANES * to : LANES * (to + 1)] = total[edge * f : edge * (f + 1)]
 
 
 def normal_of(near, slot):
@@ -350,22 +389,39 @@
     return jnp.where(along_j, 1, 2)
 
 
-def local_kernel(near, rates, calcium, buffer, fraction, inverses, ends_of, faces_of, msg, base, us, al, work, other):
+def message_kernel(
+    near_in, rates_in, calcium_in, buffer_in, fraction_in, inverses_in, const_in,
+    msg, solved,
+    near, rates, calcium, buffer, fraction, inverses, const, work, sems,
+):
     count, edge = calcium.shape[0], calcium.shape[1]
     tiles = edge // 4
     size = tiles * edge
+    copies = [
+        pltpu.make_async_copy(source, target, sems.at[x])
+        for x, (source, target) in enumerate(
+            (
+                (near_in, near),
+                (rates_in, rates),
+                (calcium_in, calcium),
+                (buffer_in, buffer),
+                (fraction_in, fraction),
+                (inverses_in, inverses),
+                (const_in, const),
+            )
+        )
+    ]
+    for copy in copies:
+        copy.start()
     first_slot = lax.axis_index("bricks") * count
+    for copy in copies:
+        copy.wait()
     normal = normal_of(near, first_slot)
     closed = 3 - normal
-    for b in range(count):
-        us[pl.ds(size * 2 * b, size), :] = tile_rows(calcium[b], edge)
-        us[pl.ds(size * (2 * b + 1), size), :] = tile_rows(buffer[b], edge)
-        al[pl.ds(size * b, size), :] = tile_rows(fraction[b], edge)
 
     @pl.when(normal == 1)
     def _():
-        swap_inner(us, edge)
-        swap_inner(al, edge)
+        swap_inner((calcium, buffer, fraction), edge)
 
     lane = lane_of((edge, LANES))
     inner = lane & (edge - 1)
@@ -374,16 +430,15 @@
     on_block = (square_row // edge) == (square_lane // edge)
     faces_u, faces_y, ends0, ends1 = [], [], [], []
     for b in range(count):
-        slot = first_slot + b
-        face = jnp.where(near[normal, 1, slot] >= 0, edge - 1, 0)
-        calc = [us[pl.ds(size * 2 * b + edge * c, edge), :] for c in range(tiles)]
-        bound = [us[pl.ds(size * (2 * b + 1) + edge * c, edge), :] for c in range(tiles)]
-        alpha = [al[pl.ds(size * b + edge * c, edge), :] for c in range(tiles)]
+        face = jnp.where(near[normal, 1, first_slot + b] >= 0, edge - 1, 0)
+        calc = [calcium[b, :, LANES * c : LANES * (c + 1)] for c in range(tiles)]
+        bound = [buffer[b, :, LANES * c : LANES * (c + 1)] for c in range(tiles)]
+        alpha = [fraction[b, :, LANES * c : LANES * (c + 1)] for c in range(tiles)]
         bind = [KON * x * (BTOT - y) - KOFF * y for x, y in zip(calc, bound)]
         source_calc = [-w + INFLUX * (1.0 - a) / a for w, a in zip(bind, alpha)]
         for q, (u, source) in enumerate(((calc, source_calc), (bound, bind))):
             at = size * (2 * b + q)
-            rate_t, rate_n = rates[b, closed, q], rates[b, normal, q]
+            rate_t, rate_n = 2.0 * rates[b, q, closed], 2.0 * rates[b, q, normal]
             ahead = [pltpu.roll(x, LANES - edge, 1) for x in u]
             behind = [pltpu.roll(x, edge, 1) for x in u]
             f = []
@@ -393,39 +448,37 @@
                 last_t = jnp.where(lane >= edge, behind[c], behind[c - 1] if c else x)
                 next_n = jnp.where(inner == edge - 1, x, pltpu.roll(x, LANES - 1, 1))
                 last_n = jnp.where(inner == 0, x, pltpu.roll(x, 1, 1))
-                along = rate_t * (next_t + last_t - 2.0 * x) + rate_n * (next_n + last_n - 2.0 * x)
-                f.append(2.0 * x + 2.0 * along + source[c])
-            g = dot(inverses[b, 0, q], jnp.concatenate(f, 1))
+                twice = x + x
+                along = rate_t * (next_t + last_t - twice) + rate_n * (next_n + last_n - twice)
+                f.append(twice + along + source[c])
+            g = dot(left_of(inverses[b, 0, q]), right_of(jnp.concatenate(f, 1)))
             for c in range(tiles):
                 work[pl.ds(edge * c, edge), :] = g[:, LANES * c : LANES * (c + 1)]
             ends0.append(work[pl.ds(0, tiles, stride=edge), :])
             ends1.append(work[pl.ds(edge - 1, tiles, stride=edge), :])
-            w = tile_rows(g, edge) - 2.0 * us[pl.ds(at, size), :]
-            block = inverses[b, normal, q]
-            block = jnp.concatenate([block] * 4, 1)
+            w = jnp.concatenate([g[:, LANES * c : LANES * (c + 1)] - 2.0 * u[c] for c in range(tiles)], 0)
+            block = jnp.concatenate([inverses[b, normal, q]] * 4, 1)
             block = jnp.where(on_block, jnp.concatenate([block] * 4, 0), 0.0)
-            y = dot(w, block)
-            work[pl.ds(0, size), :] = y
+            high = w.astype(jnp.bfloat16)
+            low = (w - high.astype(jnp.float32)).astype(jnp.bfloat16)
+            y = dot(jnp.concatenate([high, high, low], 1), right_of_swapped(block))
+            solved[pl.ds(at, size), :] = y
             face_u = jnp.zeros((edge, LANES), jnp.float32)
             face_y = jnp.zeros((edge, LANES), jnp.float32)
             for c in range(tiles):
                 shift = (c - face) & (LANES - 1)
-                face_u = face_u + jnp.where(inner == c, pltpu.roll(u[c], shift, 1), 0.0)
-                face_y = face_y + jnp.where(inner == c, pltpu.roll(y[edge * c : edge * (c + 1)], shift, 1), 0.0)
+                face_u = jnp.where(inner == c, pltpu.roll(u[c], shift, 1), face_u)
+                face_y = jnp.where(inner == c, pltpu.roll(y[edge * c : edge * (c + 1)], shift, 1), face_y)
             faces_u.append(face_u)
             faces_y.append(face_y)
-            swap_rows(work, 0, other, 0, edge)
-            solved = dot(inverses[b, closed, q], wide(other, 0, edge))
-            for c in range(tiles):
-                other[pl.ds(edge * c, edge), :] = solved[:, LANES * c : LANES * (c + 1)]
-            swap_rows(other, 0, work, 0, edge)
-            base[pl.ds(at, size), :] = us[pl.ds(at, size), :] + work[pl.ds(0, size), :]
 
     stack0 = jnp.concatenate(swap_blocks(ends0), 0)
     stack1 = jnp.concatenate(swap_blocks(ends1), 0)
-    both = dot(ends_of[...], jnp.concatenate([stack0, stack1], 1))
-    part_u = dot_lanes(faces_of[...], jnp.concatenate(faces_u, 0))
-    part_y = dot_lanes(faces_of[...], jnp.concatenate(faces_y, 0))
+    ends_of = const[:, : 3 * edge].astype(jnp.bfloat16)
+    faces_of = const[:, LANES:].astype(jnp.bfloat16)
+    both = dot(ends_of, right_of(jnp.concatenate([stack0, stack1], 1)))
+    part_u = dot_lanes(faces_of, right_of(jnp.concatenate(faces_u, 0), 1))
+    part_y = dot_lanes(faces_of, right_of(jnp.concatenate(faces_y, 0), 1))
     fields = swap_blocks([both[:, :LANES], both[:, LANES:], part_u, part_y])
     for x, part in enumerate(fields):
         msg[pl.ds(x, edge, stride=8), :] = part
@@ -433,53 +486,112 @@
         for q in range(2):
             row = jnp.where(
                 lane == 0,
-                rates[b, 0, q],
-                jnp.where(lane == 1, rates[b, closed, q], jnp.where(lane == 2, rates[b, normal, q], 0.0)),
+                rates[b, q, 0],
+                jnp.where(lane == 1, rates[b, q, closed], jnp.where(lane == 2, rates[b, q, normal], 0.0)),
             )
             msg[pl.ds(4 + 2 * b + q, edge, stride=8), :] = row
 
 
-def owner_kernel(near, eigen_of, recv, basis, turned, eigen, out, rows, tail, order):
-    edge = basis.shape[0]
+def local_kernel(
+    near_in, solved_in, inverses_in,
+    base, pick, flags, edges,
+    near, table, solved, inverses, work, other, sems,
+):
+    count, edge = inverses.shape[0], inverses.shape[3]
+    tiles = edge // 4
+    size = tiles * edge
     slots = near.shape[2]
-    me = lax.axis_index("bricks")
-
-    def find(s, heads):
-        is_head = near[0, 0, s] < 0
-        low, high = heads
-        return jnp.where(is_head & (low < 0), s, low), jnp.where(is_head, s, high)
-
-    low, high = lax.fori_loop(0, slots, find, (jnp.int32(-1), jnp.int32(-1)))
-
-    def walk(x, at):
-        for row in range(2):
-            slot = at[row]
-            place = row * edge + x
-            order[place] = slot
-            start = 8 * (slot // 2) + 2 * (slot % 2)
-            rows[pl.ds(place, 2, stride=2 * edge), :] = recv[pl.ds(start, 2), :]
-            tail[pl.ds(place, 2, stride=2 * edge), :] = recv[pl.ds(start + 4, 2), :]
-        return tuple(jnp.maximum(near[0, 1, slot], 0) for slot in at)
-
-    lax.fori_loop(0, edge, walk, (low, high))
-    normal = normal_of(near, low)
-    up = near[normal, 1, low] >= 0
-    touch = up | (near[normal, 0, low] >= 0)
-    face0 = jnp.where(up, edge - 1, 0)
-    face1 = jnp.where(up, 0, edge - 1)
-
-    parts = rows[...].T
-    y0, y1, face_u, face_y = (parts[edge * x : edge * (x + 1)] for x in range(4))
-    params = tail[...].T
-    rate_0, rate_t, rate_n = params[0:1], params[1:2], params[2:3]
+    copies = [
+        pltpu.make_async_copy(source, target, sems.at[x])
+        for x, (source, target) in enumerate(
+            (
+                (near_in, near),
+                (near_in, table),
+                (solved_in, solved),
+                (inverses_in, inverses),
+            )
+        )
+    ]
+    for copy in copies:
+        copy.start()
+    for copy in copies[:2]:
+        copy.wait()
+    normal = normal_of(near, 0)
+    closed = 3 - normal
+    up = near[normal, 1, 0] >= 0
+    touch = up | (near[normal, 0, 0] >= 0)
+
+    lane = lane_of((8, LANES))
+    back = jnp.broadcast_to(table[0, 0:1, :], (8, slots))
+    back = jnp.concatenate([back] * (LANES // slots), 1)
+    pointer = jnp.where(back >= 0, back, lane & (slots - 1))
+    place = jnp.where(back >= 0, 1, 0)
+
+    def pull(values, index):
+        return jnp.take_along_axis(values, index, axis=1, mode="promise_in_bounds")
+
+    reach = 1
+    while reach < edge:
+        place = place + pull(place, pointer)
+        pointer = pull(pointer, pointer)
+        reach *= 2
+    chain = jnp.where(pointer == pointer[:, 0:1], 0, edge) + place
+    goal = pull(chain, (lane & (edge - 1)) * count + lane // (2 * edge)) + 2 * (lane & edge)
+    hit = lax.broadcasted_iota(jnp.int32, (LANES, LANES), 0) == goal[0:1]
+    pick[...] = hit.astype(jnp.float32).T
+    face = jnp.where(((lane & edge) == 0) == up, edge - 1, 0).astype(jnp.float32)
+    depth = lax.broadcasted_iota(jnp.int32, (8, LANES), 0)
+    angle = jnp.full((8, LANES), lax.axis_index("bricks")).astype(jnp.float32) * (0.5 * math.pi / edge)
+    half = jnp.sin(angle)
+    flags[...] = jnp.where(
+        depth == 0,
+        face,
+        jnp.where(
+            depth == 1,
+            jnp.where(touch, 1.0, 0.0),
+            jnp.where(depth == 2, jnp.where(normal == 2, 1.0, 0.0), 4.0 * half * half),
+        ),
+    )
+
+    for copy in copies[2:]:
+        copy.wait()
+    first_slot = lax.axis_index("bricks") * count
+    for b in range(count):
+        face = jnp.where(near[normal, 1, first_slot + b] >= 0, edge - 1, 0)
+        for q in range(2):
+            x = 2 * b + q
+            at = size * x
+            swap_rows(solved, at, other, 0, edge)
+            whole = dot(left_of(inverses[b, closed, q]), right_of(wide(other, 0, edge)))
+            for c in range(tiles):
+                other[pl.ds(edge * c, edge), :] = whole[:, LANES * c : LANES * (c + 1)]
+            swap_rows(other, 0, work, 0, edge)
+            base[pl.ds(at, size), :] = work[...]
+            row_n = jnp.concatenate([inverses[b, normal, q, pl.ds(face, 1), :]] * 4, 1)
+            edges[x, 0] = jnp.broadcast_to(inverses[b, 0, q, :, 0:1], (edge, LANES))
+            edges[x, 1] = jnp.broadcast_to(inverses[b, 0, q, :, edge - 1 : edge], (edge, LANES))
+            edges[x, 2] = jnp.broadcast_to(row_n, (edge, LANES))
+
+
+def owner_kernel(recv, pick, flags, const, out):
+    edge = const.shape[0]
+    basis = const[:, 0 : 3 * edge].astype(jnp.bfloat16)
+    turned = const[:, LANES : LANES + 3 * edge].astype(jnp.bfloat16)
+    lam = const[:, 2 * LANES : 3 * LANES]
+    v_first = const[:, 3 * LANES : 4 * LANES]
+    v_last = const[:, 4 * LANES : 5 * LANES]
+    face, touch, normal_2, my_lam = flags[0:1], flags[1:2], flags[2:3], flags[3:4]
+
+    hit = pick[...].astype(jnp.bfloat16)
+    data = jnp.concatenate([recv[pl.ds(x, edge, stride=8), :] for x in range(4)], 0).T
+    tail = jnp.concatenate([recv[pl.ds(4 + x, edge, stride=8), :] for x in range(4)], 0).T[:16]
+    parts = dot(exact_of(jnp.concatenate([tail, data], 0)), jnp.concatenate([hit] * 3, 0))
+    rate_0, rate_t, rate_n = parts[0:1], parts[1:2], parts[2:3]
+    y0, y1, face_u, face_y = (parts[16 + edge * x : 16 + edge * (x + 1)] for x in range(4))
 
     lane = lane_of((1, LANES))
     place = lane & (edge - 1)
     first_row = (lane & edge) == 0
-    face = jnp.where(first_row, face0, face1)
-    v = basis[...]
-    vt = turned[...]
-    lam = eigen[...]
 
     def partner(x):
         return jnp.where(first_row, pltpu.roll(x, LANES - edge, 1), pltpu.roll(x, edge, 1))
@@ -492,32 +604,33 @@
 
     damp_0 = 1.0 / (1.0 + lam * rate_0)
     damp_n = 1.0 / (1.0 + lam * rate_n)
-    damp_t = 1.0 / (1.0 + eigen_of[me] * rate_t)
+    damp_t = 1.0 / (1.0 + my_lam * rate_t)
     other_n = partner(rate_n)
-    g = jnp.where(touch, 2.0 * rate_n * other_n / (rate_n + other_n), 0.0)
+    g = jnp.where(touch > 0.5, 2.0 * rate_n * other_n / (rate_n + other_n), 0.0)
     cross = 2.0 * g * (partner(face_u) - face_u)
-    first_vec = vt[0:edge, 0:1]
-    last_vec = vt[edge - 1 : edge, :]
-    v_first, v_last = v[:, 0:1], v[:, edge - 1 : edge]
+    near_c = jnp.sum(damp_0 * v_first * v_first, 0, keepdims=True)
+    far_c = jnp.sum(damp_0 * v_first * v_last, 0, keepdims=True)
+    end_n = jnp.sum(damp_n * v_first * v_first, 0, keepdims=True)
     pieces = dot(
-        vt,
-        jnp.concatenate(
-            [
-                damp_0 * dot(v, cross),
-                damp_0 * v_first,
-                damp_0 * v_last,
-                damp_n * jnp.where(face == 0, v_first, v_last),
-            ],
-            1,
+        turned,
+        right_of(
+            jnp.concatenate(
+                [
+                    damp_0 * dot(basis, right_of(cross)),
+                    damp_0 * v_first,
+                    damp_0 * v_last,
+                    damp_n * jnp.where(face < 0.5, v_first, v_last),
+                ],
+                1,
+            )
         ),
     )
     spread, col_0, col_1, col_n = (pieces[:, LANES * x : LANES * (x + 1)] for x in range(4))
-    depth = lax.broadcasted_iota(jnp.int32, (edge, LANES), 0)
+    depth = lax.broadcasted_iota(jnp.int32, (edge, LANES), 0).astype(jnp.float32)
     at_face = depth == face
     y0 = y0 + jnp.where(at_face, spread[0:1], 0.0)
     y1 = y1 + jnp.where(at_face, spread[edge - 1 : edge], 0.0)
 
-    near_c, far_c = col_0[0:1], col_0[edge - 1 : edge]
     inv_rate = 1.0 / rate_0
     open_face = place < edge - 1
     diag = jnp.where(open_face, 0.5 * (inv_rate + after(inv_rate)) + near_c + after(near_c), 1.0)
@@ -526,8 +639,9 @@
     right = jnp.where(open_face, y1 - after(y0), 0.0)
     step = 1
     while step < edge:
-        back = -lower / before(diag, step)
-        fore = -upper / after(diag, step)
+        inverse = 1.0 / diag
+        back = -lower * before(inverse, step)
+        fore = -upper * after(inverse, step)
         diag = diag + back * before(upper, step) + fore * after(lower, step)
         right = right + back * before(right, step) + fore * after(right, step)
         lower = back * before(lower, step)
@@ -536,84 +650,73 @@
     flux_up = right / diag
     flux_down = jnp.where(place > 0, before(flux_up), 0.0)
 
-    end_n = jnp.where(face == 0, col_n[0:1], col_n[edge - 1 : edge])
     weight_down = jnp.sum(col_n * flux_down, 0, keepdims=True)
     weight_up = jnp.sum(col_n * flux_up, 0, keepdims=True)
-    reach = face_y
-    halo = end_n * spread + col_0 * weight_down - col_1 * weight_up
-    reach_t = jnp.where(normal == 2, damp_t, 1.0)
-    ends = reach_t * (reach + halo)
-    jump = g * (ends - partner(ends)) / (1.0 + g * (end_n + partner(end_n)))
-    face_out = jnp.where(normal == 2, damp_t * spread - jump, damp_t * (spread - jump))
-    lines = dot(v, jnp.concatenate([flux_down, flux_up], 1))
-    lines = jnp.concatenate([damp_n, damp_n], 1) * lines
-    lines = dot(vt, lines)
+    ends = face_y + end_n * spread + col_0 * weight_down - col_1 * weight_up
+    ends = jnp.where(normal_2 > 0.5, damp_t, 1.0) * ends
+    jump = g / (1.0 + g * (end_n + partner(end_n))) * (ends - partner(ends))
+    face_out = jnp.where(normal_2 > 0.5, damp_t * spread - jump, damp_t * (spread - jump))
+    lines = dot(basis, right_of(jnp.concatenate([flux_down, flux_up], 1)))
+    lines = dot(turned, right_of(jnp.concatenate([damp_n * damp_t] * 2, 1) * lines))
     packed = jnp.concatenate(
-        [
-            damp_t * lines[:, :LANES],
-            damp_t * lines[:, LANES:],
-            face_out,
-            jnp.zeros((edge, LANES), jnp.float32),
-        ],
-        0,
-    )
-    rows[...] = packed.T
-
-    def hand_out(x, carry):
-        slot = order[x]
-        out[pl.ds(4 * (slot // 2) + 2 * (slot % 2), 2), :] = rows[pl.ds(x, 2, stride=2 * edge), :]
-        return carry
-
-    lax.fori_loop(0, slots, hand_out, 0)
-
-
-def update_kernel(near, recv, base, inverses, spread_of, calcium_next, buffer_next, work):
-    count, edge = calcium_next.shape[0], calcium_next.shape[1]
+        [lines[:, :LANES], lines[:, LANES:], face_out, jnp.zeros((edge, LANES), jnp.float32)], 0
+    )
+    reply = dot_lanes(jnp.concatenate([hit] * 3, 1), exact_of(packed))
+    for x in range(4):
+        out[pl.ds(x, edge, stride=4), :] = reply[edge * x : edge * (x + 1)]
+
+
+def update_kernel(
+    recv, base, edges, flags, calcium, buffer, const,
+    calcium_out, buffer_out,
+    calcium_next, buffer_next, work, sems,
+):
+    count, edge = calcium.shape[0], calcium.shape[1]
     tiles = edge // 4
     size = tiles * edge
-    first_slot = lax.axis_index("bricks") * count
-    normal = normal_of(near, first_slot)
-    lane = lane_of((edge, LANES))
+    swapped = flags[2, 0] < 0.5
+    old = jnp.where(flags[2:3] < 0.5, 0.0, 1.0)
     fields = [recv[pl.ds(x, edge, stride=2 * count), :] for x in range(2 * count)]
     low, high, face_part, _ = swap_blocks(fields)
-    turn = jnp.concatenate([face_part, jnp.zeros((LANES - edge, LANES), jnp.float32)], 0).T[:, :edge]
-    expand = wide(spread_of, 0, edge)
-    face_wide = dot(turn, expand)
-    group = lane // edge
-
-    def repeat(x, at):
-        x = jnp.where(group == at, x, 0.0)
-        x = x + pltpu.roll(x, 64, 1)
-        return x + pltpu.roll(x, 32, 1)
-
+    high_s, low_s = parts_of(face_part)
+    turn = jnp.concatenate([high_s, low_s, high_s, jnp.zeros_like(high_s)], 0).T.astype(jnp.bfloat16)
+    face_wide = dot(turn, const[:, LANES:].astype(jnp.bfloat16))
+    lines = dot(const[:edge, : 3 * edge].astype(jnp.bfloat16), right_of(jnp.concatenate([low, high], 1)))
+    rows = []
+    for e in range(2):
+        work[pl.ds(edge * e, edge), :] = lines[:, LANES * e : LANES * (e + 1)]
+        rows.append(swap_blocks([work[pl.ds(edge * e + t4, tiles, stride=4), :] for t4 in range(4)]))
+
+    stores = [
+        pltpu.make_async_copy(source.at[b], to.at[b], sems.at[2 * b + q])
+        for b in range(count)
+        for q, (source, to) in enumerate(((calcium_next, calcium_out), (buffer_next, buffer_out)))
+    ]
     for b in range(count):
-        slot = first_slot + b
-        face = jnp.where(near[normal, 1, slot] >= 0, edge - 1, 0)
-        for q in range(2):
+        for q, (ref, now) in enumerate(((calcium_next, calcium), (buffer_next, buffer))):
             x = 2 * b + q
             at = size * x
-            low_x, high_x = repeat(low, x), repeat(high, x)
-            col_0 = inverses[b, 0, q, :, 0:1]
-            col_1 = inverses[b, 0, q, :, edge - 1 : edge]
-            row_n = inverses[b, normal, q, pl.ds(face, 1), :]
-            row_n = jnp.concatenate([row_n] * 4, 1)
+            col_0, col_1, row_n = edges[x, 0], edges[x, 1], edges[x, 2]
             for c in range(tiles):
-                basis_c = spread_of[pl.ds(edge * c, edge), :]
-                row_low = jnp.sum(basis_c * low_x, 0, keepdims=True)
-                row_high = jnp.sum(basis_c * high_x, 0, keepdims=True)
-                add = face_wide[edge * x : edge * (x + 1), LANES * c : LANES * (c + 1)] * row_n
-                work[pl.ds(at + edge * c, edge), :] = (
-                    base[pl.ds(at + edge * c, edge), :] + col_0 * row_low - col_1 * row_high + add
+                part = slice(LANES * c, LANES * (c + 1))
+                ref[b, :, part] = (
+                    (base[pl.ds(at + edge * c, edge), :] + old * now[b, :, part])
+                    + face_wide[edge * x : edge * (x + 1), part] * row_n
+                    + (col_0 * rows[0][x][c : c + 1] - col_1 * rows[1][x][c : c + 1])
                 )
-
-    @pl.when(normal == 1)
+            stores[x].start()
+    for store in stores:
+        store.wait()
+
+    @pl.when(swapped)
     def _():
-        swap_inner(work, edge)
-
-    for b in range(count):
-        for q, ref in enumerate((calcium_next, buffer_next)):
-            for c in range(tiles):
-                ref[b, :, LANES * c : LANES * (c + 1)] = work[pl.ds(size * (2 * b + q) + edge * c, edge), :]
+        swap_inner((calcium_next, buffer_next), edge)
+        calcium_next[...] = calcium_next[...] + calcium[...]
+        buffer_next[...] = buffer_next[...] + buffer[...]
+        for store in stores:
+            store.start()
+        for store in stores:
+            store.wait()
 
 
 def fast_body(calcium, buffer, fraction, rates, inverses, neighbors, ranks):
@@ -628,63 +731,92 @@
     ends_of[:, (place % 4) * tiles + place // 4] = basis
     faces_of = np.zeros((edge, LANES))
     faces_of[:, (place % 4) * edge + place // 4] = basis
-    spread_of = np.repeat(basis, edge, 1).reshape(edge, tiles, LANES).transpose(1, 0, 2).reshape(size, LANES)
+    pad = lambda x: np.pad(x, ((0, 0), (0, LANES - x.shape[1])))
+    message_const = np.concatenate([pad(host_left(ends_of)), host_left(faces_of)], 1)
+    lanes_of = lambda x: np.tile(x[:, None], (1, LANES))
+    owner_const = np.concatenate(
+        [pad(host_left(basis)), pad(host_left(basis.T))]
+        + [lanes_of(x) for x in (eigen, basis[:, 0], basis[:, -1])],
+        1,
+    )
+    expand = np.pad(host_right(np.repeat(basis, edge, 1)), ((0, LANES - 3 * edge), (0, 0)))
+    back_const = np.pad(pad(host_left(basis.T)), ((0, LANES - edge), (0, 0)))
+    update_const = np.concatenate([back_const, expand], 1)
     smem = pl.BlockSpec(memory_space=pltpu.SMEM)
     vmem = pl.BlockSpec(memory_space=pltpu.VMEM)
+    hbm = pl.BlockSpec(memory_space=pltpu.HBM)
     params = pltpu.CompilerParams(vmem_limit_bytes=48 * 2**20)
     const = lambda x: jnp.asarray(x, f32)
-
-    msg, base = pl.pallas_call(
+    field = jax.ShapeDtypeStruct(calcium.shape, f32)
+    tall = jax.ShapeDtypeStruct((2 * count * size, LANES), f32)
+
+    stay = lambda x: pltpu.with_memory_space_constraint(x, pltpu.HBM)
+    msg, solved = pl.pallas_call(
+        message_kernel,
+        out_shape=(jax.ShapeDtypeStruct((devices * 8, LANES), f32), tall),
+        in_specs=[hbm] * 7,
+        out_specs=(vmem, vmem),
+        scratch_shapes=[
+            pltpu.SMEM(neighbors.shape, jnp.int32),
+            pltpu.SMEM((count, 2, 3), f32),
+            pltpu.VMEM(calcium.shape, f32),
+            pltpu.VMEM(calcium.shape, f32),
+            pltpu.VMEM(fraction.shape, f32),
+            pltpu.VMEM(inverses.shape, f32),
+            pltpu.VMEM(message_const.shape, f32),
+            pltpu.VMEM((size, LANES), f32),
+            pltpu.SemaphoreType.DMA((7,)),
+        ],
+        compiler_params=pltpu.CompilerParams(vmem_limit_bytes=48 * 2**20),
+        name="message",
+    )(*(stay(x) for x in (neighbors, rates.transpose(0, 2, 1), calcium, buffer, fraction, inverses, const(message_const))))
+    recv = lax.all_to_all(msg.reshape(devices, 8, LANES), "bricks", 0, 0, tiled=True)
+    base, pick, flags, edges = pl.pallas_call(
         local_kernel,
         out_shape=(
-            jax.ShapeDtypeStruct((devices * 8, LANES), f32),
-            jax.ShapeDtypeStruct((2 * count * size, LANES), f32),
+            tall,
+            jax.ShapeDtypeStruct((LANES, LANES), f32),
+            jax.ShapeDtypeStruct((8, LANES), f32),
+            jax.ShapeDtypeStruct((2 * count, 3, edge, LANES), f32),
         ),
-        in_specs=[smem, smem] + [vmem] * 6,
-        out_specs=(vmem, vmem),
+        in_specs=[hbm] * 3,
+        out_specs=(vmem,) * 4,
         scratch_shapes=[
-            pltpu.VMEM((2 * count * size, LANES), f32),
-            pltpu.VMEM((count * size, LANES), f32),
+            pltpu.SMEM(neighbors.shape, jnp.int32),
+            pltpu.VMEM(neighbors.shape, jnp.int32),
+            pltpu.VMEM(tall.shape, f32),
+            pltpu.VMEM(inverses.shape, f32),
             pltpu.VMEM((size, LANES), f32),
             pltpu.VMEM((size, LANES), f32),
+            pltpu.SemaphoreType.DMA((4,)),
         ],
-        compiler_params=params,
-        name="local_solutions",
-    )(neighbors, rates, calcium, buffer, fraction, inverses, const(ends_of), const(faces_of))
-    recv = lax.all_to_all(msg.reshape(devices, 8, LANES), "bricks", 0, 0, tiled=True)
+        compiler_params=pltpu.CompilerParams(vmem_limit_bytes=48 * 2**20),
+        cost_estimate=pl.CostEstimate(flops=2 * 10**7, bytes_accessed=4 * 10**6, transcendentals=0),
+        name="local_solution",
+    )(neighbors, solved, inverses)
     reply = pl.pallas_call(
         owner_kernel,
         out_shape=jax.ShapeDtypeStruct((devices * 2 * count, LANES), f32),
-        in_specs=[smem, smem] + [vmem] * 4,
+        in_specs=[vmem] * 4,
         out_specs=vmem,
-        scratch_shapes=[
-            pltpu.VMEM((LANES, LANES), f32),
-            pltpu.VMEM((LANES, LANES), f32),
-            pltpu.SMEM((devices * count,), jnp.int32),
-        ],
         compiler_params=params,
         name="chain_and_face_solves",
-    )(
-        neighbors,
-        const(eigen),
-        recv.reshape(devices * 8, LANES),
-        const(basis),
-        const(basis.T),
-        const(np.tile(eigen[:, None], (1, LANES))),
-    )
+    )(recv.reshape(devices * 8, LANES), pick, flags, const(owner_const))
     back = lax.all_to_all(reply.reshape(devices, 2 * count, LANES), "bricks", 0, 0, tiled=True)
     return pl.pallas_call(
         update_kernel,
-        out_shape=(
-            jax.ShapeDtypeStruct(calcium.shape, f32),
-            jax.ShapeDtypeStruct(buffer.shape, f32),
-        ),
-        in_specs=[smem] + [vmem] * 4,
-        out_specs=(vmem, vmem),
-        scratch_shapes=[pltpu.VMEM((2 * count * size, LANES), f32)],
+        out_shape=(field, field),
+        in_specs=[vmem] * 7,
+        out_specs=(hbm, hbm),
+        scratch_shapes=[
+            pltpu.VMEM(calcium.shape, f32),
+            pltpu.VMEM(buffer.shape, f32),
+            pltpu.VMEM((2 * edge, LANES), f32),
+            pltpu.SemaphoreType.DMA((2 * count,)),
+        ],
         compiler_params=params,
         name="rank_three_update",
-    )(neighbors, back.reshape(devices * 2 * count, LANES), base, inverses, const(spread_of))
+    )(back.reshape(devices * 2 * count, LANES), base, edges, flags, calcium, buffer, const(update_const))
 
 
 def body(calcium, buffer, fraction, rates, inverses, neighbors, ranks):

time: 43.5 us -> 31.9 us (0.73)
  blocking collectives: 24.5 us -> 9.18 us
  starting transfers between devices: 0 us -> 7.3 us
  local copies, waits for them, and re-layouts: 6.03 us -> 0.04 us
  waiting for transfers between devices: 0 us -> 5.49 us
  Pallas kernels: 11.8 us -> 8.99 us
    all_to_all x1 -> x0, blocking collectives: 15.3 us -> none  [fast_body(): lax.all_to_all(msg.reshape(devices, 8, LANES), 'bricks', 0, 0, tiled=True)]
    all_to_all x0 -> x1, starting transfers between devices: none -> 7.3 us  [fast_body(): lax.all_to_all(msg.reshape(devices, 8, LANES), 'bricks', 0, 0, tiled=True)]
    unnamed x27 -> x12, local copies, waits for them, and re-layouts: 6.03 us -> 0.04 us
    all_to_all x0 -> x1, waiting for transfers between devices: none -> 5.49 us  [fast_body(): lax.all_to_all(msg.reshape(devices, 8, LANES), 'bricks', 0, 0, tiled=True)]
    pallas_call x1, Pallas kernels: 4.2 us -> 1.5 us  [fast_body(): pl.pallas_call(owner_kernel, out_shape=jax.ShapeDtypeStruct((devices * 2...]
    pallas_call x2 -> x3, Pallas kernels: 7.64 us -> 7.49 us  [the longest x1 3.36 us: fast_body(): pl.pallas_call(message_kernel, out_shape=(jax.ShapeDtypeStruct((devices *...]
  transfers between devices with their start and end apart: 0 -> 1, of which waited for: 0 -> 1; matrix products, arithmetic and copies ran while one was open for 0% -> 0% of each run, Pallas kernels for 0% -> 8%
where the time goes in v2:
time: 31.9 us; the launch traced here: 31.7 us
  blocking collectives  9.18 us (29%)
  Pallas kernels  8.99 us (28%)
  starting transfers between devices  7.3 us (23%)
  waiting for transfers between devices  5.49 us (17%)
  between operations  0.73 us (2%)
    all_to_all x1, blocking collectives, fast_body(): lax.all_to_all(reply.reshape(devices, 2 * count, LANES), 'bricks', 0, 0,...  9.18 us
    all_to_all x1, starting transfers between devices, fast_body(): lax.all_to_all(msg.reshape(devices, 8, LANES), 'bricks', 0, 0, tiled=True)  7.3 us
    all_to_all x1, waiting for transfers between devices, fast_body(): lax.all_to_all(msg.reshape(devices, 8, LANES), 'bricks', 0, 0, tiled=True)  5.49 us
    pallas_call x1, Pallas kernels, fast_body(): pl.pallas_call(message_kernel, out_shape=(jax.ShapeDtypeStruct((devices *...  3.36 us
    pallas_call x1, Pallas kernels, fast_body(): pl.pallas_call(local_kernel, out_shape=(tall, jax.ShapeDtypeStruct((LANES...  2.67 us
    pallas_call x1, Pallas kernels, fast_body(): pl.pallas_call(owner_kernel, out_shape=jax.ShapeDtypeStruct((devices * 2...  1.5 us
    pallas_call x1, Pallas kernels, fast_body(): pl.pallas_call(update_kernel, out_shape=(field, field), in_specs=[vmem] *...  1.45 us
  transfers between devices with their start and end apart: 1, of which 1 were waited for; matrix products, arithmetic and copies ran while one was open for 0% of the time, Pallas kernels for 8%

profile of v2, /device:TPU:0, one launch (start us, length us, event | category | flops | bytes accessed | tf_op | source)
XLA Modules:
  0.0 31.7 jit_solution(6864364400275464227)
XLA Ops:
  0.6 0.0 copy-start.5
  0.6 3.4 %message.1 = (f32[256,128]{1,0:T(8,128)}, f32[1024,128]{1,0:T(8,128)S(1)}) custom-call(s32[3,2,64]{2,1,0:T(2,128)} %near_in.3, f32[2,2,3]{2,1,0:T(2,128)} %bitcast.8, f32[2,32,1024]{2,1,0:T(8,128)} %calcium.1, f32[2,32,1024]{2,1,0:T(8,128)} %buffer.1, f32[2,32,1024]{2,1,0:T(8,128)} %fraction_in.1, f32[2,3,2,32,32]{4,3,2,1,0:T(8,128)} %inverses_in.3, ...), custom_call_target="tpu_custom_call" | custom-call | tf_op jit(solution)/shard_map/message/pallas_call | solution.py:754
  4.0 0.0 copy-start.2
  4.0 0.0 copy-start.4
  4.0 7.3 %all-to-all-start = ((f32[32,8,128]{2,1,0:T(8,128)}), f32[32,8,128]{2,1,0:T(8,128)S(1)}, u32[]{:S(2)}, u32[]{:S(2)}) async-start(f32[32,8,128]{2,1,0:T(8,128)} %bitcast.1), calls=%async_computation | async-start | bytes 262144 | tf_op jit(solution)/shard_map/all_to_all | solution.py:773
  11.3 0.0 copy-done.5
  11.4 0.0 copy-done.2
  11.4 0.0 copy-start.1
  11.4 0.0 copy-start.3
  11.4 2.7 %local_solution.1 = (f32[1024,128]{1,0:T(8,128)S(1)}, f32[128,128]{1,0:T(8,128)S(1)}, f32[8,128]{1,0:T(8,128)S(1)}, f32[4,3,32,128]{3,2,1,0:T(8,128)S(1)}) custom-call(s32[3,2,64]{2,1,0:T(2,128)S(1)} %copy-done.5, f32[1024,128]{1,0:T(8,128)S(1)} %get-tuple-element.9.solved_in, f32[2,3,2,32,32]{4,3,2,1,0:T(8,128)S(1)} %copy-done.2), custom_call_target="tpu_custom_call" | custom-call | flops 20000000 | bytes 4000000 | tf_op jit(solution)/shard_map/local_solution/pallas_call | solution.py:774
  14.1 0.0 copy-start
  14.1 5.5 %all-to-all-done = f32[32,8,128]{2,1,0:T(8,128)S(1)} async-done(((f32[32,8,128]{2,1,0:T(8,128)}), f32[32,8,128]{2,1,0:T(8,128)S(1)}, u32[]{:S(2)}, u32[]{:S(2)}) %all-to-all-start) | async-done | bytes 131104 | tf_op jit(solution)/shard_map/all_to_all | solution.py:773
  19.6 0.0 copy-done.4
  19.6 1.5 %chain_and_face_solves.1 = f32[128,128]{1,0:T(8,128)S(1)} custom-call(f32[256,128]{1,0:T(8,128)S(1)} %bitcast.5, f32[128,128]{1,0:T(8,128)S(1)} %get-tuple-element.10.pick, f32[8,128]{1,0:T(8,128)S(1)} %get-tuple-element.11.flags, f32[32,640]{1,0:T(8,128)S(1)} %copy-done.4), custom_call_target="tpu_custom_call" | custom-call | tf_op jit(solution)/shard_map/chain_and_face_solves/pallas_call | solution.py:797
  21.1 9.2 %all_to_all.10 = f32[32,4,128]{2,1,0:T(4,128)S(1)} all-to-all(f32[32,4,128]{2,1,0:T(4,128)S(1)} %bitcast.6), channel_id=1, replica_groups=mesh['bricks'=32] {'bricks'}, dimensions={0} | all-to-all | bytes 131072 | tf_op jit(solution)/shard_map/all_to_all | solution.py:805
  30.3 0.0 copy-done.1
  30.3 0.0 copy-done.3
  30.3 0.0 copy-done
  30.3 1.5 %rank_three_update.1 = (f32[2,32,1024]{2,1,0:T(8,128)}, f32[2,32,1024]{2,1,0:T(8,128)}) custom-call(f32[128,128]{1,0:T(8,128)S(1)} %bitcast.7, f32[1024,128]{1,0:T(8,128)S(1)} %get-tuple-element.12.base, f32[4,3,32,128]{3,2,1,0:T(8,128)S(1)} %get-tuple-element.13.edges, f32[8,128]{1,0:T(8,128)S(1)} %get-tuple-element.11.flags, f32[2,32,1024]{2,1,0:T(8,128)S(1)} %copy-done, ...), custom_call_target="tpu_custom_call" | custom-call | tf_op jit(solution)/shard_map/rank_three_update/pallas_call | solution.py:806
Async XLA Ops:
  0.6 10.7 %copy-start.5 = (s32[3,2,64]{2,1,0:T(2,128)S(1)}, s32[3,2,64]{2,1,0:T(2,128)}, u32[]{:S(2)}) copy-start(s32[3,2,64]{2,1,0:T(2,128)} %near_in.3) | copy-start | bytes 4612
  4.0 7.3 %copy-start.2 = (f32[2,3,2,32,32]{4,3,2,1,0:T(8,128)S(1)}, f32[2,3,2,32,32]{4,3,2,1,0:T(8,128)}, u32[]{:S(2)}) copy-start(f32[2,3,2,32,32]{4,3,2,1,0:T(8,128)} %inverses_in.3) | copy-start | bytes 147460
  4.0 15.6 %copy-start.4 = (f32[32,640]{1,0:T(8,128)S(1)}, f32[32,640]{1,0:T(8,128)}, u32[]{:S(2)}) copy-start(f32[32,640]{1,0:T(8,128)} %constant.7.clone.const) | copy-start | bytes 245764
  4.0 15.5 %all-to-all-start = ((f32[32,8,128]{2,1,0:T(8,128)}), f32[32,8,128]{2,1,0:T(8,128)S(1)}, u32[]{:S(2)}, u32[]{:S(2)}) async-start(f32[32,8,128]{2,1,0:T(8,128)} %bitcast.1), calls=%async_computation | async-start | bytes 262144 | tf_op jit(solution)/shard_map/all_to_all | solution.py:773
  11.4 18.9 %copy-start.1 = (f32[2,32,1024]{2,1,0:T(8,128)S(1)}, f32[2,32,1024]{2,1,0:T(8,128)}, u32[]{:S(2)}) copy-start(f32[2,32,1024]{2,1,0:T(8,128)} %buffer.1) | copy-start | bytes 786436
  11.4 18.9 %copy-start.3 = (f32[128,1152]{1,0:T(8,128)S(1)}, f32[128,1152]{1,0:T(8,128)}, u32[]{:S(2)}) copy-start(f32[128,1152]{1,0:T(8,128)} %constant.8.clone.const) | copy-start | bytes 1769476
  14.1 16.2 %copy-start = (f32[2,32,1024]{2,1,0:T(8,128)S(1)}, f32[2,32,1024]{2,1,0:T(8,128)}, u32[]{:S(2)}) copy-start(f32[2,32,1024]{2,1,0:T(8,128)} %calcium.1) | copy-start | bytes 786436

commit v3 on v2

--- a/solution.py
+++ b/solution.py
@@ -273,6 +273,9 @@
 LANES = 128
 
 
+ROWS = 5
+
+
 def cosine_basis(edge):
     wave = np.arange(edge)[:, None]
     place = np.arange(edge)[None, :]
@@ -392,7 +395,7 @@
 def message_kernel(
     near_in, rates_in, calcium_in, buffer_in, fraction_in, inverses_in, const_in,
     msg, solved,
-    near, rates, calcium, buffer, fraction, inverses, const, work, sems,
+    near, rates, calcium, buffer, fraction, inverses, const, sems,
 ):
     count, edge = calcium.shape[0], calcium.shape[1]
     tiles = edge // 4
@@ -452,10 +455,8 @@
                 along = rate_t * (next_t + last_t - twice) + rate_n * (next_n + last_n - twice)
                 f.append(twice + along + source[c])
             g = dot(left_of(inverses[b, 0, q]), right_of(jnp.concatenate(f, 1)))
-            for c in range(tiles):
-                work[pl.ds(edge * c, edge), :] = g[:, LANES * c : LANES * (c + 1)]
-            ends0.append(work[pl.ds(0, tiles, stride=edge), :])
-            ends1.append(work[pl.ds(edge - 1, tiles, stride=edge), :])
+            ends0.append(jnp.concatenate([g[0:1, LANES * c : LANES * (c + 1)] for c in range(tiles)], 0))
+            ends1.append(jnp.concatenate([g[edge - 1 : edge, LANES * c : LANES * (c + 1)] for c in range(tiles)], 0))
             w = jnp.concatenate([g[:, LANES * c : LANES * (c + 1)] - 2.0 * u[c] for c in range(tiles)], 0)
             block = jnp.concatenate([inverses[b, normal, q]] * 4, 1)
             block = jnp.where(on_block, jnp.concatenate([block] * 4, 0), 0.0)
@@ -472,24 +473,24 @@
             faces_u.append(face_u)
             faces_y.append(face_y)
 
-    stack0 = jnp.concatenate(swap_blocks(ends0), 0)
-    stack1 = jnp.concatenate(swap_blocks(ends1), 0)
+    stack = jnp.concatenate(swap_blocks(ends0) + swap_blocks(ends1), 0)
     ends_of = const[:, : 3 * edge].astype(jnp.bfloat16)
-    faces_of = const[:, LANES:].astype(jnp.bfloat16)
-    both = dot(ends_of, right_of(jnp.concatenate([stack0, stack1], 1)))
+    faces_of = const[:, LANES : 4 * LANES].astype(jnp.bfloat16)
+    turn = right_of_swapped(jnp.where(on_block, jnp.concatenate([const[:, 4 * LANES :]] * 4, 0), 0.0))
+    stack = dot(right_of(stack, 1), turn)
+    both = dot(ends_of, right_of(jnp.concatenate([stack[:edge], stack[edge:]], 1)))
     part_u = dot_lanes(faces_of, right_of(jnp.concatenate(faces_u, 0), 1))
+    part_u = dot(right_of(part_u, 1), turn)
     part_y = dot_lanes(faces_of, right_of(jnp.concatenate(faces_y, 0), 1))
     fields = swap_blocks([both[:, :LANES], both[:, LANES:], part_u, part_y])
     for x, part in enumerate(fields):
-        msg[pl.ds(x, edge, stride=8), :] = part
+        msg[pl.ds(x, edge, stride=ROWS), :] = part
+    row = jnp.zeros((edge, LANES), jnp.float32)
     for b in range(count):
         for q in range(2):
-            row = jnp.where(
-                lane == 0,
-                rates[b, q, 0],
-                jnp.where(lane == 1, rates[b, q, closed], jnp.where(lane == 2, rates[b, q, normal], 0.0)),
-            )
-            msg[pl.ds(4 + 2 * b + q, edge, stride=8), :] = row
+            for x, rate in enumerate((rates[b, q, 0], rates[b, q, closed], rates[b, q, normal])):
+                row = jnp.where(lane == (2 * b + q) * edge + x, rate, row)
+    msg[pl.ds(4, edge, stride=ROWS), :] = row
 
 
 def local_kernel(
@@ -575,16 +576,16 @@
 
 def owner_kernel(recv, pick, flags, const, out):
     edge = const.shape[0]
-    basis = const[:, 0 : 3 * edge].astype(jnp.bfloat16)
-    turned = const[:, LANES : LANES + 3 * edge].astype(jnp.bfloat16)
-    lam = const[:, 2 * LANES : 3 * LANES]
-    v_first = const[:, 3 * LANES : 4 * LANES]
-    v_last = const[:, 4 * LANES : 5 * LANES]
+    turned = const[:, : 3 * edge].astype(jnp.bfloat16)
+    lam = const[:, LANES : 2 * LANES]
+    v_first = const[:, 2 * LANES : 3 * LANES]
+    v_last = const[:, 3 * LANES : 4 * LANES]
     face, touch, normal_2, my_lam = flags[0:1], flags[1:2], flags[2:3], flags[3:4]
 
     hit = pick[...].astype(jnp.bfloat16)
-    data = jnp.concatenate([recv[pl.ds(x, edge, stride=8), :] for x in range(4)], 0).T
-    tail = jnp.concatenate([recv[pl.ds(4 + x, edge, stride=8), :] for x in range(4)], 0).T[:16]
+    data = jnp.concatenate([recv[pl.ds(x, edge, stride=ROWS), :] for x in range(4)], 0).T
+    tail = recv[pl.ds(4, edge, stride=ROWS), :]
+    tail = jnp.concatenate([tail] + [pltpu.roll(tail, LANES - edge * x, 1) for x in range(1, 4)], 0).T[:16]
     parts = dot(exact_of(jnp.concatenate([tail, data], 0)), jnp.concatenate([hit] * 3, 0))
     rate_0, rate_t, rate_n = parts[0:1], parts[1:2], parts[2:3]
     y0, y1, face_u, face_y = (parts[16 + edge * x : 16 + edge * (x + 1)] for x in range(4))
@@ -611,25 +612,12 @@
     near_c = jnp.sum(damp_0 * v_first * v_first, 0, keepdims=True)
     far_c = jnp.sum(damp_0 * v_first * v_last, 0, keepdims=True)
     end_n = jnp.sum(damp_n * v_first * v_first, 0, keepdims=True)
-    pieces = dot(
-        turned,
-        right_of(
-            jnp.concatenate(
-                [
-                    damp_0 * dot(basis, right_of(cross)),
-                    damp_0 * v_first,
-                    damp_0 * v_last,
-                    damp_n * jnp.where(face < 0.5, v_first, v_last),
-                ],
-                1,
-            )
-        ),
-    )
-    spread, col_0, col_1, col_n = (pieces[:, LANES * x : LANES * (x + 1)] for x in range(4))
-    depth = lax.broadcasted_iota(jnp.int32, (edge, LANES), 0).astype(jnp.float32)
-    at_face = depth == face
-    y0 = y0 + jnp.where(at_face, spread[0:1], 0.0)
-    y1 = y1 + jnp.where(at_face, spread[edge - 1 : edge], 0.0)
+    damped = damp_0 * cross
+    pieces = dot(turned, right_of(jnp.concatenate([damped, damp_0 * v_first, damp_0 * v_last], 1)))
+    spread, col_0, col_1 = (pieces[:, LANES * x : LANES * (x + 1)] for x in range(3))
+    v_face = jnp.where(face < 0.5, v_first, v_last)
+    y0 = y0 + v_face * jnp.sum(v_first * damped, 0, keepdims=True)
+    y1 = y1 + v_face * jnp.sum(v_last * damped, 0, keepdims=True)
 
     inv_rate = 1.0 / rate_0
     open_face = place < edge - 1
@@ -650,20 +638,21 @@
     flux_up = right / diag
     flux_down = jnp.where(place > 0, before(flux_up), 0.0)
 
-    weight_down = jnp.sum(col_n * flux_down, 0, keepdims=True)
-    weight_up = jnp.sum(col_n * flux_up, 0, keepdims=True)
+    weight_down = jnp.sum(damp_n * v_face * flux_down, 0, keepdims=True)
+    weight_up = jnp.sum(damp_n * v_face * flux_up, 0, keepdims=True)
     ends = face_y + end_n * spread + col_0 * weight_down - col_1 * weight_up
     ends = jnp.where(normal_2 > 0.5, damp_t, 1.0) * ends
     jump = g / (1.0 + g * (end_n + partner(end_n))) * (ends - partner(ends))
     face_out = jnp.where(normal_2 > 0.5, damp_t * spread - jump, damp_t * (spread - jump))
-    lines = dot(basis, right_of(jnp.concatenate([flux_down, flux_up], 1)))
-    lines = dot(turned, right_of(jnp.concatenate([damp_n * damp_t] * 2, 1) * lines))
+    damp_nt = damp_n * damp_t
+    lines = dot(turned, right_of(jnp.concatenate([damp_nt * flux_down, damp_nt * flux_up], 1)))
     packed = jnp.concatenate(
         [lines[:, :LANES], lines[:, LANES:], face_out, jnp.zeros((edge, LANES), jnp.float32)], 0
     )
     reply = dot_lanes(jnp.concatenate([hit] * 3, 1), exact_of(packed))
-    for x in range(4):
-        out[pl.ds(x, edge, stride=4), :] = reply[edge * x : edge * (x + 1)]
+    kinds = swap_blocks([reply[edge * x : edge * (x + 1)] for x in range(4)])
+    for x in range(3):
+        out[pl.ds(x, edge, stride=3), :] = kinds[x]
 
 
 def update_kernel(
@@ -676,8 +665,7 @@
     size = tiles * edge
     swapped = flags[2, 0] < 0.5
     old = jnp.where(flags[2:3] < 0.5, 0.0, 1.0)
-    fields = [recv[pl.ds(x, edge, stride=2 * count), :] for x in range(2 * count)]
-    low, high, face_part, _ = swap_blocks(fields)
+    low, high, face_part = (recv[pl.ds(x, edge, stride=3), :] for x in range(3))
     high_s, low_s = parts_of(face_part)
     turn = jnp.concatenate([high_s, low_s, high_s, jnp.zeros_like(high_s)], 0).T.astype(jnp.bfloat16)
     face_wide = dot(turn, const[:, LANES:].astype(jnp.bfloat16))
@@ -732,10 +720,10 @@
     faces_of = np.zeros((edge, LANES))
     faces_of[:, (place % 4) * edge + place // 4] = basis
     pad = lambda x: np.pad(x, ((0, 0), (0, LANES - x.shape[1])))
-    message_const = np.concatenate([pad(host_left(ends_of)), host_left(faces_of)], 1)
+    message_const = np.concatenate([pad(host_left(ends_of)), host_left(faces_of), np.tile(basis.T, (1, 4))], 1)
     lanes_of = lambda x: np.tile(x[:, None], (1, LANES))
     owner_const = np.concatenate(
-        [pad(host_left(basis)), pad(host_left(basis.T))]
+        [pad(host_left(basis.T))]
         + [lanes_of(x) for x in (eigen, basis[:, 0], basis[:, -1])],
         1,
     )
@@ -753,7 +741,7 @@
     stay = lambda x: pltpu.with_memory_space_constraint(x, pltpu.HBM)
     msg, solved = pl.pallas_call(
         message_kernel,
-        out_shape=(jax.ShapeDtypeStruct((devices * 8, LANES), f32), tall),
+        out_shape=(jax.ShapeDtypeStruct((devices * ROWS, LANES), f32), tall),
         in_specs=[hbm] * 7,
         out_specs=(vmem, vmem),
         scratch_shapes=[
@@ -764,13 +752,12 @@
             pltpu.VMEM(fraction.shape, f32),
             pltpu.VMEM(inverses.shape, f32),
             pltpu.VMEM(message_const.shape, f32),
-            pltpu.VMEM((size, LANES), f32),
             pltpu.SemaphoreType.DMA((7,)),
         ],
         compiler_params=pltpu.CompilerParams(vmem_limit_bytes=48 * 2**20),
         name="message",
     )(*(stay(x) for x in (neighbors, rates.transpose(0, 2, 1), calcium, buffer, fraction, inverses, const(message_const))))
-    recv = lax.all_to_all(msg.reshape(devices, 8, LANES), "bricks", 0, 0, tiled=True)
+    recv = lax.all_to_all(msg.reshape(devices * ROWS, 1, LANES), "bricks", 0, 0, tiled=True).reshape(devices * ROWS, LANES)
     base, pick, flags, edges = pl.pallas_call(
         local_kernel,
         out_shape=(
@@ -796,13 +783,13 @@
     )(neighbors, solved, inverses)
     reply = pl.pallas_call(
         owner_kernel,
-        out_shape=jax.ShapeDtypeStruct((devices * 2 * count, LANES), f32),
+        out_shape=jax.ShapeDtypeStruct((devices * 3, LANES), f32),
         in_specs=[vmem] * 4,
         out_specs=vmem,
         compiler_params=params,
         name="chain_and_face_solves",
-    )(recv.reshape(devices * 8, LANES), pick, flags, const(owner_const))
-    back = lax.all_to_all(reply.reshape(devices, 2 * count, LANES), "bricks", 0, 0, tiled=True)
+    )(recv, pick, flags, const(owner_const))
+    back = lax.all_to_all(reply.reshape(devices * 3, 1, LANES), "bricks", 0, 0, tiled=True)
     return pl.pallas_call(
         update_kernel,
         out_shape=(field, field),
@@ -816,7 +803,7 @@
         ],
         compiler_params=params,
         name="rank_three_update",
-    )(back.reshape(devices * 2 * count, LANES), base, edges, flags, calcium, buffer, const(update_const))
+    )(back.reshape(devices * 3, LANES), base, edges, flags, calcium, buffer, const(update_const))
 
 
 def body(calcium, buffer, fraction, rates, inverses, neighbors, ranks):

time: 31.9 us -> 31.1 us (0.975)
  waiting for transfers between devices: 5.49 us -> 4.88 us
    all_to_all x1, waiting for transfers between devices: 5.49 us -> 4.88 us  [fast_body(): lax.all_to_all(msg.reshape(devices * ROWS, 1, LANES), 'bricks', 0, 0, til...]
  transfers between devices with their start and end apart: 1 -> 1, of which waited for: 1 -> 1; matrix products, arithmetic and copies ran while one was open for 0% -> 0% of each run, Pallas kernels for 8% -> 9%
where the time goes in v3:
time: 31.1 us; the launch traced here: 30.9 us
  blocking collectives  9.03 us (29%)
  Pallas kernels  8.96 us (29%)
  starting transfers between devices  7.3 us (23%)
  waiting for transfers between devices  4.88 us (16%)
  between operations  0.73 us (2%)
    all_to_all x1, blocking collectives, fast_body(): lax.all_to_all(reply.reshape(devices * 3, 1, LANES), 'bricks', 0, 0, tile...  9.03 us
    all_to_all x1, starting transfers between devices, fast_body(): lax.all_to_all(msg.reshape(devices * ROWS, 1, LANES), 'bricks', 0, 0, til...  7.3 us
    all_to_all x1, waiting for transfers between devices, fast_body(): lax.all_to_all(msg.reshape(devices * ROWS, 1, LANES), 'bricks', 0, 0, til...  4.88 us
    pallas_call x1, Pallas kernels, fast_body(): pl.pallas_call(message_kernel, out_shape=(jax.ShapeDtypeStruct((devices *...  3.64 us
    pallas_call x1, Pallas kernels, fast_body(): pl.pallas_call(local_kernel, out_shape=(tall, jax.ShapeDtypeStruct((LANES...  2.67 us
    pallas_call x1, Pallas kernels, fast_body(): pl.pallas_call(owner_kernel, out_shape=jax.ShapeDtypeStruct((devices * 3,...  1.33 us
    pallas_call x1, Pallas kernels, fast_body(): pl.pallas_call(update_kernel, out_shape=(field, field), in_specs=[vmem] *...  1.31 us
  transfers between devices with their start and end apart: 1, of which 1 were waited for; matrix products, arithmetic and copies ran while one was open for 0% of the time, Pallas kernels for 9%

profile of v3, /device:TPU:0, one launch (start us, length us, event | category | flops | bytes accessed | tf_op | source)
XLA Modules:
  0.0 30.9 jit_solution(1707900853729746568)
XLA Ops:
  0.6 0.0 copy-start.2
  0.6 0.0 copy-start.5
  0.7 3.6 %message.1 = (f32[160,128]{1,0:T(8,128)}, f32[1024,128]{1,0:T(8,128)S(1)}) custom-call(s32[3,2,64]{2,1,0:T(2,128)} %near_in.3, f32[2,2,3]{2,1,0:T(2,128)} %bitcast.12, f32[2,32,1024]{2,1,0:T(8,128)} %calcium.1, f32[2,32,1024]{2,1,0:T(8,128)} %buffer.1, f32[2,32,1024]{2,1,0:T(8,128)} %fraction_in.1, f32[2,3,2,32,32]{4,3,2,1,0:T(8,128)} %inverses_in.3, ...), custom_call_target="tpu_custom_call" | custom-call | tf_op jit(solution)/shard_map/message/pallas_call | solution.py:742
  4.3 0.0 copy-start.4
  4.3 0.0 copy-start.3
  4.3 7.3 %all-to-all-start = ((f32[160,1,128]{2,1,0:T(1,128)}), f32[160,1,128]{2,1,0:T(1,128)S(1)}, u32[]{:S(2)}, u32[]{:S(2)}) async-start(f32[160,1,128]{2,1,0:T(1,128)} %bitcast.2), calls=%async_computation | async-start | bytes 163840 | tf_op jit(solution)/shard_map/all_to_all | solution.py:760
  11.6 0.0 copy-done.2
  11.6 0.0 copy-done.5
  11.7 0.0 copy-start.1
  11.7 2.7 %local_solution.1 = (f32[1024,128]{1,0:T(8,128)S(1)}, f32[128,128]{1,0:T(8,128)S(1)}, f32[8,128]{1,0:T(8,128)S(1)}, f32[4,3,32,128]{3,2,1,0:T(8,128)S(1)}) custom-call(s32[3,2,64]{2,1,0:T(2,128)S(1)} %copy-done.5, f32[1024,128]{1,0:T(8,128)S(1)} %get-tuple-element.9.solved_in, f32[2,3,2,32,32]{4,3,2,1,0:T(8,128)S(1)} %copy-done.2), custom_call_target="tpu_custom_call" | custom-call | flops 20000000 | bytes 4000000 | tf_op jit(solution)/shard_map/local_solution/pallas_call | solution.py:761
  14.3 0.0 copy-start
  14.4 4.9 %all-to-all-done = f32[160,1,128]{2,1,0:T(1,128)S(1)} async-done(((f32[160,1,128]{2,1,0:T(1,128)}), f32[160,1,128]{2,1,0:T(1,128)S(1)}, u32[]{:S(2)}, u32[]{:S(2)}) %all-to-all-start) | async-done | bytes 81952 | tf_op jit(solution)/shard_map/all_to_all | solution.py:760
  19.2 0.0 copy-done.4
  19.2 1.3 %chain_and_face_solves.1 = f32[96,128]{1,0:T(8,128)S(1)} custom-call(f32[160,128]{1,0:T(8,128)S(1)} %bitcast.9, f32[128,128]{1,0:T(8,128)S(1)} %get-tuple-element.10.pick, f32[8,128]{1,0:T(8,128)S(1)} %get-tuple-element.11.flags, f32[32,512]{1,0:T(8,128)S(1)} %copy-done.4), custom_call_target="tpu_custom_call" | custom-call | tf_op jit(solution)/shard_map/chain_and_face_solves/pallas_call | solution.py:784
  20.6 9.0 %all_to_all.10 = f32[96,1,128]{2,1,0:T(1,128)S(1)} all-to-all(f32[96,1,128]{2,1,0:T(1,128)S(1)} %bitcast.10), channel_id=1, replica_groups=mesh['bricks'=32] {'bricks'}, dimensions={0} | all-to-all | bytes 98304 | tf_op jit(solution)/shard_map/all_to_all | solution.py:792
  29.6 0.0 copy-done.3
  29.6 0.0 copy-done.1
  29.6 0.0 copy-done
  29.6 1.3 %rank_three_update.1 = (f32[2,32,1024]{2,1,0:T(8,128)}, f32[2,32,1024]{2,1,0:T(8,128)}) custom-call(f32[96,128]{1,0:T(8,128)S(1)} %bitcast.11, f32[1024,128]{1,0:T(8,128)S(1)} %get-tuple-element.12.base, f32[4,3,32,128]{3,2,1,0:T(8,128)S(1)} %get-tuple-element.13.edges, f32[8,128]{1,0:T(8,128)S(1)} %get-tuple-element.11.flags, f32[2,32,1024]{2,1,0:T(8,128)S(1)} %copy-done, ...), custom_call_target="tpu_custom_call" | custom-call | tf_op jit(solution)/shard_map/rank_three_update/pallas_call | solution.py:793
Async XLA Ops:
  0.6 11.0 %copy-start.2 = (f32[2,3,2,32,32]{4,3,2,1,0:T(8,128)S(1)}, f32[2,3,2,32,32]{4,3,2,1,0:T(8,128)}, u32[]{:S(2)}) copy-start(f32[2,3,2,32,32]{4,3,2,1,0:T(8,128)} %inverses_in.3) | copy-start | bytes 147460
  0.6 11.0 %copy-start.5 = (s32[3,2,64]{2,1,0:T(2,128)S(1)}, s32[3,2,64]{2,1,0:T(2,128)}, u32[]{:S(2)}) copy-start(s32[3,2,64]{2,1,0:T(2,128)} %near_in.3) | copy-start | bytes 4612
  4.3 14.9 %copy-start.4 = (f32[32,512]{1,0:T(8,128)S(1)}, f32[32,512]{1,0:T(8,128)}, u32[]{:S(2)}) copy-start(f32[32,512]{1,0:T(8,128)} %constant.7.clone.const) | copy-start | bytes 196612
  4.3 25.3 %copy-start.3 = (f32[128,1152]{1,0:T(8,128)S(1)}, f32[128,1152]{1,0:T(8,128)}, u32[]{:S(2)}) copy-start(f32[128,1152]{1,0:T(8,128)} %constant.8.clone.const) | copy-start | bytes 1769476
  4.3 14.9 %all-to-all-start = ((f32[160,1,128]{2,1,0:T(1,128)}), f32[160,1,128]{2,1,0:T(1,128)S(1)}, u32[]{:S(2)}, u32[]{:S(2)}) async-start(f32[160,1,128]{2,1,0:T(1,128)} %bitcast.2), calls=%async_computation | async-start | bytes 163840 | tf_op jit(solution)/shard_map/all_to_all | solution.py:760
  11.7 18.0 %copy-start.1 = (f32[2,32,1024]{2,1,0:T(8,128)S(1)}, f32[2,32,1024]{2,1,0:T(8,128)}, u32[]{:S(2)}) copy-start(f32[2,32,1024]{2,1,0:T(8,128)} %buffer.1) | copy-start | bytes 786436
  14.3 15.3 %copy-start = (f32[2,32,1024]{2,1,0:T(8,128)S(1)}, f32[2,32,1024]{2,1,0:T(8,128)}, u32[]{:S(2)}) copy-start(f32[2,32,1024]{2,1,0:T(8,128)} %calcium.1) | copy-start | bytes 786436

commit v4 on v3

--- a/solution.py
+++ b/solution.py
@@ -305,6 +305,11 @@
     high = x.astype(jnp.bfloat16)
     low = (x - high.astype(jnp.float32)).astype(jnp.bfloat16)
     return jnp.concatenate([high, low, high], 0)
+
+
+def pair_of(x):
+    high = x.astype(jnp.bfloat16)
+    return jnp.concatenate([high, (x - high.astype(jnp.float32)).astype(jnp.bfloat16)], 1)
 
 
 def exact_of(x):
@@ -475,12 +480,9 @@
 
     stack = jnp.concatenate(swap_blocks(ends0) + swap_blocks(ends1), 0)
     ends_of = const[:, : 3 * edge].astype(jnp.bfloat16)
-    faces_of = const[:, LANES : 4 * LANES].astype(jnp.bfloat16)
-    turn = right_of_swapped(jnp.where(on_block, jnp.concatenate([const[:, 4 * LANES :]] * 4, 0), 0.0))
-    stack = dot(right_of(stack, 1), turn)
+    faces_of = const[:, LANES:].astype(jnp.bfloat16)
     both = dot(ends_of, right_of(jnp.concatenate([stack[:edge], stack[edge:]], 1)))
     part_u = dot_lanes(faces_of, right_of(jnp.concatenate(faces_u, 0), 1))
-    part_u = dot(right_of(part_u, 1), turn)
     part_y = dot_lanes(faces_of, right_of(jnp.concatenate(faces_y, 0), 1))
     fields = swap_blocks([both[:, :LANES], both[:, LANES:], part_u, part_y])
     for x, part in enumerate(fields):
@@ -580,13 +582,14 @@
     lam = const[:, LANES : 2 * LANES]
     v_first = const[:, 2 * LANES : 3 * LANES]
     v_last = const[:, 3 * LANES : 4 * LANES]
+    basis = const[:, 4 * LANES : 4 * LANES + 3 * edge].astype(jnp.bfloat16)
     face, touch, normal_2, my_lam = flags[0:1], flags[1:2], flags[2:3], flags[3:4]
 
     hit = pick[...].astype(jnp.bfloat16)
     data = jnp.concatenate([recv[pl.ds(x, edge, stride=ROWS), :] for x in range(4)], 0).T
     tail = recv[pl.ds(4, edge, stride=ROWS), :]
     tail = jnp.concatenate([tail] + [pltpu.roll(tail, LANES - edge * x, 1) for x in range(1, 4)], 0).T[:16]
-    parts = dot(exact_of(jnp.concatenate([tail, data], 0)), jnp.concatenate([hit] * 3, 0))
+    parts = dot(pair_of(jnp.concatenate([tail, data], 0)), jnp.concatenate([hit] * 2, 0))
     rate_0, rate_t, rate_n = parts[0:1], parts[1:2], parts[2:3]
     y0, y1, face_u, face_y = (parts[16 + edge * x : 16 + edge * (x + 1)] for x in range(4))
 
@@ -612,19 +615,21 @@
     near_c = jnp.sum(damp_0 * v_first * v_first, 0, keepdims=True)
     far_c = jnp.sum(damp_0 * v_first * v_last, 0, keepdims=True)
     end_n = jnp.sum(damp_n * v_first * v_first, 0, keepdims=True)
-    damped = damp_0 * cross
+    open_face = place < edge - 1
+    right = jnp.where(open_face, y1 - after(y0), 0.0)
+    both = dot(basis, right_of(jnp.concatenate([cross, right], 1)))
+    damped = damp_0 * both[:, :LANES]
     pieces = dot(turned, right_of(jnp.concatenate([damped, damp_0 * v_first, damp_0 * v_last], 1)))
     spread, col_0, col_1 = (pieces[:, LANES * x : LANES * (x + 1)] for x in range(3))
     v_face = jnp.where(face < 0.5, v_first, v_last)
-    y0 = y0 + v_face * jnp.sum(v_first * damped, 0, keepdims=True)
-    y1 = y1 + v_face * jnp.sum(v_last * damped, 0, keepdims=True)
+    at_first = v_face * jnp.sum(v_first * damped, 0, keepdims=True)
+    at_last = v_face * jnp.sum(v_last * damped, 0, keepdims=True)
+    right = both[:, LANES:] + jnp.where(open_face, at_last - after(at_first), 0.0)
 
     inv_rate = 1.0 / rate_0
-    open_face = place < edge - 1
     diag = jnp.where(open_face, 0.5 * (inv_rate + after(inv_rate)) + near_c + after(near_c), 1.0)
     lower = jnp.where(open_face & (place > 0), -far_c, 0.0)
     upper = jnp.where(place < edge - 2, -after(far_c), 0.0)
-    right = jnp.where(open_face, y1 - after(y0), 0.0)
     step = 1
     while step < edge:
         inverse = 1.0 / diag
@@ -649,7 +654,7 @@
     packed = jnp.concatenate(
         [lines[:, :LANES], lines[:, LANES:], face_out, jnp.zeros((edge, LANES), jnp.float32)], 0
     )
-    reply = dot_lanes(jnp.concatenate([hit] * 3, 1), exact_of(packed))
+    reply = dot_lanes(jnp.concatenate([hit] * 2, 1), pair_of(packed))
     kinds = swap_blocks([reply[edge * x : edge * (x + 1)] for x in range(4)])
     for x in range(3):
         out[pl.ds(x, edge, stride=3), :] = kinds[x]
@@ -720,11 +725,12 @@
     faces_of = np.zeros((edge, LANES))
     faces_of[:, (place % 4) * edge + place // 4] = basis
     pad = lambda x: np.pad(x, ((0, 0), (0, LANES - x.shape[1])))
-    message_const = np.concatenate([pad(host_left(ends_of)), host_left(faces_of), np.tile(basis.T, (1, 4))], 1)
+    message_const = np.concatenate([pad(host_left(ends_of)), host_left(faces_of)], 1)
     lanes_of = lambda x: np.tile(x[:, None], (1, LANES))
     owner_const = np.concatenate(
         [pad(host_left(basis.T))]
-        + [lanes_of(x) for x in (eigen, basis[:, 0], basis[:, -1])],
+        + [lanes_of(x) for x in (eigen, basis[:, 0], basis[:, -1])]
+        + [pad(host_left(basis))],
         1,
     )
     expand = np.pad(host_right(np.repeat(basis, edge, 1)), ((0, LANES - 3 * edge), (0, 0)))

time: 31.1 us -> 31 us (level)
  no operation moved by 1% of the time
where the time goes in v4:
time: 31 us; the launch traced here: 30.8 us
  blocking collectives  9.03 us (29%)
  Pallas kernels  8.82 us (28%)
  starting transfers between devices  7.3 us (24%)
  waiting for transfers between devices  4.86 us (16%)
  between operations  0.73 us (2%)
    all_to_all x1, blocking collectives, fast_body(): lax.all_to_all(reply.reshape(devices * 3, 1, LANES), 'bricks', 0, 0, tile...  9.03 us
    all_to_all x1, starting transfers between devices, fast_body(): lax.all_to_all(msg.reshape(devices * ROWS, 1, LANES), 'bricks', 0, 0, til...  7.3 us
    all_to_all x1, waiting for transfers between devices, fast_body(): lax.all_to_all(msg.reshape(devices * ROWS, 1, LANES), 'bricks', 0, 0, til...  4.86 us
    pallas_call x1, Pallas kernels, fast_body(): pl.pallas_call(message_kernel, out_shape=(jax.ShapeDtypeStruct((devices *...  3.39 us
    pallas_call x1, Pallas kernels, fast_body(): pl.pallas_call(local_kernel, out_shape=(tall, jax.ShapeDtypeStruct((LANES...  2.67 us
    pallas_call x1, Pallas kernels, fast_body(): pl.pallas_call(owner_kernel, out_shape=jax.ShapeDtypeStruct((devices * 3,...  1.44 us
    pallas_call x1, Pallas kernels, fast_body(): pl.pallas_call(update_kernel, out_shape=(field, field), in_specs=[vmem] *...  1.32 us
  transfers between devices with their start and end apart: 1, of which 1 were waited for; matrix products, arithmetic and copies ran while one was open for 0% of the time, Pallas kernels for 9%

profile of v4, /device:TPU:0, one launch (start us, length us, event | category | flops | bytes accessed | tf_op | source)
XLA Modules:
  0.0 30.8 jit_solution(8370495986410943141)
XLA Ops:
  0.6 0.0 copy-start.2
  0.6 3.4 %message.1 = (f32[160,128]{1,0:T(8,128)}, f32[1024,128]{1,0:T(8,128)S(1)}) custom-call(s32[3,2,64]{2,1,0:T(2,128)} %near_in.3, f32[2,2,3]{2,1,0:T(2,128)} %bitcast.12, f32[2,32,1024]{2,1,0:T(8,128)} %calcium.1, f32[2,32,1024]{2,1,0:T(8,128)} %buffer.1, f32[2,32,1024]{2,1,0:T(8,128)} %fraction_in.1, f32[2,3,2,32,32]{4,3,2,1,0:T(8,128)} %inverses_in.3, ...), custom_call_target="tpu_custom_call" | custom-call | tf_op jit(solution)/shard_map/message/pallas_call | solution.py:748
  4.0 0.0 copy-start.5
  4.1 0.0 copy-start.4
  4.1 7.3 %all-to-all-start = ((f32[160,1,128]{2,1,0:T(1,128)}), f32[160,1,128]{2,1,0:T(1,128)S(1)}, u32[]{:S(2)}, u32[]{:S(2)}) async-start(f32[160,1,128]{2,1,0:T(1,128)} %bitcast.2), calls=%async_computation | async-start | bytes 163840 | tf_op jit(solution)/shard_map/all_to_all | solution.py:766
  11.4 0.0 copy-start.3
  11.4 0.0 copy-done.2
  11.4 0.0 copy-done.5
  11.4 0.0 copy-start.1
  11.4 2.7 %local_solution.1 = (f32[1024,128]{1,0:T(8,128)S(1)}, f32[128,128]{1,0:T(8,128)S(1)}, f32[8,128]{1,0:T(8,128)S(1)}, f32[4,3,32,128]{3,2,1,0:T(8,128)S(1)}) custom-call(s32[3,2,64]{2,1,0:T(2,128)S(1)} %copy-done.5, f32[1024,128]{1,0:T(8,128)S(1)} %get-tuple-element.9.solved_in, f32[2,3,2,32,32]{4,3,2,1,0:T(8,128)S(1)} %copy-done.2), custom_call_target="tpu_custom_call" | custom-call | flops 20000000 | bytes 4000000 | tf_op jit(solution)/shard_map/local_solution/pallas_call | solution.py:767
  14.1 0.0 copy-start
  14.1 4.9 %all-to-all-done = f32[160,1,128]{2,1,0:T(1,128)S(1)} async-done(((f32[160,1,128]{2,1,0:T(1,128)}), f32[160,1,128]{2,1,0:T(1,128)S(1)}, u32[]{:S(2)}, u32[]{:S(2)}) %all-to-all-start) | async-done | bytes 81952 | tf_op jit(solution)/shard_map/all_to_all | solution.py:766
  19.0 0.0 copy-done.4
  19.0 1.4 %chain_and_face_solves.1 = f32[96,128]{1,0:T(8,128)S(1)} custom-call(f32[160,128]{1,0:T(8,128)S(1)} %bitcast.9, f32[128,128]{1,0:T(8,128)S(1)} %get-tuple-element.10.pick, f32[8,128]{1,0:T(8,128)S(1)} %get-tuple-element.11.flags, f32[32,640]{1,0:T(8,128)S(1)} %copy-done.4), custom_call_target="tpu_custom_call" | custom-call | tf_op jit(solution)/shard_map/chain_and_face_solves/pallas_call | solution.py:790
  20.4 9.0 %all_to_all.10 = f32[96,1,128]{2,1,0:T(1,128)S(1)} all-to-all(f32[96,1,128]{2,1,0:T(1,128)S(1)} %bitcast.10), channel_id=1, replica_groups=mesh['bricks'=32] {'bricks'}, dimensions={0} | all-to-all | bytes 98304 | tf_op jit(solution)/shard_map/all_to_all | solution.py:798
  29.5 0.0 copy-done.3
  29.5 0.0 copy-done.1
  29.5 0.0 copy-done
  29.5 1.3 %rank_three_update.1 = (f32[2,32,1024]{2,1,0:T(8,128)}, f32[2,32,1024]{2,1,0:T(8,128)}) custom-call(f32[96,128]{1,0:T(8,128)S(1)} %bitcast.11, f32[1024,128]{1,0:T(8,128)S(1)} %get-tuple-element.12.base, f32[4,3,32,128]{3,2,1,0:T(8,128)S(1)} %get-tuple-element.13.edges, f32[8,128]{1,0:T(8,128)S(1)} %get-tuple-element.11.flags, f32[2,32,1024]{2,1,0:T(8,128)S(1)} %copy-done, ...), custom_call_target="tpu_custom_call" | custom-call | tf_op jit(solution)/shard_map/rank_three_update/pallas_call | solution.py:799
Async XLA Ops:
  0.6 10.8 %copy-start.2 = (f32[2,3,2,32,32]{4,3,2,1,0:T(8,128)S(1)}, f32[2,3,2,32,32]{4,3,2,1,0:T(8,128)}, u32[]{:S(2)}) copy-start(f32[2,3,2,32,32]{4,3,2,1,0:T(8,128)} %inverses_in.3) | copy-start | bytes 147460
  4.0 7.4 %copy-start.5 = (s32[3,2,64]{2,1,0:T(2,128)S(1)}, s32[3,2,64]{2,1,0:T(2,128)}, u32[]{:S(2)}) copy-start(s32[3,2,64]{2,1,0:T(2,128)} %near_in.3) | copy-start | bytes 4612
  4.1 14.9 %copy-start.4 = (f32[32,640]{1,0:T(8,128)S(1)}, f32[32,640]{1,0:T(8,128)}, u32[]{:S(2)}) copy-start(f32[32,640]{1,0:T(8,128)} %constant.7.clone.const) | copy-start | bytes 245764
  4.1 14.9 %all-to-all-start = ((f32[160,1,128]{2,1,0:T(1,128)}), f32[160,1,128]{2,1,0:T(1,128)S(1)}, u32[]{:S(2)}, u32[]{:S(2)}) async-start(f32[160,1,128]{2,1,0:T(1,128)} %bitcast.2), calls=%async_computation | async-start | bytes 163840 | tf_op jit(solution)/shard_map/all_to_all | solution.py:766
  11.4 18.1 %copy-start.3 = (f32[128,1152]{1,0:T(8,128)S(1)}, f32[128,1152]{1,0:T(8,128)}, u32[]{:S(2)}) copy-start(f32[128,1152]{1,0:T(8,128)} %constant.8.clone.const) | copy-start | bytes 1769476
  11.4 18.0 %copy-start.1 = (f32[2,32,1024]{2,1,0:T(8,128)S(1)}, f32[2,32,1024]{2,1,0:T(8,128)}, u32[]{:S(2)}) copy-start(f32[2,32,1024]{2,1,0:T(8,128)} %buffer.1) | copy-start | bytes 786436
  14.1 15.4 %copy-start = (f32[2,32,1024]{2,1,0:T(8,128)S(1)}, f32[2,32,1024]{2,1,0:T(8,128)}, u32[]{:S(2)}) copy-start(f32[2,32,1024]{2,1,0:T(8,128)} %calcium.1) | copy-start | bytes 786436

commit v5 on v4

--- a/solution.py
+++ b/solution.py
@@ -286,37 +286,28 @@
 
 
 def parts_of(x):
-    high = x.astype(jnp.bfloat16).astype(jnp.float32)
-    return high, (x - high).astype(jnp.bfloat16).astype(jnp.float32)
-
-
-def left_of(x):
-    high, low = parts_of(x)
-    return jnp.concatenate([high, low, high], 1).astype(jnp.bfloat16)
-
-
-def right_of(x, axis=0):
-    high = x.astype(jnp.bfloat16)
-    low = (x - high.astype(jnp.float32)).astype(jnp.bfloat16)
-    return jnp.concatenate([high, high, low], axis)
-
-
-def right_of_swapped(x):
-    high = x.astype(jnp.bfloat16)
-    low = (x - high.astype(jnp.float32)).astype(jnp.bfloat16)
-    return jnp.concatenate([high, low, high], 0)
-
-
-def pair_of(x):
-    high = x.astype(jnp.bfloat16)
-    return jnp.concatenate([high, (x - high.astype(jnp.float32)).astype(jnp.bfloat16)], 1)
-
-
-def exact_of(x):
     high = x.astype(jnp.bfloat16)
     rest = x - high.astype(jnp.float32)
     middle = rest.astype(jnp.bfloat16)
-    return jnp.concatenate([high, middle, (rest - middle.astype(jnp.float32)).astype(jnp.bfloat16)], 1)
+    return high, middle, (rest - middle.astype(jnp.float32)).astype(jnp.bfloat16)
+
+
+LEFT = (0, 0, 0, 1, 1, 2)
+RIGHT = (0, 1, 2, 0, 1, 0)
+
+
+def left_of(x):
+    parts = [part.astype(jnp.float32) for part in parts_of(x)]
+    return jnp.concatenate([parts[p] for p in LEFT], 1).astype(jnp.bfloat16)
+
+
+def right_of(x, axis=0):
+    parts = parts_of(x)
+    return jnp.concatenate([parts[p] for p in RIGHT], axis)
+
+
+def exact_of(x):
+    return jnp.concatenate(parts_of(x), 1)
 
 
 def dot(a, b):
@@ -327,16 +318,22 @@
     return lax.dot_general(a, b, (((1,), (1,)), ((), ())), preferred_element_type=jnp.float32)
 
 
+def host_parts(x):
+    parts = []
+    for _ in range(3):
+        parts.append(x.astype(jnp.bfloat16).astype(np.float64))
+        x = x - parts[-1]
+    return parts
+
+
 def host_left(x):
-    high = x.astype(jnp.bfloat16).astype(np.float64)
-    low = (x - high).astype(jnp.bfloat16).astype(np.float64)
-    return np.concatenate([high, low, high], 1)
+    parts = host_parts(x)
+    return np.concatenate([parts[p] for p in LEFT], 1)
 
 
 def host_right(x):
-    high = x.astype(jnp.bfloat16).astype(np.float64)
-    low = (x - high).astype(jnp.bfloat16).astype(np.float64)
-    return np.concatenate([high, high, low], 0)
+    parts = host_parts(x)
+    return np.concatenate([parts[p] for p in RIGHT], 0)
 
 
 def lane_of(shape):
@@ -443,7 +440,7 @@
         bound = [buffer[b, :, LANES * c : LANES * (c + 1)] for c in range(tiles)]
         alpha = [fraction[b, :, LANES * c : LANES * (c + 1)] for c in range(tiles)]
         bind = [KON * x * (BTOT - y) - KOFF * y for x, y in zip(calc, bound)]
-        source_calc = [-w + INFLUX * (1.0 - a) / a for w, a in zip(bind, alpha)]
+        source_calc = [INFLUX / a - (w + INFLUX) for w, a in zip(bind, alpha)]
         for q, (u, source) in enumerate(((calc, source_calc), (bound, bind))):
             at = size * (2 * b + q)
             rate_t, rate_n = 2.0 * rates[b, q, closed], 2.0 * rates[b, q, normal]
@@ -463,11 +460,12 @@
             ends0.append(jnp.concatenate([g[0:1, LANES * c : LANES * (c + 1)] for c in range(tiles)], 0))
             ends1.append(jnp.concatenate([g[edge - 1 : edge, LANES * c : LANES * (c + 1)] for c in range(tiles)], 0))
             w = jnp.concatenate([g[:, LANES * c : LANES * (c + 1)] - 2.0 * u[c] for c in range(tiles)], 0)
-            block = jnp.concatenate([inverses[b, normal, q]] * 4, 1)
-            block = jnp.where(on_block, jnp.concatenate([block] * 4, 0), 0.0)
-            high = w.astype(jnp.bfloat16)
-            low = (w - high.astype(jnp.float32)).astype(jnp.bfloat16)
-            y = dot(jnp.concatenate([high, high, low], 1), right_of_swapped(block))
+            sides = [
+                jnp.where(on_block, jnp.concatenate([jnp.concatenate([x.astype(jnp.float32)] * 4, 1)] * 4, 0), 0.0)
+                for x in parts_of(inverses[b, normal, q])
+            ]
+            sides = [x.astype(jnp.bfloat16) for x in sides]
+            y = dot(right_of(w, 1), jnp.concatenate([sides[p] for p in LEFT], 0))
             solved[pl.ds(at, size), :] = y
             face_u = jnp.zeros((edge, LANES), jnp.float32)
             face_y = jnp.zeros((edge, LANES), jnp.float32)
@@ -479,8 +477,8 @@
             faces_y.append(face_y)
 
     stack = jnp.concatenate(swap_blocks(ends0) + swap_blocks(ends1), 0)
-    ends_of = const[:, : 3 * edge].astype(jnp.bfloat16)
-    faces_of = const[:, LANES:].astype(jnp.bfloat16)
+    ends_of = const[:, : 6 * edge]
+    faces_of = const[:, 2 * LANES :]
     both = dot(ends_of, right_of(jnp.concatenate([stack[:edge], stack[edge:]], 1)))
     part_u = dot_lanes(faces_of, right_of(jnp.concatenate(faces_u, 0), 1))
     part_y = dot_lanes(faces_of, right_of(jnp.concatenate(faces_y, 0), 1))
@@ -578,18 +576,16 @@
 
 def owner_kernel(recv, pick, flags, const, out):
     edge = const.shape[0]
-    turned = const[:, : 3 * edge].astype(jnp.bfloat16)
-    lam = const[:, LANES : 2 * LANES]
-    v_first = const[:, 2 * LANES : 3 * LANES]
-    v_last = const[:, 3 * LANES : 4 * LANES]
-    basis = const[:, 4 * LANES : 4 * LANES + 3 * edge].astype(jnp.bfloat16)
+    turned = const[:, : 6 * edge].astype(jnp.bfloat16)
+    basis = const[:, 2 * LANES : 2 * LANES + 6 * edge].astype(jnp.bfloat16)
+    lam, v_first, v_last = (const[:, LANES * x : LANES * (x + 1)] for x in (4, 5, 6))
     face, touch, normal_2, my_lam = flags[0:1], flags[1:2], flags[2:3], flags[3:4]
 
     hit = pick[...].astype(jnp.bfloat16)
     data = jnp.concatenate([recv[pl.ds(x, edge, stride=ROWS), :] for x in range(4)], 0).T
     tail = recv[pl.ds(4, edge, stride=ROWS), :]
     tail = jnp.concatenate([tail] + [pltpu.roll(tail, LANES - edge * x, 1) for x in range(1, 4)], 0).T[:16]
-    parts = dot(pair_of(jnp.concatenate([tail, data], 0)), jnp.concatenate([hit] * 2, 0))
+    parts = dot(exact_of(jnp.concatenate([tail, data], 0)), jnp.concatenate([hit] * 3, 0))
     rate_0, rate_t, rate_n = parts[0:1], parts[1:2], parts[2:3]
     y0, y1, face_u, face_y = (parts[16 + edge * x : 16 + edge * (x + 1)] for x in range(4))
 
@@ -654,7 +650,7 @@
     packed = jnp.concatenate(
         [lines[:, :LANES], lines[:, LANES:], face_out, jnp.zeros((edge, LANES), jnp.float32)], 0
     )
-    reply = dot_lanes(jnp.concatenate([hit] * 2, 1), pair_of(packed))
+    reply = dot_lanes(jnp.concatenate([hit] * 3, 1), exact_of(packed))
     kinds = swap_blocks([reply[edge * x : edge * (x + 1)] for x in range(4)])
     for x in range(3):
         out[pl.ds(x, edge, stride=3), :] = kinds[x]
@@ -671,10 +667,11 @@
     swapped = flags[2, 0] < 0.5
     old = jnp.where(flags[2:3] < 0.5, 0.0, 1.0)
     low, high, face_part = (recv[pl.ds(x, edge, stride=3), :] for x in range(3))
-    high_s, low_s = parts_of(face_part)
-    turn = jnp.concatenate([high_s, low_s, high_s, jnp.zeros_like(high_s)], 0).T.astype(jnp.bfloat16)
-    face_wide = dot(turn, const[:, LANES:].astype(jnp.bfloat16))
-    lines = dot(const[:edge, : 3 * edge].astype(jnp.bfloat16), right_of(jnp.concatenate([low, high], 1)))
+    parts = [part.astype(jnp.float32) for part in parts_of(face_part)]
+    turn = jnp.concatenate([parts[p] for p in LEFT] + [jnp.zeros_like(parts[0])] * 2, 0)
+    turn = turn.T[:, : 6 * edge].astype(jnp.bfloat16)
+    face_wide = dot(turn, const[:, 2 * LANES :])
+    lines = dot(const[:edge, : 6 * edge], right_of(jnp.concatenate([low, high], 1)))
     rows = []
     for e in range(2):
         work[pl.ds(edge * e, edge), :] = lines[:, LANES * e : LANES * (e + 1)]
@@ -724,17 +721,16 @@
     ends_of[:, (place % 4) * tiles + place // 4] = basis
     faces_of = np.zeros((edge, LANES))
     faces_of[:, (place % 4) * edge + place // 4] = basis
-    pad = lambda x: np.pad(x, ((0, 0), (0, LANES - x.shape[1])))
+    pad = lambda x: np.pad(x, ((0, 0), (0, 2 * LANES - x.shape[1])))
     message_const = np.concatenate([pad(host_left(ends_of)), host_left(faces_of)], 1)
     lanes_of = lambda x: np.tile(x[:, None], (1, LANES))
     owner_const = np.concatenate(
-        [pad(host_left(basis.T))]
-        + [lanes_of(x) for x in (eigen, basis[:, 0], basis[:, -1])]
-        + [pad(host_left(basis))],
+        [pad(host_left(basis.T)), pad(host_left(basis))]
+        + [lanes_of(x) for x in (eigen, basis[:, 0], basis[:, -1])],
         1,
     )
-    expand = np.pad(host_right(np.repeat(basis, edge, 1)), ((0, LANES - 3 * edge), (0, 0)))
-    back_const = np.pad(pad(host_left(basis.T)), ((0, LANES - edge), (0, 0)))
+    expand = host_right(np.repeat(basis, edge, 1))
+    back_const = np.pad(pad(host_left(basis.T)), ((0, 5 * edge), (0, 0)))
     update_const = np.concatenate([back_const, expand], 1)
     smem = pl.BlockSpec(memory_space=pltpu.SMEM)
     vmem = pl.BlockSpec(memory_space=pltpu.VMEM)
@@ -757,12 +753,12 @@
             pltpu.VMEM(calcium.shape, f32),
             pltpu.VMEM(fraction.shape, f32),
             pltpu.VMEM(inverses.shape, f32),
-            pltpu.VMEM(message_const.shape, f32),
+            pltpu.VMEM(message_const.shape, jnp.bfloat16),
             pltpu.SemaphoreType.DMA((7,)),
         ],
         compiler_params=pltpu.CompilerParams(vmem_limit_bytes=48 * 2**20),
         name="message",
-    )(*(stay(x) for x in (neighbors, rates.transpose(0, 2, 1), calcium, buffer, fraction, inverses, const(message_const))))
+    )(*(stay(x) for x in (neighbors, rates.transpose(0, 2, 1), calcium, buffer, fraction, inverses, jnp.asarray(message_const, jnp.bfloat16))))
     recv = lax.all_to_all(msg.reshape(devices * ROWS, 1, LANES), "bricks", 0, 0, tiled=True).reshape(devices * ROWS, LANES)
     base, pick, flags, edges = pl.pallas_call(
         local_kernel,
@@ -809,7 +805,7 @@
         ],
         compiler_params=params,
         name="rank_three_update",
-    )(back.reshape(devices * 3, LANES), base, edges, flags, calcium, buffer, const(update_const))
+    )(back.reshape(devices * 3, LANES), base, edges, flags, calcium, buffer, jnp.asarray(update_const, jnp.bfloat16))
 
 
 def body(calcium, buffer, fraction, rates, inverses, neighbors, ranks):

time: 31 us -> 31.3 us (level)
  Pallas kernels: 8.82 us -> 9.18 us
where the time goes in v5:
time: 31.3 us; the launch traced here: 31.1 us
  Pallas kernels  9.18 us (29%)
  blocking collectives  9.03 us (29%)
  starting transfers between devices  7.3 us (23%)
  waiting for transfers between devices  4.79 us (15%)
  between operations  0.73 us (2%)
    all_to_all x1, blocking collectives, fast_body(): lax.all_to_all(reply.reshape(devices * 3, 1, LANES), 'bricks', 0, 0, tile...  9.03 us
    all_to_all x1, starting transfers between devices, fast_body(): lax.all_to_all(msg.reshape(devices * ROWS, 1, LANES), 'bricks', 0, 0, til...  7.3 us
    all_to_all x1, waiting for transfers between devices, fast_body(): lax.all_to_all(msg.reshape(devices * ROWS, 1, LANES), 'bricks', 0, 0, til...  4.79 us
    pallas_call x1, Pallas kernels, fast_body(): pl.pallas_call(message_kernel, out_shape=(jax.ShapeDtypeStruct((devices *...  3.64 us
    pallas_call x1, Pallas kernels, fast_body(): pl.pallas_call(local_kernel, out_shape=(tall, jax.ShapeDtypeStruct((LANES...  2.75 us
    pallas_call x1, Pallas kernels, fast_body(): pl.pallas_call(owner_kernel, out_shape=jax.ShapeDtypeStruct((devices * 3,...  1.48 us
    pallas_call x1, Pallas kernels, fast_body(): pl.pallas_call(update_kernel, out_shape=(field, field), in_specs=[vmem] *...  1.31 us
  transfers between devices with their start and end apart: 1, of which 1 were waited for; matrix products, arithmetic and copies ran while one was open for 0% of the time, Pallas kernels for 9%

profile of v5, /device:TPU:0, one launch (start us, length us, event | category | flops | bytes accessed | tf_op | source)
XLA Modules:
  0.0 31.1 jit_solution(16954391431638760242)
XLA Ops:
  0.6 0.0 copy-start.2
  0.6 3.6 %message.1 = (f32[160,128]{1,0:T(8,128)}, f32[1024,128]{1,0:T(8,128)S(1)}) custom-call(s32[3,2,64]{2,1,0:T(2,128)} %near_in.3, f32[2,2,3]{2,1,0:T(2,128)} %bitcast.12, f32[2,32,1024]{2,1,0:T(8,128)} %calcium.1, f32[2,32,1024]{2,1,0:T(8,128)} %buffer.1, f32[2,32,1024]{2,1,0:T(8,128)} %fraction_in.1, f32[2,3,2,32,32]{4,3,2,1,0:T(8,128)} %inverses_in.3, ...), custom_call_target="tpu_custom_call" | custom-call | tf_op jit(solution)/shard_map/message/pallas_call | solution.py:744
  4.3 0.0 copy-start.5
  4.3 0.0 copy-start.4
  4.3 7.3 %all-to-all-start = ((f32[160,1,128]{2,1,0:T(1,128)}), f32[160,1,128]{2,1,0:T(1,128)S(1)}, u32[]{:S(2)}, u32[]{:S(2)}) async-start(f32[160,1,128]{2,1,0:T(1,128)} %bitcast.2), calls=%async_computation | async-start | bytes 163840 | tf_op jit(solution)/shard_map/all_to_all | solution.py:762
  11.6 0.0 copy-done.2
  11.6 0.0 copy-done.5
  11.6 0.0 copy-start.1
  11.7 0.0 copy-start.3
  11.7 2.7 %local_solution.1 = (f32[1024,128]{1,0:T(8,128)S(1)}, f32[128,128]{1,0:T(8,128)S(1)}, f32[8,128]{1,0:T(8,128)S(1)}, f32[4,3,32,128]{3,2,1,0:T(8,128)S(1)}) custom-call(s32[3,2,64]{2,1,0:T(2,128)S(1)} %copy-done.5, f32[1024,128]{1,0:T(8,128)S(1)} %get-tuple-element.9.solved_in, f32[2,3,2,32,32]{4,3,2,1,0:T(8,128)S(1)} %copy-done.2), custom_call_target="tpu_custom_call" | custom-call | flops 20000000 | bytes 4000000 | tf_op jit(solution)/shard_map/local_solution/pallas_call | solution.py:763
  14.4 0.0 copy-start
  14.4 4.8 %all-to-all-done = f32[160,1,128]{2,1,0:T(1,128)S(1)} async-done(((f32[160,1,128]{2,1,0:T(1,128)}), f32[160,1,128]{2,1,0:T(1,128)S(1)}, u32[]{:S(2)}, u32[]{:S(2)}) %all-to-all-start) | async-done | bytes 81952 | tf_op jit(solution)/shard_map/all_to_all | solution.py:762
  19.2 0.0 copy-done.4
  19.2 1.5 %chain_and_face_solves.1 = f32[96,128]{1,0:T(8,128)S(1)} custom-call(f32[160,128]{1,0:T(8,128)S(1)} %bitcast.9, f32[128,128]{1,0:T(8,128)S(1)} %get-tuple-element.10.pick, f32[8,128]{1,0:T(8,128)S(1)} %get-tuple-element.11.flags, f32[32,896]{1,0:T(8,128)S(1)} %copy-done.4), custom_call_target="tpu_custom_call" | custom-call | tf_op jit(solution)/shard_map/chain_and_face_solves/pallas_call | solution.py:786
  20.7 9.0 %all_to_all.10 = f32[96,1,128]{2,1,0:T(1,128)S(1)} all-to-all(f32[96,1,128]{2,1,0:T(1,128)S(1)} %bitcast.11), channel_id=1, replica_groups=mesh['bricks'=32] {'bricks'}, dimensions={0} | all-to-all | bytes 98304 | tf_op jit(solution)/shard_map/all_to_all | solution.py:794
  29.7 0.0 copy-done.1
  29.7 0.0 copy-done.3
  29.7 0.0 copy-done
  29.8 1.3 %rank_three_update.1 = (f32[2,32,1024]{2,1,0:T(8,128)}, f32[2,32,1024]{2,1,0:T(8,128)}) custom-call(f32[96,128]{1,0:T(8,128)S(1)} %bitcast.10, f32[1024,128]{1,0:T(8,128)S(1)} %get-tuple-element.12.base, f32[4,3,32,128]{3,2,1,0:T(8,128)S(1)} %get-tuple-element.13.edges, f32[8,128]{1,0:T(8,128)S(1)} %get-tuple-element.11.flags, f32[2,32,1024]{2,1,0:T(8,128)S(1)} %copy-done, ...), custom_call_target="tpu_custom_call" | custom-call | tf_op jit(solution)/shard_map/rank_three_update/pallas_call | solution.py:795
Async XLA Ops:
  0.6 11.0 %copy-start.2 = (f32[2,3,2,32,32]{4,3,2,1,0:T(8,128)S(1)}, f32[2,3,2,32,32]{4,3,2,1,0:T(8,128)}, u32[]{:S(2)}) copy-start(f32[2,3,2,32,32]{4,3,2,1,0:T(8,128)} %inverses_in.3) | copy-start | bytes 147460
  4.3 7.3 %copy-start.5 = (s32[3,2,64]{2,1,0:T(2,128)S(1)}, s32[3,2,64]{2,1,0:T(2,128)}, u32[]{:S(2)}) copy-start(s32[3,2,64]{2,1,0:T(2,128)} %near_in.3) | copy-start | bytes 4612
  4.3 14.9 %copy-start.4 = (f32[32,896]{1,0:T(8,128)S(1)}, f32[32,896]{1,0:T(8,128)}, u32[]{:S(2)}) copy-start(f32[32,896]{1,0:T(8,128)} %constant.7.clone.const) | copy-start | bytes 344068
  4.3 14.9 %all-to-all-start = ((f32[160,1,128]{2,1,0:T(1,128)}), f32[160,1,128]{2,1,0:T(1,128)S(1)}, u32[]{:S(2)}, u32[]{:S(2)}) async-start(f32[160,1,128]{2,1,0:T(1,128)} %bitcast.2), calls=%async_computation | async-start | bytes 163840 | tf_op jit(solution)/shard_map/all_to_all | solution.py:762
  11.6 18.1 %copy-start.1 = (f32[2,32,1024]{2,1,0:T(8,128)S(1)}, f32[2,32,1024]{2,1,0:T(8,128)}, u32[]{:S(2)}) copy-start(f32[2,32,1024]{2,1,0:T(8,128)} %buffer.1) | copy-start | bytes 786436
  11.7 18.1 %copy-start.3 = (bf16[192,1280]{1,0:T(8,128)(2,1)S(1)}, bf16[192,1280]{1,0:T(8,128)(2,1)}, u32[]{:S(2)}) copy-start(bf16[192,1280]{1,0:T(8,128)(2,1)} %constant.8.clone.const) | copy-start | bytes 1474564
  14.4 15.3 %copy-start = (f32[2,32,1024]{2,1,0:T(8,128)S(1)}, f32[2,32,1024]{2,1,0:T(8,128)}, u32[]{:S(2)}) copy-start(f32[2,32,1024]{2,1,0:T(8,128)} %calcium.1) | copy-start | bytes 786436

commit v6 on v5

--- a/solution.py
+++ b/solution.py
@@ -286,10 +286,10 @@
 
 
 def parts_of(x):
-    high = x.astype(jnp.bfloat16)
-    rest = x - high.astype(jnp.float32)
-    middle = rest.astype(jnp.bfloat16)
-    return high, middle, (rest - middle.astype(jnp.float32)).astype(jnp.bfloat16)
+    high = x.astype(jnp.bfloat16).astype(jnp.float32)
+    rest = x - high
+    middle = rest.astype(jnp.bfloat16).astype(jnp.float32)
+    return high, middle, rest - middle
 
 
 LEFT = (0, 0, 0, 1, 1, 2)
@@ -297,8 +297,8 @@
 
 
 def left_of(x):
-    parts = [part.astype(jnp.float32) for part in parts_of(x)]
-    return jnp.concatenate([parts[p] for p in LEFT], 1).astype(jnp.bfloat16)
+    parts = parts_of(x)
+    return jnp.concatenate([parts[p] for p in LEFT], 1)
 
 
 def right_of(x, axis=0):
@@ -383,7 +383,7 @@
         total = jnp.zeros((len(fields) * edge, LANES), jnp.float32)
         for c in range(tiles):
             hit = ((row & (edge - 1)) == 4 * to + lane // edge) & ((lane & (edge - 1)) == 4 * c + row // edge)
-            hit = hit.astype(jnp.float32).astype(jnp.bfloat16)
+            hit = hit.astype(jnp.float32)
             total = total + dot(whole[c], jnp.concatenate([hit] * 3, 0))
         for f, (ref, b) in enumerate(fields):
             ref[b, :, LANES * to : LANES * (to + 1)] = total[edge * f : edge * (f + 1)]
@@ -464,7 +464,6 @@
                 jnp.where(on_block, jnp.concatenate([jnp.concatenate([x.astype(jnp.float32)] * 4, 1)] * 4, 0), 0.0)
                 for x in parts_of(inverses[b, normal, q])
             ]
-            sides = [x.astype(jnp.bfloat16) for x in sides]
             y = dot(right_of(w, 1), jnp.concatenate([sides[p] for p in LEFT], 0))
             solved[pl.ds(at, size), :] = y
             face_u = jnp.zeros((edge, LANES), jnp.float32)
@@ -477,8 +476,8 @@
             faces_y.append(face_y)
 
     stack = jnp.concatenate(swap_blocks(ends0) + swap_blocks(ends1), 0)
-    ends_of = const[:, : 6 * edge]
-    faces_of = const[:, 2 * LANES :]
+    ends_of = const[:, : 6 * edge].astype(jnp.float32)
+    faces_of = const[:, 2 * LANES :].astype(jnp.float32)
     both = dot(ends_of, right_of(jnp.concatenate([stack[:edge], stack[edge:]], 1)))
     part_u = dot_lanes(faces_of, right_of(jnp.concatenate(faces_u, 0), 1))
     part_y = dot_lanes(faces_of, right_of(jnp.concatenate(faces_y, 0), 1))
@@ -576,12 +575,12 @@
 
 def owner_kernel(recv, pick, flags, const, out):
     edge = const.shape[0]
-    turned = const[:, : 6 * edge].astype(jnp.bfloat16)
-    basis = const[:, 2 * LANES : 2 * LANES + 6 * edge].astype(jnp.bfloat16)
+    turned = const[:, : 6 * edge]
+    basis = const[:, 2 * LANES : 2 * LANES + 6 * edge]
     lam, v_first, v_last = (const[:, LANES * x : LANES * (x + 1)] for x in (4, 5, 6))
     face, touch, normal_2, my_lam = flags[0:1], flags[1:2], flags[2:3], flags[3:4]
 
-    hit = pick[...].astype(jnp.bfloat16)
+    hit = pick[...]
     data = jnp.concatenate([recv[pl.ds(x, edge, stride=ROWS), :] for x in range(4)], 0).T
     tail = recv[pl.ds(4, edge, stride=ROWS), :]
     tail = jnp.concatenate([tail] + [pltpu.roll(tail, LANES - edge * x, 1) for x in range(1, 4)], 0).T[:16]
@@ -669,9 +668,9 @@
     low, high, face_part = (recv[pl.ds(x, edge, stride=3), :] for x in range(3))
     parts = [part.astype(jnp.float32) for part in parts_of(face_part)]
     turn = jnp.concatenate([parts[p] for p in LEFT] + [jnp.zeros_like(parts[0])] * 2, 0)
-    turn = turn.T[:, : 6 * edge].astype(jnp.bfloat16)
-    face_wide = dot(turn, const[:, 2 * LANES :])
-    lines = dot(const[:edge, : 6 * edge], right_of(jnp.concatenate([low, high], 1)))
+    turn = turn.T[:, : 6 * edge]
+    face_wide = dot(turn, const[:, 2 * LANES :].astype(jnp.float32))
+    lines = dot(const[:edge, : 6 * edge].astype(jnp.float32), right_of(jnp.concatenate([low, high], 1)))
     rows = []
     for e in range(2):
         work[pl.ds(edge * e, edge), :] = lines[:, LANES * e : LANES * (e + 1)]

time: 31.3 us -> 31.2 us (level)
  no operation moved by 1% of the time
where the time goes in v6:
time: 31.2 us; the launch traced here: 31 us
  Pallas kernels  9.06 us (29%)
  blocking collectives  9.03 us (29%)
  starting transfers between devices  7.3 us (23%)
  waiting for transfers between devices  4.81 us (15%)
  between operations  0.73 us (2%)
    all_to_all x1, blocking collectives, fast_body(): lax.all_to_all(reply.reshape(devices * 3, 1, LANES), 'bricks', 0, 0, tile...  9.03 us
    all_to_all x1, starting transfers between devices, fast_body(): lax.all_to_all(msg.reshape(devices * ROWS, 1, LANES), 'bricks', 0, 0, til...  7.3 us
    all_to_all x1, waiting for transfers between devices, fast_body(): lax.all_to_all(msg.reshape(devices * ROWS, 1, LANES), 'bricks', 0, 0, til...  4.81 us
    pallas_call x1, Pallas kernels, fast_body(): pl.pallas_call(message_kernel, out_shape=(jax.ShapeDtypeStruct((devices *...  3.54 us
    pallas_call x1, Pallas kernels, fast_body(): pl.pallas_call(local_kernel, out_shape=(tall, jax.ShapeDtypeStruct((LANES...  2.73 us
    pallas_call x1, Pallas kernels, fast_body(): pl.pallas_call(owner_kernel, out_shape=jax.ShapeDtypeStruct((devices * 3,...  1.48 us
    pallas_call x1, Pallas kernels, fast_body(): pl.pallas_call(update_kernel, out_shape=(field, field), in_specs=[vmem] *...  1.31 us
  transfers between devices with their start and end apart: 1, of which 1 were waited for; matrix products, arithmetic and copies ran while one was open for 0% of the time, Pallas kernels for 9%

profile of v6, /device:TPU:0, one launch (start us, length us, event | category | flops | bytes accessed | tf_op | source)
XLA Modules:
  0.0 31.0 jit_solution(1145685374102909732)
XLA Ops:
  0.6 0.0 copy-start.2
  0.6 3.5 %message.1 = (f32[160,128]{1,0:T(8,128)}, f32[1024,128]{1,0:T(8,128)S(1)}) custom-call(s32[3,2,64]{2,1,0:T(2,128)} %near_in.3, f32[2,2,3]{2,1,0:T(2,128)} %bitcast.12, f32[2,32,1024]{2,1,0:T(8,128)} %calcium.1, f32[2,32,1024]{2,1,0:T(8,128)} %buffer.1, f32[2,32,1024]{2,1,0:T(8,128)} %fraction_in.1, f32[2,3,2,32,32]{4,3,2,1,0:T(8,128)} %inverses_in.3, ...), custom_call_target="tpu_custom_call" | custom-call | tf_op jit(solution)/shard_map/message/pallas_call | solution.py:743
  4.2 0.0 copy-start.5
  4.2 0.0 copy-start.4
  4.2 7.3 %all-to-all-start = ((f32[160,1,128]{2,1,0:T(1,128)}), f32[160,1,128]{2,1,0:T(1,128)S(1)}, u32[]{:S(2)}, u32[]{:S(2)}) async-start(f32[160,1,128]{2,1,0:T(1,128)} %bitcast.2), calls=%async_computation | async-start | bytes 163840 | tf_op jit(solution)/shard_map/all_to_all | solution.py:761
  11.5 0.0 copy-done.2
  11.5 0.0 copy-done.5
  11.5 0.0 copy-start.1
  11.6 0.0 copy-start.3
  11.6 2.7 %local_solution.1 = (f32[1024,128]{1,0:T(8,128)S(1)}, f32[128,128]{1,0:T(8,128)S(1)}, f32[8,128]{1,0:T(8,128)S(1)}, f32[4,3,32,128]{3,2,1,0:T(8,128)S(1)}) custom-call(s32[3,2,64]{2,1,0:T(2,128)S(1)} %copy-done.5, f32[1024,128]{1,0:T(8,128)S(1)} %get-tuple-element.9.solved_in, f32[2,3,2,32,32]{4,3,2,1,0:T(8,128)S(1)} %copy-done.2), custom_call_target="tpu_custom_call" | custom-call | flops 20000000 | bytes 4000000 | tf_op jit(solution)/shard_map/local_solution/pallas_call | solution.py:762
  14.3 0.0 copy-start
  14.3 4.8 %all-to-all-done = f32[160,1,128]{2,1,0:T(1,128)S(1)} async-done(((f32[160,1,128]{2,1,0:T(1,128)}), f32[160,1,128]{2,1,0:T(1,128)S(1)}, u32[]{:S(2)}, u32[]{:S(2)}) %all-to-all-start) | async-done | bytes 81952 | tf_op jit(solution)/shard_map/all_to_all | solution.py:761
  19.1 0.0 copy-done.4
  19.1 1.5 %chain_and_face_solves.1 = f32[96,128]{1,0:T(8,128)S(1)} custom-call(f32[160,128]{1,0:T(8,128)S(1)} %bitcast.9, f32[128,128]{1,0:T(8,128)S(1)} %get-tuple-element.10.pick, f32[8,128]{1,0:T(8,128)S(1)} %get-tuple-element.11.flags, f32[32,896]{1,0:T(8,128)S(1)} %copy-done.4), custom_call_target="tpu_custom_call" | custom-call | tf_op jit(solution)/shard_map/chain_and_face_solves/pallas_call | solution.py:785
  20.6 9.0 %all_to_all.10 = f32[96,1,128]{2,1,0:T(1,128)S(1)} all-to-all(f32[96,1,128]{2,1,0:T(1,128)S(1)} %bitcast.11), channel_id=1, replica_groups=mesh['bricks'=32] {'bricks'}, dimensions={0} | all-to-all | bytes 98304 | tf_op jit(solution)/shard_map/all_to_all | solution.py:793
  29.6 0.0 copy-done.1
  29.6 0.0 copy-done.3
  29.6 0.0 copy-done
  29.7 1.3 %rank_three_update.1 = (f32[2,32,1024]{2,1,0:T(8,128)}, f32[2,32,1024]{2,1,0:T(8,128)}) custom-call(f32[96,128]{1,0:T(8,128)S(1)} %bitcast.10, f32[1024,128]{1,0:T(8,128)S(1)} %get-tuple-element.12.base, f32[4,3,32,128]{3,2,1,0:T(8,128)S(1)} %get-tuple-element.13.edges, f32[8,128]{1,0:T(8,128)S(1)} %get-tuple-element.11.flags, f32[2,32,1024]{2,1,0:T(8,128)S(1)} %copy-done, ...), custom_call_target="tpu_custom_call" | custom-call | tf_op jit(solution)/shard_map/rank_three_update/pallas_call | solution.py:794
Async XLA Ops:
  0.6 10.9 %copy-start.2 = (f32[2,3,2,32,32]{4,3,2,1,0:T(8,128)S(1)}, f32[2,3,2,32,32]{4,3,2,1,0:T(8,128)}, u32[]{:S(2)}) copy-start(f32[2,3,2,32,32]{4,3,2,1,0:T(8,128)} %inverses_in.3) | copy-start | bytes 147460
  4.2 7.3 %copy-start.5 = (s32[3,2,64]{2,1,0:T(2,128)S(1)}, s32[3,2,64]{2,1,0:T(2,128)}, u32[]{:S(2)}) copy-start(s32[3,2,64]{2,1,0:T(2,128)} %near_in.3) | copy-start | bytes 4612
  4.2 14.9 %copy-start.4 = (f32[32,896]{1,0:T(8,128)S(1)}, f32[32,896]{1,0:T(8,128)}, u32[]{:S(2)}) copy-start(f32[32,896]{1,0:T(8,128)} %constant.7.clone.const) | copy-start | bytes 344068
  4.2 14.9 %all-to-all-start = ((f32[160,1,128]{2,1,0:T(1,128)}), f32[160,1,128]{2,1,0:T(1,128)S(1)}, u32[]{:S(2)}, u32[]{:S(2)}) async-start(f32[160,1,128]{2,1,0:T(1,128)} %bitcast.2), calls=%async_computation | async-start | bytes 163840 | tf_op jit(solution)/shard_map/all_to_all | solution.py:761
  11.5 18.1 %copy-start.1 = (f32[2,32,1024]{2,1,0:T(8,128)S(1)}, f32[2,32,1024]{2,1,0:T(8,128)}, u32[]{:S(2)}) copy-start(f32[2,32,1024]{2,1,0:T(8,128)} %buffer.1) | copy-start | bytes 786436
  11.6 18.1 %copy-start.3 = (bf16[192,1280]{1,0:T(8,128)(2,1)S(1)}, bf16[192,1280]{1,0:T(8,128)(2,1)}, u32[]{:S(2)}) copy-start(bf16[192,1280]{1,0:T(8,128)(2,1)} %constant.8.clone.const) | copy-start | bytes 1474564
  14.3 15.3 %copy-start = (f32[2,32,1024]{2,1,0:T(8,128)S(1)}, f32[2,32,1024]{2,1,0:T(8,128)}, u32[]{:S(2)}) copy-start(f32[2,32,1024]{2,1,0:T(8,128)} %calcium.1) | copy-start | bytes 786436

commit v7 on v6

--- a/solution.py
+++ b/solution.py
@@ -584,9 +584,11 @@
     data = jnp.concatenate([recv[pl.ds(x, edge, stride=ROWS), :] for x in range(4)], 0).T
     tail = recv[pl.ds(4, edge, stride=ROWS), :]
     tail = jnp.concatenate([tail] + [pltpu.roll(tail, LANES - edge * x, 1) for x in range(1, 4)], 0).T[:16]
-    parts = dot(exact_of(jnp.concatenate([tail, data], 0)), jnp.concatenate([hit] * 3, 0))
-    rate_0, rate_t, rate_n = parts[0:1], parts[1:2], parts[2:3]
-    y0, y1, face_u, face_y = (parts[16 + edge * x : 16 + edge * (x + 1)] for x in range(4))
+    hits = jnp.concatenate([hit] * 3, 0)
+    params = dot(exact_of(tail), hits)
+    rate_0, rate_t, rate_n = params[0:1], params[1:2], params[2:3]
+    parts = dot(exact_of(data), hits)
+    y0, y1, face_u, face_y = (parts[edge * x : edge * (x + 1)] for x in range(4))
 
     lane = lane_of((1, LANES))
     place = lane & (edge - 1)
@@ -606,14 +608,14 @@
     damp_t = 1.0 / (1.0 + my_lam * rate_t)
     other_n = partner(rate_n)
     g = jnp.where(touch > 0.5, 2.0 * rate_n * other_n / (rate_n + other_n), 0.0)
-    cross = 2.0 * g * (partner(face_u) - face_u)
+    cross = partner(face_u) - face_u
     near_c = jnp.sum(damp_0 * v_first * v_first, 0, keepdims=True)
     far_c = jnp.sum(damp_0 * v_first * v_last, 0, keepdims=True)
     end_n = jnp.sum(damp_n * v_first * v_first, 0, keepdims=True)
     open_face = place < edge - 1
     right = jnp.where(open_face, y1 - after(y0), 0.0)
     both = dot(basis, right_of(jnp.concatenate([cross, right], 1)))
-    damped = damp_0 * both[:, :LANES]
+    damped = damp_0 * (2.0 * g) * both[:, :LANES]
     pieces = dot(turned, right_of(jnp.concatenate([damped, damp_0 * v_first, damp_0 * v_last], 1)))
     spread, col_0, col_1 = (pieces[:, LANES * x : LANES * (x + 1)] for x in range(3))
     v_face = jnp.where(face < 0.5, v_first, v_last)
@@ -625,16 +627,29 @@
     diag = jnp.where(open_face, 0.5 * (inv_rate + after(inv_rate)) + near_c + after(near_c), 1.0)
     lower = jnp.where(open_face & (place > 0), -far_c, 0.0)
     upper = jnp.where(place < edge - 2, -after(far_c), 0.0)
-    step = 1
-    while step < edge:
-        inverse = 1.0 / diag
-        back = -lower * before(inverse, step)
-        fore = -upper * after(inverse, step)
-        diag = diag + back * before(upper, step) + fore * after(lower, step)
-        right = right + back * before(right, step) + fore * after(right, step)
-        lower = back * before(lower, step)
-        upper = fore * after(upper, step)
-        step *= 2
+    def shift(x, by):
+        return x if by == 0 else pltpu.roll(x, -by % LANES, 1)
+
+    def reduced(near_by, at, s):
+        (dm, lm, um, rm), (d, l, u, r), (dp, lp, up, rp) = (near_by[at + x * s] for x in (-1, 0, 1))
+        back, fore = -l / dm, -u / dp
+        return d + back * um + fore * lp, back * lm, fore * up, r + back * rm + fore * rp
+
+    system = (diag, lower, upper, right)
+    step, total = 1, (edge - 1).bit_length()
+    for levels in (3, total - 3):
+        reach = 2**levels - 1
+        rows_by = {x * step: tuple(shift(y, x * step) for y in system) for x in range(-reach, reach + 1)}
+        for level in range(levels):
+            reach = 2**levels - 2 ** (level + 1)
+            now = step * 2**level
+            rows_by = {
+                x * step: reduced(rows_by, x * step, now)
+                for x in range(-reach, reach + 1, 2 ** (level + 1))
+            }
+        system = rows_by[0]
+        step *= 2**levels
+    diag, lower, upper, right = system
     flux_up = right / diag
     flux_down = jnp.where(place > 0, before(flux_up), 0.0)
 

time: 31.2 us -> 31 us (level)
  no operation moved by 1% of the time
where the time goes in v7:
time: 31 us; the launch traced here: 30.8 us
  blocking collectives  9.03 us (29%)
  Pallas kernels  8.93 us (29%)
  starting transfers between devices  7.3 us (24%)
  waiting for transfers between devices  4.81 us (16%)
  between operations  0.73 us (2%)
    all_to_all x1, blocking collectives, fast_body(): lax.all_to_all(reply.reshape(devices * 3, 1, LANES), 'bricks', 0, 0, tile...  9.03 us
    all_to_all x1, starting transfers between devices, fast_body(): lax.all_to_all(msg.reshape(devices * ROWS, 1, LANES), 'bricks', 0, 0, til...  7.3 us
    all_to_all x1, waiting for transfers between devices, fast_body(): lax.all_to_all(msg.reshape(devices * ROWS, 1, LANES), 'bricks', 0, 0, til...  4.81 us
    pallas_call x1, Pallas kernels, fast_body(): pl.pallas_call(message_kernel, out_shape=(jax.ShapeDtypeStruct((devices *...  3.54 us
    pallas_call x1, Pallas kernels, fast_body(): pl.pallas_call(local_kernel, out_shape=(tall, jax.ShapeDtypeStruct((LANES...  2.73 us
    pallas_call x1, Pallas kernels, fast_body(): pl.pallas_call(owner_kernel, out_shape=jax.ShapeDtypeStruct((devices * 3,...  1.35 us
    pallas_call x1, Pallas kernels, fast_body(): pl.pallas_call(update_kernel, out_shape=(field, field), in_specs=[vmem] *...  1.31 us
  transfers between devices with their start and end apart: 1, of which 1 were waited for; matrix products, arithmetic and copies ran while one was open for 0% of the time, Pallas kernels for 9%

profile of v7, /device:TPU:0, one launch (start us, length us, event | category | flops | bytes accessed | tf_op | source)
XLA Modules:
  0.0 30.8 jit_solution(9871991730948609935)
XLA Ops:
  0.6 0.0 copy-start.2
  0.6 3.5 %message.1 = (f32[160,128]{1,0:T(8,128)}, f32[1024,128]{1,0:T(8,128)S(1)}) custom-call(s32[3,2,64]{2,1,0:T(2,128)} %near_in.3, f32[2,2,3]{2,1,0:T(2,128)} %bitcast.12, f32[2,32,1024]{2,1,0:T(8,128)} %calcium.1, f32[2,32,1024]{2,1,0:T(8,128)} %buffer.1, f32[2,32,1024]{2,1,0:T(8,128)} %fraction_in.1, f32[2,3,2,32,32]{4,3,2,1,0:T(8,128)} %inverses_in.3, ...), custom_call_target="tpu_custom_call" | custom-call | tf_op jit(solution)/shard_map/message/pallas_call | solution.py:758
  4.2 0.0 copy-start.5
  4.2 0.0 copy-start.4
  4.2 7.3 %all-to-all-start = ((f32[160,1,128]{2,1,0:T(1,128)}), f32[160,1,128]{2,1,0:T(1,128)S(1)}, u32[]{:S(2)}, u32[]{:S(2)}) async-start(f32[160,1,128]{2,1,0:T(1,128)} %bitcast.2), calls=%async_computation | async-start | bytes 163840 | tf_op jit(solution)/shard_map/all_to_all | solution.py:776
  11.5 0.0 copy-done.2
  11.5 0.0 copy-done.5
  11.5 0.0 copy-start.1
  11.6 0.0 copy-start.3
  11.6 2.7 %local_solution.1 = (f32[1024,128]{1,0:T(8,128)S(1)}, f32[128,128]{1,0:T(8,128)S(1)}, f32[8,128]{1,0:T(8,128)S(1)}, f32[4,3,32,128]{3,2,1,0:T(8,128)S(1)}) custom-call(s32[3,2,64]{2,1,0:T(2,128)S(1)} %copy-done.5, f32[1024,128]{1,0:T(8,128)S(1)} %get-tuple-element.9.solved_in, f32[2,3,2,32,32]{4,3,2,1,0:T(8,128)S(1)} %copy-done.2), custom_call_target="tpu_custom_call" | custom-call | flops 20000000 | bytes 4000000 | tf_op jit(solution)/shard_map/local_solution/pallas_call | solution.py:777
  14.3 0.0 copy-start
  14.3 4.8 %all-to-all-done = f32[160,1,128]{2,1,0:T(1,128)S(1)} async-done(((f32[160,1,128]{2,1,0:T(1,128)}), f32[160,1,128]{2,1,0:T(1,128)S(1)}, u32[]{:S(2)}, u32[]{:S(2)}) %all-to-all-start) | async-done | bytes 81952 | tf_op jit(solution)/shard_map/all_to_all | solution.py:776
  19.1 0.0 copy-done.4
  19.1 1.3 %chain_and_face_solves.1 = f32[96,128]{1,0:T(8,128)S(1)} custom-call(f32[160,128]{1,0:T(8,128)S(1)} %bitcast.9, f32[128,128]{1,0:T(8,128)S(1)} %get-tuple-element.10.pick, f32[8,128]{1,0:T(8,128)S(1)} %get-tuple-element.11.flags, f32[32,896]{1,0:T(8,128)S(1)} %copy-done.4), custom_call_target="tpu_custom_call" | custom-call | tf_op jit(solution)/shard_map/chain_and_face_solves/pallas_call | solution.py:800
  20.5 9.0 %all_to_all.10 = f32[96,1,128]{2,1,0:T(1,128)S(1)} all-to-all(f32[96,1,128]{2,1,0:T(1,128)S(1)} %bitcast.11), channel_id=1, replica_groups=mesh['bricks'=32] {'bricks'}, dimensions={0} | all-to-all | bytes 98304 | tf_op jit(solution)/shard_map/all_to_all | solution.py:808
  29.5 0.0 copy-done.1
  29.5 0.0 copy-done.3
  29.5 0.0 copy-done
  29.5 1.3 %rank_three_update.1 = (f32[2,32,1024]{2,1,0:T(8,128)}, f32[2,32,1024]{2,1,0:T(8,128)}) custom-call(f32[96,128]{1,0:T(8,128)S(1)} %bitcast.10, f32[1024,128]{1,0:T(8,128)S(1)} %get-tuple-element.12.base, f32[4,3,32,128]{3,2,1,0:T(8,128)S(1)} %get-tuple-element.13.edges, f32[8,128]{1,0:T(8,128)S(1)} %get-tuple-element.11.flags, f32[2,32,1024]{2,1,0:T(8,128)S(1)} %copy-done, ...), custom_call_target="tpu_custom_call" | custom-call | tf_op jit(solution)/shard_map/rank_three_update/pallas_call | solution.py:809
Async XLA Ops:
  0.6 10.9 %copy-start.2 = (f32[2,3,2,32,32]{4,3,2,1,0:T(8,128)S(1)}, f32[2,3,2,32,32]{4,3,2,1,0:T(8,128)}, u32[]{:S(2)}) copy-start(f32[2,3,2,32,32]{4,3,2,1,0:T(8,128)} %inverses_in.3) | copy-start | bytes 147460
  4.2 7.3 %copy-start.5 = (s32[3,2,64]{2,1,0:T(2,128)S(1)}, s32[3,2,64]{2,1,0:T(2,128)}, u32[]{:S(2)}) copy-start(s32[3,2,64]{2,1,0:T(2,128)} %near_in.3) | copy-start | bytes 4612
  4.2 14.9 %copy-start.4 = (f32[32,896]{1,0:T(8,128)S(1)}, f32[32,896]{1,0:T(8,128)}, u32[]{:S(2)}) copy-start(f32[32,896]{1,0:T(8,128)} %constant.7.clone.const) | copy-start | bytes 344068
  4.2 14.9 %all-to-all-start = ((f32[160,1,128]{2,1,0:T(1,128)}), f32[160,1,128]{2,1,0:T(1,128)S(1)}, u32[]{:S(2)}, u32[]{:S(2)}) async-start(f32[160,1,128]{2,1,0:T(1,128)} %bitcast.2), calls=%async_computation | async-start | bytes 163840 | tf_op jit(solution)/shard_map/all_to_all | solution.py:776
  11.5 18.0 %copy-start.1 = (f32[2,32,1024]{2,1,0:T(8,128)S(1)}, f32[2,32,1024]{2,1,0:T(8,128)}, u32[]{:S(2)}) copy-start(f32[2,32,1024]{2,1,0:T(8,128)} %buffer.1) | copy-start | bytes 786436
  11.6 18.0 %copy-start.3 = (bf16[192,1280]{1,0:T(8,128)(2,1)S(1)}, bf16[192,1280]{1,0:T(8,128)(2,1)}, u32[]{:S(2)}) copy-start(bf16[192,1280]{1,0:T(8,128)(2,1)} %constant.8.clone.const) | copy-start | bytes 1474564
  14.3 15.2 %copy-start = (f32[2,32,1024]{2,1,0:T(8,128)S(1)}, f32[2,32,1024]{2,1,0:T(8,128)}, u32[]{:S(2)}) copy-start(f32[2,32,1024]{2,1,0:T(8,128)} %calcium.1) | copy-start | bytes 786436

commit v8 on v7

--- a/solution.py
+++ b/solution.py
@@ -708,7 +708,8 @@
                     + face_wide[edge * x : edge * (x + 1), part] * row_n
                     + (col_0 * rows[0][x][c : c + 1] - col_1 * rows[1][x][c : c + 1])
                 )
-            stores[x].start()
+        stores[2 * b].start()
+        stores[2 * b + 1].start()
     for store in stores:
         store.wait()
 

time: 31 us -> 31 us (level)
  no operation moved by 1% of the time
where the time goes in v8:
time: 31 us; the launch traced here: 30.8 us
  blocking collectives  9.03 us (29%)
  Pallas kernels  8.93 us (29%)
  starting transfers between devices  7.3 us (24%)
  waiting for transfers between devices  4.81 us (16%)
  between operations  0.73 us (2%)
    all_to_all x1, blocking collectives, fast_body(): lax.all_to_all(reply.reshape(devices * 3, 1, LANES), 'bricks', 0, 0, tile...  9.03 us
    all_to_all x1, starting transfers between devices, fast_body(): lax.all_to_all(msg.reshape(devices * ROWS, 1, LANES), 'bricks', 0, 0, til...  7.3 us
    all_to_all x1, waiting for transfers between devices, fast_body(): lax.all_to_all(msg.reshape(devices * ROWS, 1, LANES), 'bricks', 0, 0, til...  4.81 us
    pallas_call x1, Pallas kernels, fast_body(): pl.pallas_call(message_kernel, out_shape=(jax.ShapeDtypeStruct((devices *...  3.54 us
    pallas_call x1, Pallas kernels, fast_body(): pl.pallas_call(local_kernel, out_shape=(tall, jax.ShapeDtypeStruct((LANES...  2.73 us
    pallas_call x1, Pallas kernels, fast_body(): pl.pallas_call(owner_kernel, out_shape=jax.ShapeDtypeStruct((devices * 3,...  1.35 us
    pallas_call x1, Pallas kernels, fast_body(): pl.pallas_call(update_kernel, out_shape=(field, field), in_specs=[vmem] *...  1.31 us
  transfers between devices with their start and end apart: 1, of which 1 were waited for; matrix products, arithmetic and copies ran while one was open for 0% of the time, Pallas kernels for 9%

profile of v8, /device:TPU:0, one launch (start us, length us, event | category | flops | bytes accessed | tf_op | source)
XLA Modules:
  0.0 30.8 jit_solution(9871991730948609935)
XLA Ops:
  0.6 0.0 copy-start.2
  0.6 3.5 %message.1 = (f32[160,128]{1,0:T(8,128)}, f32[1024,128]{1,0:T(8,128)S(1)}) custom-call(s32[3,2,64]{2,1,0:T(2,128)} %near_in.3, f32[2,2,3]{2,1,0:T(2,128)} %bitcast.12, f32[2,32,1024]{2,1,0:T(8,128)} %calcium.1, f32[2,32,1024]{2,1,0:T(8,128)} %buffer.1, f32[2,32,1024]{2,1,0:T(8,128)} %fraction_in.1, f32[2,3,2,32,32]{4,3,2,1,0:T(8,128)} %inverses_in.3, ...), custom_call_target="tpu_custom_call" | custom-call | tf_op jit(solution)/shard_map/message/pallas_call | solution.py:759
  4.2 0.0 copy-start.5
  4.2 0.0 copy-start.4
  4.2 7.3 %all-to-all-start = ((f32[160,1,128]{2,1,0:T(1,128)}), f32[160,1,128]{2,1,0:T(1,128)S(1)}, u32[]{:S(2)}, u32[]{:S(2)}) async-start(f32[160,1,128]{2,1,0:T(1,128)} %bitcast.2), calls=%async_computation | async-start | bytes 163840 | tf_op jit(solution)/shard_map/all_to_all | solution.py:777
  11.5 0.0 copy-done.2
  11.5 0.0 copy-done.5
  11.5 0.0 copy-start.1
  11.6 0.0 copy-start.3
  11.6 2.7 %local_solution.1 = (f32[1024,128]{1,0:T(8,128)S(1)}, f32[128,128]{1,0:T(8,128)S(1)}, f32[8,128]{1,0:T(8,128)S(1)}, f32[4,3,32,128]{3,2,1,0:T(8,128)S(1)}) custom-call(s32[3,2,64]{2,1,0:T(2,128)S(1)} %copy-done.5, f32[1024,128]{1,0:T(8,128)S(1)} %get-tuple-element.9.solved_in, f32[2,3,2,32,32]{4,3,2,1,0:T(8,128)S(1)} %copy-done.2), custom_call_target="tpu_custom_call" | custom-call | flops 20000000 | bytes 4000000 | tf_op jit(solution)/shard_map/local_solution/pallas_call | solution.py:778
  14.3 0.0 copy-start
  14.3 4.8 %all-to-all-done = f32[160,1,128]{2,1,0:T(1,128)S(1)} async-done(((f32[160,1,128]{2,1,0:T(1,128)}), f32[160,1,128]{2,1,0:T(1,128)S(1)}, u32[]{:S(2)}, u32[]{:S(2)}) %all-to-all-start) | async-done | bytes 81952 | tf_op jit(solution)/shard_map/all_to_all | solution.py:777
  19.1 0.0 copy-done.4
  19.1 1.3 %chain_and_face_solves.1 = f32[96,128]{1,0:T(8,128)S(1)} custom-call(f32[160,128]{1,0:T(8,128)S(1)} %bitcast.9, f32[128,128]{1,0:T(8,128)S(1)} %get-tuple-element.10.pick, f32[8,128]{1,0:T(8,128)S(1)} %get-tuple-element.11.flags, f32[32,896]{1,0:T(8,128)S(1)} %copy-done.4), custom_call_target="tpu_custom_call" | custom-call | tf_op jit(solution)/shard_map/chain_and_face_solves/pallas_call | solution.py:801
  20.5 9.0 %all_to_all.10 = f32[96,1,128]{2,1,0:T(1,128)S(1)} all-to-all(f32[96,1,128]{2,1,0:T(1,128)S(1)} %bitcast.11), channel_id=1, replica_groups=mesh['bricks'=32] {'bricks'}, dimensions={0} | all-to-all | bytes 98304 | tf_op jit(solution)/shard_map/all_to_all | solution.py:809
  29.5 0.0 copy-done.1
  29.5 0.0 copy-done.3
  29.5 0.0 copy-done
  29.5 1.3 %rank_three_update.1 = (f32[2,32,1024]{2,1,0:T(8,128)}, f32[2,32,1024]{2,1,0:T(8,128)}) custom-call(f32[96,128]{1,0:T(8,128)S(1)} %bitcast.10, f32[1024,128]{1,0:T(8,128)S(1)} %get-tuple-element.12.base, f32[4,3,32,128]{3,2,1,0:T(8,128)S(1)} %get-tuple-element.13.edges, f32[8,128]{1,0:T(8,128)S(1)} %get-tuple-element.11.flags, f32[2,32,1024]{2,1,0:T(8,128)S(1)} %copy-done, ...), custom_call_target="tpu_custom_call" | custom-call | tf_op jit(solution)/shard_map/rank_three_update/pallas_call | solution.py:810
Async XLA Ops:
  0.6 10.9 %copy-start.2 = (f32[2,3,2,32,32]{4,3,2,1,0:T(8,128)S(1)}, f32[2,3,2,32,32]{4,3,2,1,0:T(8,128)}, u32[]{:S(2)}) copy-start(f32[2,3,2,32,32]{4,3,2,1,0:T(8,128)} %inverses_in.3) | copy-start | bytes 147460
  4.2 7.3 %copy-start.5 = (s32[3,2,64]{2,1,0:T(2,128)S(1)}, s32[3,2,64]{2,1,0:T(2,128)}, u32[]{:S(2)}) copy-start(s32[3,2,64]{2,1,0:T(2,128)} %near_in.3) | copy-start | bytes 4612
  4.2 14.9 %copy-start.4 = (f32[32,896]{1,0:T(8,128)S(1)}, f32[32,896]{1,0:T(8,128)}, u32[]{:S(2)}) copy-start(f32[32,896]{1,0:T(8,128)} %constant.7.clone.const) | copy-start | bytes 344068
  4.2 14.9 %all-to-all-start = ((f32[160,1,128]{2,1,0:T(1,128)}), f32[160,1,128]{2,1,0:T(1,128)S(1)}, u32[]{:S(2)}, u32[]{:S(2)}) async-start(f32[160,1,128]{2,1,0:T(1,128)} %bitcast.2), calls=%async_computation | async-start | bytes 163840 | tf_op jit(solution)/shard_map/all_to_all | solution.py:777
  11.5 18.0 %copy-start.1 = (f32[2,32,1024]{2,1,0:T(8,128)S(1)}, f32[2,32,1024]{2,1,0:T(8,128)}, u32[]{:S(2)}) copy-start(f32[2,32,1024]{2,1,0:T(8,128)} %buffer.1) | copy-start | bytes 786436
  11.6 18.0 %copy-start.3 = (bf16[192,1280]{1,0:T(8,128)(2,1)S(1)}, bf16[192,1280]{1,0:T(8,128)(2,1)}, u32[]{:S(2)}) copy-start(bf16[192,1280]{1,0:T(8,128)(2,1)} %constant.8.clone.const) | copy-start | bytes 1474564
  14.3 15.2 %copy-start = (f32[2,32,1024]{2,1,0:T(8,128)S(1)}, f32[2,32,1024]{2,1,0:T(8,128)}, u32[]{:S(2)}) copy-start(f32[2,32,1024]{2,1,0:T(8,128)} %calcium.1) | copy-start | bytes 786436

commit v9 on v8

--- a/solution.py
+++ b/solution.py
@@ -406,12 +406,12 @@
         pltpu.make_async_copy(source, target, sems.at[x])
         for x, (source, target) in enumerate(
             (
-                (near_in, near),
-                (rates_in, rates),
                 (calcium_in, calcium),
                 (buffer_in, buffer),
                 (fraction_in, fraction),
                 (inverses_in, inverses),
+                (near_in, near),
+                (rates_in, rates),
                 (const_in, const),
             )
         )

time: 31 us -> 31.1 us (level)
  no operation moved by 1% of the time
where the time goes in v9:
time: 31.1 us; the launch traced here: 30.9 us
  blocking collectives  9.03 us (29%)
  Pallas kernels  8.96 us (29%)
  starting transfers between devices  7.3 us (23%)
  waiting for transfers between devices  4.81 us (15%)
  between operations  0.73 us (2%)
    all_to_all x1, blocking collectives, fast_body(): lax.all_to_all(reply.reshape(devices * 3, 1, LANES), 'bricks', 0, 0, tile...  9.03 us
    all_to_all x1, starting transfers between devices, fast_body(): lax.all_to_all(msg.reshape(devices * ROWS, 1, LANES), 'bricks', 0, 0, til...  7.3 us
    all_to_all x1, waiting for transfers between devices, fast_body(): lax.all_to_all(msg.reshape(devices * ROWS, 1, LANES), 'bricks', 0, 0, til...  4.81 us
    pallas_call x1, Pallas kernels, fast_body(): pl.pallas_call(message_kernel, out_shape=(jax.ShapeDtypeStruct((devices *...  3.56 us
    pallas_call x1, Pallas kernels, fast_body(): pl.pallas_call(local_kernel, out_shape=(tall, jax.ShapeDtypeStruct((LANES...  2.73 us
    pallas_call x1, Pallas kernels, fast_body(): pl.pallas_call(owner_kernel, out_shape=jax.ShapeDtypeStruct((devices * 3,...  1.35 us
    pallas_call x1, Pallas kernels, fast_body(): pl.pallas_call(update_kernel, out_shape=(field, field), in_specs=[vmem] *...  1.31 us
  transfers between devices with their start and end apart: 1, of which 1 were waited for; matrix products, arithmetic and copies ran while one was open for 0% of the time, Pallas kernels for 9%

profile of v9, /device:TPU:0, one launch (start us, length us, event | category | flops | bytes accessed | tf_op | source)
XLA Modules:
  0.0 30.9 jit_solution(4704148517318397126)
XLA Ops:
  0.6 0.0 copy-start.2
  0.6 3.6 %message.1 = (f32[160,128]{1,0:T(8,128)}, f32[1024,128]{1,0:T(8,128)S(1)}) custom-call(s32[3,2,64]{2,1,0:T(2,128)} %near_in.3, f32[2,2,3]{2,1,0:T(2,128)} %bitcast.12, f32[2,32,1024]{2,1,0:T(8,128)} %calcium.1, f32[2,32,1024]{2,1,0:T(8,128)} %buffer.1, f32[2,32,1024]{2,1,0:T(8,128)} %fraction_in.1, f32[2,3,2,32,32]{4,3,2,1,0:T(8,128)} %inverses_in.3, ...), custom_call_target="tpu_custom_call" | custom-call | tf_op jit(solution)/shard_map/message/pallas_call | solution.py:759
  4.2 0.0 copy-start.5
  4.2 0.0 copy-start.4
  4.2 7.3 %all-to-all-start = ((f32[160,1,128]{2,1,0:T(1,128)}), f32[160,1,128]{2,1,0:T(1,128)S(1)}, u32[]{:S(2)}, u32[]{:S(2)}) async-start(f32[160,1,128]{2,1,0:T(1,128)} %bitcast.2), calls=%async_computation | async-start | bytes 163840 | tf_op jit(solution)/shard_map/all_to_all | solution.py:777
  11.5 0.0 copy-done.2
  11.6 0.0 copy-done.5
  11.6 0.0 copy-start.1
  11.6 0.0 copy-start.3
  11.6 2.7 %local_solution.1 = (f32[1024,128]{1,0:T(8,128)S(1)}, f32[128,128]{1,0:T(8,128)S(1)}, f32[8,128]{1,0:T(8,128)S(1)}, f32[4,3,32,128]{3,2,1,0:T(8,128)S(1)}) custom-call(s32[3,2,64]{2,1,0:T(2,128)S(1)} %copy-done.5, f32[1024,128]{1,0:T(8,128)S(1)} %get-tuple-element.9.solved_in, f32[2,3,2,32,32]{4,3,2,1,0:T(8,128)S(1)} %copy-done.2), custom_call_target="tpu_custom_call" | custom-call | flops 20000000 | bytes 4000000 | tf_op jit(solution)/shard_map/local_solution/pallas_call | solution.py:778
  14.3 0.0 copy-start
  14.3 4.8 %all-to-all-done = f32[160,1,128]{2,1,0:T(1,128)S(1)} async-done(((f32[160,1,128]{2,1,0:T(1,128)}), f32[160,1,128]{2,1,0:T(1,128)S(1)}, u32[]{:S(2)}, u32[]{:S(2)}) %all-to-all-start) | async-done | bytes 81952 | tf_op jit(solution)/shard_map/all_to_all | solution.py:777
  19.2 0.0 copy-done.4
  19.2 1.3 %chain_and_face_solves.1 = f32[96,128]{1,0:T(8,128)S(1)} custom-call(f32[160,128]{1,0:T(8,128)S(1)} %bitcast.9, f32[128,128]{1,0:T(8,128)S(1)} %get-tuple-element.10.pick, f32[8,128]{1,0:T(8,128)S(1)} %get-tuple-element.11.flags, f32[32,896]{1,0:T(8,128)S(1)} %copy-done.4), custom_call_target="tpu_custom_call" | custom-call | tf_op jit(solution)/shard_map/chain_and_face_solves/pallas_call | solution.py:801
  20.5 9.0 %all_to_all.10 = f32[96,1,128]{2,1,0:T(1,128)S(1)} all-to-all(f32[96,1,128]{2,1,0:T(1,128)S(1)} %bitcast.11), channel_id=1, replica_groups=mesh['bricks'=32] {'bricks'}, dimensions={0} | all-to-all | bytes 98304 | tf_op jit(solution)/shard_map/all_to_all | solution.py:809
  29.5 0.0 copy-done.1
  29.5 0.0 copy-done.3
  29.5 0.0 copy-done
  29.5 1.3 %rank_three_update.1 = (f32[2,32,1024]{2,1,0:T(8,128)}, f32[2,32,1024]{2,1,0:T(8,128)}) custom-call(f32[96,128]{1,0:T(8,128)S(1)} %bitcast.10, f32[1024,128]{1,0:T(8,128)S(1)} %get-tuple-element.12.base, f32[4,3,32,128]{3,2,1,0:T(8,128)S(1)} %get-tuple-element.13.edges, f32[8,128]{1,0:T(8,128)S(1)} %get-tuple-element.11.flags, f32[2,32,1024]{2,1,0:T(8,128)S(1)} %copy-done, ...), custom_call_target="tpu_custom_call" | custom-call | tf_op jit(solution)/shard_map/rank_three_update/pallas_call | solution.py:810
Async XLA Ops:
  0.6 10.9 %copy-start.2 = (f32[2,3,2,32,32]{4,3,2,1,0:T(8,128)S(1)}, f32[2,3,2,32,32]{4,3,2,1,0:T(8,128)}, u32[]{:S(2)}) copy-start(f32[2,3,2,32,32]{4,3,2,1,0:T(8,128)} %inverses_in.3) | copy-start | bytes 147460
  4.2 7.3 %copy-start.5 = (s32[3,2,64]{2,1,0:T(2,128)S(1)}, s32[3,2,64]{2,1,0:T(2,128)}, u32[]{:S(2)}) copy-start(s32[3,2,64]{2,1,0:T(2,128)} %near_in.3) | copy-start | bytes 4612
  4.2 14.9 %copy-start.4 = (f32[32,896]{1,0:T(8,128)S(1)}, f32[32,896]{1,0:T(8,128)}, u32[]{:S(2)}) copy-start(f32[32,896]{1,0:T(8,128)} %constant.7.clone.const) | copy-start | bytes 344068
  4.2 14.9 %all-to-all-start = ((f32[160,1,128]{2,1,0:T(1,128)}), f32[160,1,128]{2,1,0:T(1,128)S(1)}, u32[]{:S(2)}, u32[]{:S(2)}) async-start(f32[160,1,128]{2,1,0:T(1,128)} %bitcast.2), calls=%async_computation | async-start | bytes 163840 | tf_op jit(solution)/shard_map/all_to_all | solution.py:777
  11.6 18.0 %copy-start.1 = (f32[2,32,1024]{2,1,0:T(8,128)S(1)}, f32[2,32,1024]{2,1,0:T(8,128)}, u32[]{:S(2)}) copy-start(f32[2,32,1024]{2,1,0:T(8,128)} %buffer.1) | copy-start | bytes 786436
  11.6 18.0 %copy-start.3 = (bf16[192,1280]{1,0:T(8,128)(2,1)S(1)}, bf16[192,1280]{1,0:T(8,128)(2,1)}, u32[]{:S(2)}) copy-start(bf16[192,1280]{1,0:T(8,128)(2,1)} %constant.8.clone.const) | copy-start | bytes 1474564
  14.3 15.2 %copy-start = (f32[2,32,1024]{2,1,0:T(8,128)S(1)}, f32[2,32,1024]{2,1,0:T(8,128)}, u32[]{:S(2)}) copy-start(f32[2,32,1024]{2,1,0:T(8,128)} %calcium.1) | copy-start | bytes 786436
